TPU v7x, 32 devices: a whole 2x2x4 slice. The times are simulated.
32 devices in a mesh: fsdp: 4 (over y, x), seq: 8 (over z, core).
Axes of the slice: x: 2, y: 2, z: 4, core: 2. Of those that a mesh axis runs over, the one named last changes fastest.
Arguments:
- tokens: bfloat16 [4, 3072, 2048], P('fsdp', 'seq'), may hold values from -40 to 40
- starts: int32 [4, 3], P('fsdp'), may hold values from 0 to 3072, as said below
- w_query: bfloat16 [2048, 2048], P(('fsdp', 'seq')), may hold values from -0.1875 to 0.1875
- w_key: bfloat16 [2048, 256], P(('fsdp', 'seq')), may hold values from -0.1875 to 0.1875
- w_value: bfloat16 [2048, 256], P(('fsdp', 'seq')), may hold values from -0.125 to 0.125
- w_out: bfloat16 [2048, 2048], P(None, ('fsdp', 'seq')), may hold values from -1 to 1
- w_gate: bfloat16 [2048, 5632], P(('fsdp', 'seq')), may hold values from -0.125 to 0.125
- w_up: bfloat16 [2048, 5632], P(('fsdp', 'seq')), may hold values from -0.125 to 0.125
- w_down: bfloat16 [5632, 2048], P(None, ('fsdp', 'seq')), may hold values from -0.078125 to 0.078125
- norm_attn: bfloat16 [2048], P(('fsdp', 'seq')), may hold values from 0.5 to 1.5
- norm_mlp: bfloat16 [2048], P(('fsdp', 'seq')), may hold values from 0.5 to 1.5
- cotangent: bfloat16 [4, 3072, 2048], P('fsdp', 'seq'), may hold values from -6 to 6
Outputs:
- out: bfloat16 [4, 3072, 2048], P('fsdp', 'seq')
- grad_tokens: bfloat16 [4, 3072, 2048], P('fsdp', 'seq')
- grad_query: float32 [2048, 2048], P(('fsdp', 'seq'))
- grad_key: float32 [2048, 256], P(('fsdp', 'seq'))
- grad_value: float32 [2048, 256], P(('fsdp', 'seq'))
- grad_out: float32 [2048, 2048], P(None, ('fsdp', 'seq'))
- grad_gate: float32 [2048, 5632], P(('fsdp', 'seq'))
- grad_up: float32 [2048, 5632], P(('fsdp', 'seq'))
- grad_down: float32 [5632, 2048], P(None, ('fsdp', 'seq'))
- grad_norm_attn: float32 [2048], P(('fsdp', 'seq'))
- grad_norm_mlp: float32 [2048], P(('fsdp', 'seq'))
Inputs may be any that keep to these rules, and one draw needn't show every extreme that they name: `starts`: each row lists the first positions of its sequence's documents in rising order, beginning with 0; unused slots hold 3072. Every document has 1024 to 2048 tokens, and each sequence has one of exactly 2048 tokens.
All inputs are finite; a program needn't handle non-finite values.
Results may differ from a plain program's by a relative error of at most 0.02.
Values may be sent and summed in bfloat16 or wider, within the bound.
A program may use at most 448 MiB of HBM per device.

v0:
```python
import jax
import jax.numpy as jnp
from jax import lax
from jax.sharding import PartitionSpec as P

HEADS = 32
KV = 4
HD = 64
BLOCK = 512


EPSILON = 1e-05
ROPE_BASE = 10000.0
MASKED = -1e30


def contract(left, right, left_dim, right_dim):
    return lax.dot_general(
        left, right, (((left_dim,), (right_dim,)), ((), ())), preferred_element_type=jnp.float32
    )


def doc_first(start_row, places):
    inside = start_row[None, :] <= places[:, None]
    return jnp.max(jnp.where(inside, start_row[None, :], 0), axis=1)


def rotary_tables(places, firsts):
    half_dim = HD // 2
    frequency = ROPE_BASE ** (-(jnp.arange(half_dim, dtype=jnp.float32) / half_dim))
    angles = frequency[:, None] * (places - firsts).astype(jnp.float32)[None, :]
    return (jnp.cos(angles), jnp.sin(angles))


def rotate(values, cos_table, sine_table):
    half_dim = HD // 2
    front_half = values[:, :half_dim]
    back_half = values[:, half_dim:]
    return jnp.concatenate(
        [
            front_half * cos_table - back_half * sine_table,
            back_half * cos_table + front_half * sine_table,
        ],
        axis=1,
    )


def unrotate(grads_in, cos_table, sine_table):
    half_dim = HD // 2
    front_half = grads_in[:, :half_dim]
    back_half = grads_in[:, half_dim:]
    return jnp.concatenate(
        [
            front_half * cos_table + back_half * sine_table,
            back_half * cos_table - front_half * sine_table,
        ],
        axis=1,
    )


def norm_forward(values, gain):
    scale_rows = lax.rsqrt(jnp.mean(values * values, axis=1, keepdims=True) + EPSILON)
    return (values * scale_rows * gain, scale_rows)


def norm_backward(values, scale_rows, gain, grads_in):
    weighted = grads_in * gain
    gain_grad = jnp.sum(grads_in * values * scale_rows, axis=0)
    inner_mean = jnp.mean(weighted * values, axis=1, keepdims=True)
    return (
        scale_rows * weighted - values * (scale_rows * scale_rows * scale_rows) * inner_mean,
        gain_grad,
    )


def block_scores(query_part, keyvals, first_rows, query_start, key_block):
    key_start = key_block * BLOCK
    keyval_part = lax.dynamic_slice_in_dim(keyvals, key_start, BLOCK, 1)
    scores = jnp.einsum(
        "pdq,dk->pqk", query_part, keyval_part[:HD], preferred_element_type=jnp.float32
    ) * HD ** (-0.5)
    query_at = query_start + jnp.arange(BLOCK, dtype=jnp.int32)
    key_at = key_start + jnp.arange(BLOCK, dtype=jnp.int32)
    allowed = (key_at[None, :] <= query_at[:, None]) & (key_at[None, :] >= first_rows[:, None])
    return (jnp.where(allowed[None], scores, MASKED), keyval_part)


def attend_forward(queries, keyvals, first_all):
    head_count = queries.shape[0]
    length = queries.shape[2]

    def query_step(block_index, state):
        out_all, total_all = state
        query_start = block_index * BLOCK
        query_part = lax.dynamic_slice_in_dim(queries, query_start, BLOCK, 2)
        first_rows = lax.dynamic_slice_in_dim(first_all, query_start, BLOCK, 0)
        lowest = first_all[query_start] // BLOCK

        def stat_step(key_block, carry):
            running, totals = carry
            scores, unused_part = block_scores(
                query_part, keyvals, first_rows, query_start, key_block
            )
            highest = jnp.maximum(running, jnp.max(scores, axis=2))
            totals = totals * jnp.exp(running - highest) + jnp.sum(
                jnp.exp(scores - highest[:, :, None]), axis=2
            )
            return (highest, totals)

        running, totals = lax.fori_loop(
            lowest,
            block_index + 1,
            stat_step,
            (
                jnp.full((head_count, BLOCK), MASKED, jnp.float32),
                jnp.zeros((head_count, BLOCK), jnp.float32),
            ),
        )
        log_total = running + jnp.log(totals)

        def out_step(key_block, weighted_sum):
            scores, keyval_part = block_scores(
                query_part, keyvals, first_rows, query_start, key_block
            )
            weights = jnp.exp(scores - log_total[:, :, None]).astype(jnp.bfloat16)
            return weighted_sum + jnp.einsum(
                "pqk,dk->pdq", weights, keyval_part[HD:], preferred_element_type=jnp.float32
            )

        weighted_sum = lax.fori_loop(
            lowest, block_index + 1, out_step, jnp.zeros((head_count, HD, BLOCK), jnp.float32)
        )
        out_all = lax.dynamic_update_slice_in_dim(
            out_all, weighted_sum.astype(jnp.bfloat16), query_start, 2
        )
        total_all = lax.dynamic_update_slice_in_dim(total_all, log_total, query_start, 1)
        return (out_all, total_all)

    start_state = (
        jnp.zeros((head_count, HD, length), jnp.bfloat16),
        jnp.zeros((head_count, length), jnp.float32),
    )
    return lax.fori_loop(0, length // BLOCK, query_step, start_state)


def attend_backward(queries, keyvals, first_all, total_all, grad_out_all):
    head_count = queries.shape[0]
    length = queries.shape[2]
    score_scale = HD ** (-0.5)

    def query_step(block_index, state):
        query_grads, keyval_grads = state
        query_start = block_index * BLOCK
        query_part = lax.dynamic_slice_in_dim(queries, query_start, BLOCK, 2)
        first_rows = lax.dynamic_slice_in_dim(first_all, query_start, BLOCK, 0)
        log_total = lax.dynamic_slice_in_dim(total_all, query_start, BLOCK, 1)
        grad_part = lax.dynamic_slice_in_dim(grad_out_all, query_start, BLOCK, 2)
        lowest = first_all[query_start] // BLOCK

        def block_probs(key_block):
            scores, keyval_part = block_scores(
                query_part, keyvals, first_rows, query_start, key_block
            )
            weights = jnp.exp(scores - log_total[:, :, None])
            grad_weights = jnp.einsum(
                "pdq,dk->pqk", grad_part, keyval_part[HD:], preferred_element_type=jnp.float32
            )
            return (weights, grad_weights, keyval_part)

        def delta_step(key_block, row_delta):
            weights, grad_weights, unused_part = block_probs(key_block)
            return row_delta + jnp.sum(weights * grad_weights, axis=2)

        row_delta = lax.fori_loop(
            lowest, block_index + 1, delta_step, jnp.zeros((head_count, BLOCK), jnp.float32)
        )

        def grad_step(key_block, carry):
            query_sum, keyval_sum = carry
            weights, grad_weights, keyval_part = block_probs(key_block)
            grad_scores = (weights * (grad_weights - row_delta[:, :, None])).astype(jnp.bfloat16)
            query_sum = query_sum + jnp.einsum(
                "pqk,dk->pdq", grad_scores, keyval_part[:HD], preferred_element_type=jnp.float32
            )
            key_grad = (
                jnp.einsum(
                    "pqk,pdq->dk", grad_scores, query_part, preferred_element_type=jnp.float32
                )
                * score_scale
            )
            value_grad = jnp.einsum(
                "pqk,pdq->dk",
                weights.astype(jnp.bfloat16),
                grad_part,
                preferred_element_type=jnp.float32,
            )
            key_start = key_block * BLOCK
            previous = lax.dynamic_slice_in_dim(keyval_sum, key_start, BLOCK, 1)
            updated = previous + jnp.concatenate([key_grad, value_grad], axis=0)
            return (query_sum, lax.dynamic_update_slice_in_dim(keyval_sum, updated, key_start, 1))

        query_sum, keyval_grads = lax.fori_loop(
            lowest,
            block_index + 1,
            grad_step,
            (jnp.zeros((head_count, HD, BLOCK), jnp.float32), keyval_grads),
        )
        query_grads = lax.dynamic_update_slice_in_dim(
            query_grads, (query_sum * score_scale).astype(jnp.bfloat16), query_start, 2
        )
        return (query_grads, keyval_grads)

    start_state = (
        jnp.zeros((head_count, HD, length), jnp.bfloat16),
        jnp.zeros((2 * HD, length), jnp.float32),
    )
    query_grads, keyval_grads = lax.fori_loop(0, length // BLOCK, query_step, start_state)
    return (query_grads, keyval_grads.astype(jnp.bfloat16))


def shards(
    tokens,
    starts,
    w_query,
    w_key,
    w_value,
    w_out,
    w_gate,
    w_up,
    w_down,
    norm_attn,
    norm_mlp,
    cotangent,
):
    seq_count = lax.axis_size("seq")
    fsdp_count = lax.axis_size("fsdp")
    seq_rank = lax.axis_index("seq")
    tok_rows = tokens.shape[1]
    length = tok_rows * seq_count
    per_slot = HEADS // seq_count
    repeats = seq_count // KV
    sectioned_parts = (
        lax.all_gather(w_query[None], "fsdp", axis=0, tiled=True),
        lax.all_gather(w_key[None], "fsdp", axis=0, tiled=True),
        lax.all_gather(w_value[None], "fsdp", axis=0, tiled=True),
        lax.all_gather(w_out[:, None], "fsdp", axis=1, tiled=True),
        lax.all_gather(w_gate[None], "fsdp", axis=0, tiled=True),
        lax.all_gather(w_up[None], "fsdp", axis=0, tiled=True),
        lax.all_gather(w_down[:, None], "fsdp", axis=1, tiled=True),
        lax.all_gather(norm_attn[None], "fsdp", axis=0, tiled=True),
        lax.all_gather(norm_mlp[None], "fsdp", axis=0, tiled=True),
    )
    gathered = (
        lax.all_gather(sectioned_parts[0], "seq", axis=1, tiled=True),
        lax.all_gather(sectioned_parts[1], "seq", axis=1, tiled=True),
        lax.all_gather(sectioned_parts[2], "seq", axis=1, tiled=True),
        lax.all_gather(sectioned_parts[3], "seq", axis=2, tiled=True),
        lax.all_gather(sectioned_parts[4], "seq", axis=1, tiled=True),
        lax.all_gather(sectioned_parts[5], "seq", axis=1, tiled=True),
        lax.all_gather(sectioned_parts[6], "seq", axis=2, tiled=True),
        lax.all_gather(sectioned_parts[7], "seq", axis=1, tiled=True),
        lax.all_gather(sectioned_parts[8], "seq", axis=1, tiled=True),
    )
    full_query = gathered[0].reshape(-1, w_query.shape[1])
    full_key = gathered[1].reshape(-1, w_key.shape[1])
    full_value = gathered[2].reshape(-1, w_value.shape[1])
    full_out = gathered[3].reshape(w_out.shape[0], -1)
    full_gate = gathered[4].reshape(-1, w_gate.shape[1])
    full_up = gathered[5].reshape(-1, w_up.shape[1])
    full_down = gathered[6].reshape(w_down.shape[0], -1)
    gain_attn = gathered[7].reshape(-1).astype(jnp.float32)
    gain_mlp = gathered[8].reshape(-1).astype(jnp.float32)
    inputs = tokens[0].astype(jnp.float32)
    start_row = starts[0]
    places = seq_rank * tok_rows + jnp.arange(tok_rows, dtype=jnp.int32)
    firsts = doc_first(start_row, places)
    cos_table, sine_table = rotary_tables(places, firsts)
    normed, scale_attn = norm_forward(inputs, gain_attn)
    normed_low = normed.astype(jnp.bfloat16)
    query_pre = contract(full_query, normed_low, 0, 1).reshape(HEADS, HD, tok_rows)
    key_pre = contract(full_key, normed_low, 0, 1).reshape(KV, HD, tok_rows)
    value_pre = contract(full_value, normed_low, 0, 1).reshape(KV, HD, tok_rows)
    query_low = (
        rotate(query_pre, cos_table, sine_table)
        .astype(jnp.bfloat16)
        .reshape(seq_count, per_slot * HD, tok_rows)
    )
    key_low = rotate(key_pre, cos_table, sine_table).astype(jnp.bfloat16)
    keyvals = jnp.repeat(
        jnp.concatenate([key_low, value_pre.astype(jnp.bfloat16)], axis=1), repeats, axis=0
    )
    head_query, head_keyvals = (
        lax.all_to_all(query_low, "seq", split_axis=0, concat_axis=2, tiled=True),
        lax.all_to_all(keyvals, "seq", split_axis=0, concat_axis=2, tiled=True),
    )
    head_query = head_query.reshape(per_slot, HD, length)
    head_keyvals = head_keyvals.reshape(2 * HD, length)
    first_all = doc_first(start_row, jnp.arange(length, dtype=jnp.int32))
    head_out, head_totals = attend_forward(head_query, head_keyvals, first_all)
    attended = lax.all_to_all(
        head_out.reshape(1, per_slot * HD, length), "seq", split_axis=2, concat_axis=0, tiled=True
    ).reshape(HEADS * HD, tok_rows)
    middle = inputs + contract(attended, full_out, 0, 0)
    normed_mid, scale_mlp = norm_forward(middle, gain_mlp)
    normed_mid_low = normed_mid.astype(jnp.bfloat16)
    gate_values = jnp.dot(normed_mid_low, full_gate, preferred_element_type=jnp.float32)
    up_values = jnp.dot(normed_mid_low, full_up, preferred_element_type=jnp.float32)
    activated = jax.nn.silu(gate_values)
    hidden = (activated * up_values).astype(jnp.bfloat16)
    result = middle + jnp.dot(hidden, full_down, preferred_element_type=jnp.float32)
    grad_result = cotangent[0]
    grad_down = contract(hidden, grad_result, 0, 0)
    back_hidden = contract(grad_result, full_down, 1, 1)
    sigmoid_gate = jax.nn.sigmoid(gate_values)
    back_gate = (
        back_hidden * up_values * sigmoid_gate * (1.0 + gate_values * (1.0 - sigmoid_gate))
    ).astype(jnp.bfloat16)
    back_up = (back_hidden * activated).astype(jnp.bfloat16)
    grad_gate = contract(normed_mid_low, back_gate, 0, 0)
    grad_up = contract(normed_mid_low, back_up, 0, 0)
    back_normed_mid = contract(back_gate, full_gate, 1, 1) + contract(back_up, full_up, 1, 1)
    back_middle, grad_gain_mlp = norm_backward(middle, scale_mlp, gain_mlp, back_normed_mid)
    back_middle = back_middle + grad_result.astype(jnp.float32)
    sectioned_mlp = (
        lax.psum_scatter(
            grad_gate.reshape(fsdp_count, -1, grad_gate.shape[1]).astype(jnp.bfloat16),
            "seq",
            scatter_dimension=1,
            tiled=True,
        ).astype(jnp.float32),
        lax.psum_scatter(
            grad_up.reshape(fsdp_count, -1, grad_up.shape[1]).astype(jnp.bfloat16),
            "seq",
            scatter_dimension=1,
            tiled=True,
        ).astype(jnp.float32),
        lax.psum_scatter(
            grad_down.reshape(grad_down.shape[0], fsdp_count, -1).astype(jnp.bfloat16),
            "seq",
            scatter_dimension=2,
            tiled=True,
        ).astype(jnp.float32),
        lax.psum_scatter(
            grad_gain_mlp.reshape(fsdp_count, -1).astype(jnp.bfloat16),
            "seq",
            scatter_dimension=1,
            tiled=True,
        ).astype(jnp.float32),
    )
    mlp_sums = (
        lax.psum_scatter(
            sectioned_mlp[0].astype(jnp.bfloat16), "fsdp", scatter_dimension=0, tiled=True
        ).astype(jnp.float32),
        lax.psum_scatter(
            sectioned_mlp[1].astype(jnp.bfloat16), "fsdp", scatter_dimension=0, tiled=True
        ).astype(jnp.float32),
        lax.psum_scatter(
            sectioned_mlp[2].astype(jnp.bfloat16), "fsdp", scatter_dimension=1, tiled=True
        ).astype(jnp.float32),
        lax.psum_scatter(
            sectioned_mlp[3].astype(jnp.bfloat16), "fsdp", scatter_dimension=0, tiled=True
        ).astype(jnp.float32),
    )
    back_branch = back_middle.astype(jnp.bfloat16)
    grad_out = contract(attended, back_branch, 1, 0)
    back_attended = (
        contract(full_out, back_branch, 1, 1)
        .astype(jnp.bfloat16)
        .reshape(seq_count, per_slot * HD, tok_rows)
    )
    head_grads = lax.all_to_all(
        back_attended, "seq", split_axis=0, concat_axis=2, tiled=True
    ).reshape(per_slot, HD, length)
    back_head_query, back_head_keyvals = attend_backward(
        head_query, head_keyvals, first_all, head_totals, head_grads
    )
    back_query_tok, back_keyvals_tok = (
        lax.all_to_all(
            back_head_query.reshape(1, per_slot * HD, length),
            "seq",
            split_axis=2,
            concat_axis=0,
            tiled=True,
        ),
        lax.all_to_all(
            back_head_keyvals.reshape(1, 2 * HD, length),
            "seq",
            split_axis=2,
            concat_axis=0,
            tiled=True,
        ),
    )
    back_query = (
        unrotate(
            back_query_tok.reshape(HEADS, HD, tok_rows).astype(jnp.float32), cos_table, sine_table
        )
        .astype(jnp.bfloat16)
        .reshape(HEADS * HD, tok_rows)
    )
    back_keyvals = jnp.sum(
        back_keyvals_tok.astype(jnp.float32).reshape(KV, repeats, 2 * HD, tok_rows), axis=1
    )
    back_key = (
        unrotate(back_keyvals[:, :HD], cos_table, sine_table)
        .astype(jnp.bfloat16)
        .reshape(KV * HD, tok_rows)
    )
    back_value = back_keyvals[:, HD:].astype(jnp.bfloat16).reshape(KV * HD, tok_rows)
    grad_query = contract(normed_low, back_query, 0, 1)
    grad_key = contract(normed_low, back_key, 0, 1)
    grad_value = contract(normed_low, back_value, 0, 1)
    back_normed = (
        contract(back_query, full_query, 0, 1)
        + contract(back_key, full_key, 0, 1)
        + contract(back_value, full_value, 0, 1)
    )
    back_inputs, grad_gain_attn = norm_backward(inputs, scale_attn, gain_attn, back_normed)
    back_inputs = back_inputs + back_middle
    sectioned_attn = (
        lax.psum_scatter(
            grad_query.reshape(fsdp_count, -1, grad_query.shape[1]).astype(jnp.bfloat16),
            "seq",
            scatter_dimension=1,
            tiled=True,
        ).astype(jnp.float32),
        lax.psum_scatter(
            grad_key.reshape(fsdp_count, -1, grad_key.shape[1]).astype(jnp.bfloat16),
            "seq",
            scatter_dimension=1,
            tiled=True,
        ).astype(jnp.float32),
        lax.psum_scatter(
            grad_value.reshape(fsdp_count, -1, grad_value.shape[1]).astype(jnp.bfloat16),
            "seq",
            scatter_dimension=1,
            tiled=True,
        ).astype(jnp.float32),
        lax.psum_scatter(
            grad_out.reshape(grad_out.shape[0], fsdp_count, -1).astype(jnp.bfloat16),
            "seq",
            scatter_dimension=2,
            tiled=True,
        ).astype(jnp.float32),
        lax.psum_scatter(
            grad_gain_attn.reshape(fsdp_count, -1).astype(jnp.bfloat16),
            "seq",
            scatter_dimension=1,
            tiled=True,
        ).astype(jnp.float32),
    )
    attn_sums = (
        lax.psum_scatter(
            sectioned_attn[0].astype(jnp.bfloat16), "fsdp", scatter_dimension=0, tiled=True
        ).astype(jnp.float32),
        lax.psum_scatter(
            sectioned_attn[1].astype(jnp.bfloat16), "fsdp", scatter_dimension=0, tiled=True
        ).astype(jnp.float32),
        lax.psum_scatter(
            sectioned_attn[2].astype(jnp.bfloat16), "fsdp", scatter_dimension=0, tiled=True
        ).astype(jnp.float32),
        lax.psum_scatter(
            sectioned_attn[3].astype(jnp.bfloat16), "fsdp", scatter_dimension=1, tiled=True
        ).astype(jnp.float32),
        lax.psum_scatter(
            sectioned_attn[4].astype(jnp.bfloat16), "fsdp", scatter_dimension=0, tiled=True
        ).astype(jnp.float32),
    )
    return (
        result.astype(jnp.bfloat16)[None],
        back_inputs.astype(jnp.bfloat16)[None],
        attn_sums[0].reshape(-1, grad_query.shape[1]),
        attn_sums[1].reshape(-1, grad_key.shape[1]),
        attn_sums[2].reshape(-1, grad_value.shape[1]),
        attn_sums[3].reshape(grad_out.shape[0], -1),
        mlp_sums[0].reshape(-1, grad_gate.shape[1]),
        mlp_sums[1].reshape(-1, grad_up.shape[1]),
        mlp_sums[2].reshape(grad_down.shape[0], -1),
        attn_sums[4].reshape(-1),
        mlp_sums[3].reshape(-1),
    )


def solution(mesh):
    placed = (
        P("fsdp", "seq", None),
        P("fsdp", None),
        P(("fsdp", "seq"), None),
        P(("fsdp", "seq"), None),
        P(("fsdp", "seq"), None),
        P(None, ("fsdp", "seq")),
        P(("fsdp", "seq"), None),
        P(("fsdp", "seq"), None),
        P(None, ("fsdp", "seq")),
        P(("fsdp", "seq")),
        P(("fsdp", "seq")),
        P("fsdp", "seq", None),
    )
    return jax.shard_map(
        shards,
        mesh=mesh,
        in_specs=placed,
        out_specs=(
            P("fsdp", "seq", None),
            P("fsdp", "seq", None),
            P(("fsdp", "seq"), None),
            P(("fsdp", "seq"), None),
            P(("fsdp", "seq"), None),
            P(None, ("fsdp", "seq")),
            P(("fsdp", "seq"), None),
            P(("fsdp", "seq"), None),
            P(None, ("fsdp", "seq")),
            P(("fsdp", "seq")),
            P(("fsdp", "seq")),
        ),
        check_vma=False,
    )
```

profile of v0, /device:TPU:0, one launch (start us, length us, event | category | flops | bytes accessed | tf_op | source)
XLA Modules:
  0.0 2804.1 jit_solution(7050358304583550685)
XLA Ops:
  40.2 27.7 all-gather.40.cloned.1.call-done
  68.0 43.6 %all-gather.42.cloned.1.call-done = bf16[256,5632]{1,0:T(8,128)(2,1)} async-done(((bf16[64,5632]{1,0:T(8,128)(2,1)}), bf16[256,5632]{1,0:T(8,128)(2,1)}) %all-gather.42.cloned.1.call-update) | async-done | bytes 2883600 | tf_op jit(solution)/shard_map/all_gather | solution.py:247
  111.6 43.5 %all-gather.44.cloned.1.call-done = bf16[256,5632]{1,0:T(8,128)(2,1)} async-done(((bf16[64,5632]{1,0:T(8,128)(2,1)}), bf16[256,5632]{1,0:T(8,128)(2,1)}) %all-gather.44.cloned.1.call-update) | async-done | bytes 2883600 | tf_op jit(solution)/shard_map/all_gather | solution.py:248
  181.6 20.4 all-gather.28.cloned.1.call-done
  208.6 90.3 %all-gather.24.cloned.1.call-done = bf16[4,512,2048]{2,1,0:T(8,128)(2,1)} async-done(((bf16[4,64,2048]{2,1,0:T(8,128)(2,1)}), bf16[4,512,2048]{2,1,0:T(8,128)(2,1)}) %all-gather.24.cloned.1.call-update) | async-done | bytes 8388624 | tf_op jit(solution)/shard_map/all_gather | solution.py:254
  320.5 21.0 all-gather.46.cloned.1.call-done
  341.4 23.5 all-to-all-done
  373.4 84.0 %while.173 = (s32[]{:T(128)}, bf16[4,64,3072]{2,1,0:T(8,128)(2,1)}, f32[4,3072]{1,0:T(4,128)S(1)}, s32[3072]{0:T(1024)S(1)}, bf16[4,64,3072]{2,1,0:T(8,128)(2,1)...) while((s32[]{:T(128)}, bf16[4,64,3072]{2,1,0:T(8,128)(2,1)}, ...), condition=%wide.region_10.11_spmd, body=%wide.region_3.10_spmd.sunk | while | flops 416030720 | bytes 13494783 | solution.py:143
  491.4 58.3 %all-gather.10 = bf16[8,64,4]{1,2,0:T(4,128)(2,1)S(1)} all-gather(bf16[1,64,4]{1,2,0:T(4,128)(2,1)S(1)} %bitcast.474), channel_id=1, replica_groups=mesh['fsdp'=4,'seq'=8] {'seq'}, dimensions={0}, use_global_device_ids=true | all-gather | bytes 4608 | tf_op jit(solution)/shard_map/all_gather | solution.py:262
  549.8 20.3 all-to-all-done.2
  591.1 72.2 %all-gather.32.cloned.1.call-done = bf16[4,512,5632]{2,1,0:T(8,128)(2,1)} async-done(((bf16[4,64,5632]{2,1,0:T(8,128)(2,1)}), bf16[4,512,5632]{2,1,0:T(8,128)(2,1)}) %all-gather.32.cloned.1.call-update) | async-done | bytes 23068688 | tf_op jit(solution)/shard_map/all_gather | solution.py:258
  678.9 186.9 %all-gather.34.cloned.1.call-done = bf16[4,512,5632]{2,1,0:T(8,128)(2,1)} async-done(((bf16[4,64,5632]{2,1,0:T(8,128)(2,1)}), bf16[4,512,5632]{2,1,0:T(8,128)(2,1)}) %all-gather.34.cloned.1.call-update) | async-done | bytes 23068688 | tf_op jit(solution)/shard_map/all_gather | solution.py:259
  881.9 186.2 %all-gather.36.cloned.1.call-done = bf16[5632,4,512]{0,2,1:T(8,128)(2,1)} async-done(((bf16[5632,4,64]{0,2,1:T(8,128)(2,1)}), bf16[5632,4,512]{0,2,1:T(8,128)(2,1)}) %all-gather.36.cloned.1.call-update) | async-done | bytes 23068688 | tf_op jit(solution)/shard_map/all_gather | solution.py:260
  1068.1 24.0 multiply_convert_fusion.1
  1144.5 37.7 %all-to-all-done.3 = bf16[8,256,384]{1,2,0:T(8,128)(2,1)S(1)} async-done(((bf16[8,256,384]{1,2,0:T(8,128)(2,1)}), bf16[8,256,384]{1,2,0:T(8,128)(2,1)S(1)}, u32[]{:S(2)}, u32[]{:S(2)}) %all-to-all-start.3) | async-done | bytes 1572896 | tf_op jit(solution)/shard_map/all_to_all | solution.py:371
  1189.5 246.1 %while.176 = (s32[]{:T(128)}, bf16[4,64,3072]{2,1,0:T(8,128)(2,1)}, f32[128,3072]{1,0:T(8,128)S(1)}, s32[3072]{0:T(1024)S(1)}, bf16[4,64,3072]{2,1,0:T(8,128)(2,...) while((s32[]{:T(128)}, bf16[4,64,3072]{2,1,0:T(8,128)(2,1)}, ...), condition=%wide.region_19.20_spmd, body=%wide.region_13.19_spmd.sunk | while | flops 957384704 | bytes 53920984 | solution.py:217
  1275.0 28.6 %while.180 = (s32[]{:T(128)}, f32[4,64,512]{2,1,0:T(8,128)S(1)}, f32[128,3072]{1,0:T(8,128)S(1)}, s32[]{:T(128)}, bf16[128,3072]{1,0:T(8,128)(2,1)S(1)}, /*index...) while((s32[]{:T(128)}, f32[4,64,512]{2,1,0:T(8,128)S(1)}, ...), condition=%wide.region_18.18_spmd, body=%wide.region_17.17_spmd.sunk | while | flops 682656768 | bytes 40864036 | solution.py:202
  1308.8 26.7 while.179
  1336.2 38.2 %while.180 = (s32[]{:T(128)}, f32[4,64,512]{2,1,0:T(8,128)S(1)}, f32[128,3072]{1,0:T(8,128)S(1)}, s32[]{:T(128)}, bf16[128,3072]{1,0:T(8,128)(2,1)S(1)}, /*index...) while((s32[]{:T(128)}, f32[4,64,512]{2,1,0:T(8,128)S(1)}, ...), condition=%wide.region_18.18_spmd, body=%wide.region_17.17_spmd.sunk | while | flops 682656768 | bytes 40864036 | solution.py:202
  1507.5 23.8 all-to-all-done.4
  1638.1 72.4 %reduce-scatter.41.cloned.1.call-done = bf16[2048,4,64]{0,2,1:T(8,128)(2,1)} async-done(((bf16[2048,4,512]{0,2,1:T(8,128)(2,1)}), bf16[2048,4,64]{0,2,1:T(8,128)(2,1)}) %reduce-scatter.41.cloned.1.call-update) | async-done | bytes 1048592 | tf_op jit(solution)/shard_map/reduce_scatter | solution.py:438
  1710.6 90.1 %reduce-scatter.35.cloned.1.call-done = bf16[4,64,2048]{2,1,0:T(8,128)(2,1)} async-done(((bf16[4,512,2048]{2,1,0:T(8,128)(2,1)}), bf16[4,64,2048]{2,1,0:T(8,128)(2,1)}) %reduce-scatter.35.cloned.1.call-update) | async-done | bytes 1048592 | tf_op jit(solution)/shard_map/reduce_scatter | solution.py:420
  1800.7 227.9 %reduce-scatter.45.cloned.1.call-done = bf16[4,64,5632]{2,1,0:T(8,128)(2,1)} async-done(((bf16[4,512,5632]{2,1,0:T(8,128)(2,1)}), bf16[4,64,5632]{2,1,0:T(8,128)(2,1)}) %reduce-scatter.45.cloned.1.call-update) | async-done | bytes 2883600 | tf_op jit(solution)/shard_map/reduce_scatter | solution.py:331
  2028.7 228.0 %reduce-scatter.43.cloned.1.call-done = bf16[4,64,5632]{2,1,0:T(8,128)(2,1)} async-done(((bf16[4,512,5632]{2,1,0:T(8,128)(2,1)}), bf16[4,64,5632]{2,1,0:T(8,128)(2,1)}) %reduce-scatter.43.cloned.1.call-update) | async-done | bytes 2883600 | tf_op jit(solution)/shard_map/reduce_scatter | solution.py:325
  2256.8 228.1 %reduce-scatter.47.cloned.1.call-done = bf16[5632,4,64]{0,2,1:T(8,128)(2,1)} async-done(((bf16[5632,4,512]{0,2,1:T(8,128)(2,1)}), bf16[5632,4,64]{0,2,1:T(8,128)(2,1)}) %reduce-scatter.47.cloned.1.call-update) | async-done | bytes 2883600 | tf_op jit(solution)/shard_map/reduce_scatter | solution.py:337
  2516.9 30.5 %reduce-scatter.49.cloned.1.call-done = bf16[64,4]{1,0:T(8,128)(2,1)} async-done(((bf16[512,4]{1,0:T(8,128)(2,1)}), bf16[64,4]{1,0:T(8,128)(2,1)}) %reduce-scatter.49.cloned.1.call-update) | async-done | bytes 528
  2573.5 25.4 reduce-scatter.55.cloned.1.call-done
  2600.4 29.1 %reduce-scatter.59.cloned.1.call-done = bf16[2048,1,64]{0,2,1:T(8,128)(2,1)} async-done(((bf16[2048,4,64]{0,2,1:T(8,128)(2,1)}), bf16[2048,1,64]{0,2,1:T(8,128)(2,1)}) %reduce-scatter.59.cloned.1.call-update) | async-done | bytes 262160
  2631.3 29.1 %reduce-scatter.53.cloned.1.call-done = bf16[1,64,2048]{2,1,0:T(8,128)(2,1)} async-done(((bf16[4,64,2048]{2,1,0:T(8,128)(2,1)}), bf16[1,64,2048]{2,1,0:T(8,128)(2,1)}) %reduce-scatter.53.cloned.1.call-update) | async-done | bytes 262160
  2662.2 42.9 %reduce-scatter.63.cloned.1.call-done = bf16[1,64,5632]{2,1,0:T(8,128)(2,1)} async-done(((bf16[4,64,5632]{2,1,0:T(8,128)(2,1)}), bf16[1,64,5632]{2,1,0:T(8,128)(2,1)}) %reduce-scatter.63.cloned.1.call-update) | async-done | bytes 720912
  2707.4 42.4 %reduce-scatter.61.cloned.1.call-done = bf16[1,64,5632]{2,1,0:T(8,128)(2,1)} async-done(((bf16[4,64,5632]{2,1,0:T(8,128)(2,1)}), bf16[1,64,5632]{2,1,0:T(8,128)(2,1)}) %reduce-scatter.61.cloned.1.call-update) | async-done | bytes 720912
  2752.0 42.5 %reduce-scatter.65.cloned.1.call-done = bf16[5632,1,64]{0,2,1:T(8,128)(2,1)} async-done(((bf16[5632,4,64]{0,2,1:T(8,128)(2,1)}), bf16[5632,1,64]{0,2,1:T(8,128)(2,1)}) %reduce-scatter.65.cloned.1.call-update) | async-done | bytes 720912
  (723 shorter events, 955.5 us)
Async XLA Ops:
  7.9 60.0 %all-gather.40.cloned.1.call-start = ((), (), s32[]{:S(2)}) async-start(), calls=%async_computation.37 | async-start | bytes 1310720 | tf_op jit(solution)/shard_map/all_gather | solution.py:246
  8.7 102.9 %all-gather.42.cloned.1.call-start = ((), (), s32[]{:S(2)}) async-start(), calls=%async_computation.38 | async-start | bytes 3604480 | tf_op jit(solution)/shard_map/all_gather | solution.py:247
  9.4 145.7 %all-gather.44.cloned.1.call-start = ((), (), s32[]{:S(2)}) async-start(), calls=%async_computation.39 | async-start | bytes 3604480 | tf_op jit(solution)/shard_map/all_gather | solution.py:248
  10.0 169.2 %all-gather.26.cloned.1.call-start = ((), (), s32[]{:S(2)}) async-start(), calls=%async_computation.23 | async-start | bytes 1179648 | tf_op jit(solution)/shard_map/all_gather | solution.py:255
  21.4 180.6 %all-gather.28.cloned.1.call-start = ((), (), s32[]{:S(2)}) async-start(), calls=%async_computation.24 | async-start | bytes 1179648 | tf_op jit(solution)/shard_map/all_gather | solution.py:256
  30.4 268.5 %all-gather.24.cloned.1.call-start = ((), (), s32[]{:S(2)}) async-start(), calls=%async_computation.22 | async-start | bytes 9437184 | tf_op jit(solution)/shard_map/all_gather | solution.py:254
  39.4 302.0 %all-gather.46.cloned.1.call-start = ((), (), s32[]{:S(2)}) async-start(), calls=%async_computation.40 | async-start | bytes 3604480 | tf_op jit(solution)/shard_map/all_gather | solution.py:249
  40.2 542.2 %all-gather.30.cloned.1.call-start = ((), (), s32[]{:S(2)}) async-start(), calls=%async_computation.25 | async-start | bytes 9437184 | tf_op jit(solution)/shard_map/all_gather | solution.py:257
  68.0 595.3 %all-gather.32.cloned.1.call-start = ((), (), s32[]{:S(2)}) async-start(), calls=%async_computation.26 | async-start | bytes 25952256 | tf_op jit(solution)/shard_map/all_gather | solution.py:258
  111.6 754.2 %all-gather.34.cloned.1.call-start = ((), (), s32[]{:S(2)}) async-start(), calls=%async_computation.27 | async-start | bytes 25952256 | tf_op jit(solution)/shard_map/all_gather | solution.py:259
  205.1 110.0 %all-to-all-start.1 = ((bf16[8,128,384]{2,1,0:T(8,128)(2,1)}), bf16[8,128,384]{2,1,0:T(8,128)(2,1)S(1)}, u32[]{:S(2)}, u32[]{:S(2)}) async-start(bf16[8,128,384]{2,1,0:T(8,128)(2,1)} %bitcast.44), calls=%async_computation.1 | async-start | bytes 1572864 | tf_op jit(solution)/shard_map/all_to_all | solution.py:294
  315.1 49.8 %all-to-all-start = ((bf16[8,256,384]{2,1,0:T(8,128)(2,1)}), bf16[8,256,384]{2,1,0:T(8,128)(2,1)}, u32[]{:S(2)}, u32[]{:S(2)}) async-start(bf16[8,256,384]{2,1,0:T(8,128)(2,1)} %bitcast.422), calls=%async_computation | async-start | bytes 3145728 | tf_op jit(solution)/shard_map/all_to_all | solution.py:293
  319.4 748.7 %all-gather.36.cloned.1.call-start = ((), (), s32[]{:S(2)}) async-start(), calls=%async_computation.28 | async-start | bytes 25952256 | tf_op jit(solution)/shard_map/all_gather | solution.py:260
  487.0 83.1 %all-to-all-start.2 = ((bf16[8,2,49152]{2,1,0:T(2,128)(2,1)}), bf16[8,2,49152]{2,1,0:T(2,128)(2,1)}, u32[]{:S(2)}, u32[]{:S(2)}) async-start(bf16[8,2,49152]{2,1,0:T(2,128)(2,1)} %reshape.734), calls=%async_computation.2 | async-start | bytes 3145728 | tf_op jit(solution)/shard_map/all_to_all | solution.py:300
  1140.9 41.3 %all-to-all-start.3 = ((bf16[8,256,384]{1,2,0:T(8,128)(2,1)}), bf16[8,256,384]{1,2,0:T(8,128)(2,1)S(1)}, u32[]{:S(2)}, u32[]{:S(2)}) async-start(bf16[8,256,384]{1,2,0:T(8,128)(2,1)} %bitcast.424), calls=%async_computation.3 | async-start | bytes 3145728 | tf_op jit(solution)/shard_map/all_to_all | solution.py:371
  1488.3 42.9 %all-to-all-start.4 = ((bf16[8,2,49152]{2,1,0:T(2,128)(2,1)}), bf16[8,2,49152]{2,1,0:T(2,128)(2,1)}, u32[]{:S(2)}, u32[]{:S(2)}) async-start(bf16[8,2,49152]{2,1,0:T(2,128)(2,1)} %reshape.736), calls=%async_computation.4 | async-start | bytes 3145728 | tf_op jit(solution)/shard_map/all_to_all | solution.py:378
  1493.3 143.3 %reduce-scatter.39.cloned.1.call-start = ((), (), s32[]{:S(2)}) async-start(), calls=%async_computation.31 | async-start | bytes 1179648 | tf_op jit(solution)/shard_map/reduce_scatter | solution.py:432
  1555.8 81.6 %reduce-scatter.37.cloned.1.call-start = ((), (), s32[]{:S(2)}) async-start(), calls=%async_computation.30 | async-start | bytes 1179648 | tf_op jit(solution)/shard_map/reduce_scatter | solution.py:426
  1557.5 153.0 %reduce-scatter.41.cloned.1.call-start = ((), (), s32[]{:S(2)}) async-start(), calls=%async_computation.32 | async-start | bytes 9437184 | tf_op jit(solution)/shard_map/reduce_scatter | solution.py:438
  1569.3 231.4 %reduce-scatter.35.cloned.1.call-start = ((), (), s32[]{:S(2)}) async-start(), calls=%async_computation.29 | async-start | bytes 9437184 | tf_op jit(solution)/shard_map/reduce_scatter | solution.py:420
  1577.6 451.1 %reduce-scatter.45.cloned.1.call-start = ((), (), s32[]{:S(2)}) async-start(), calls=%async_computation.34 | async-start | bytes 25952256 | tf_op jit(solution)/shard_map/reduce_scatter | solution.py:331
  1596.5 660.2 %reduce-scatter.43.cloned.1.call-start = ((), (), s32[]{:S(2)}) async-start(), calls=%async_computation.33 | async-start | bytes 25952256 | tf_op jit(solution)/shard_map/reduce_scatter | solution.py:325
  1614.4 870.5 %reduce-scatter.47.cloned.1.call-start = ((), (), s32[]{:S(2)}) async-start(), calls=%async_computation.35 | async-start | bytes 25952256 | tf_op jit(solution)/shard_map/reduce_scatter | solution.py:337
  1634.2 882.0 %reduce-scatter.51.cloned.1.call-start = ((), (), s32[]{:S(2)}) async-start(), calls=%async_computation.42 | async-start | bytes 147456
  1635.7 911.8 %reduce-scatter.49.cloned.1.call-start = ((), (), s32[]{:S(2)}) async-start(), calls=%async_computation.41 | async-start | bytes 147456
  1636.6 935.6 %reduce-scatter.57.cloned.1.call-start = ((), (), s32[]{:S(2)}) async-start(), calls=%async_computation.45 | async-start | bytes 163840
  1637.3 961.7 %reduce-scatter.55.cloned.1.call-start = ((), (), s32[]{:S(2)}) async-start(), calls=%async_computation.44 | async-start | bytes 163840
  1638.0 991.4 %reduce-scatter.59.cloned.1.call-start = ((), (), s32[]{:S(2)}) async-start(), calls=%async_computation.46 | async-start | bytes 1310720
  1710.5 949.9 %reduce-scatter.53.cloned.1.call-start = ((), (), s32[]{:S(2)}) async-start(), calls=%async_computation.43 | async-start | bytes 1310720
  1800.7 904.4 %reduce-scatter.63.cloned.1.call-start = ((), (), s32[]{:S(2)}) async-start(), calls=%async_computation.48 | async-start | bytes 3604480
  2028.7 721.0 %reduce-scatter.61.cloned.1.call-start = ((), (), s32[]{:S(2)}) async-start(), calls=%async_computation.47 | async-start | bytes 3604480
  2256.7 537.8 %reduce-scatter.65.cloned.1.call-start = ((), (), s32[]{:S(2)}) async-start(), calls=%async_computation.49 | async-start | bytes 3604480
  (63 other events, 1987.4 us)
Sparse Core Ops, SparseCore 0:
  9.9 29.4 all-gather.37
  41.2 26.6 all-gather.39
  69.7 41.7 all-gather.41
  113.3 41.7 all-gather.43
  156.6 22.1 all-gather.25
  180.2 21.7 all-gather.27
  203.6 95.3 all-gather.23
  300.8 40.5 all-gather.45
  343.0 83.6 all-gather.29
  428.1 235.1 all-gather.31
  664.9 200.8 all-gather.33
  867.2 200.8 all-gather.35
  1555.9 31.0 reduce-scatter.38
  1589.6 30.6 reduce-scatter.36
  1622.5 87.9 reduce-scatter.40
  1712.7 87.9 reduce-scatter.34
  1802.9 225.7 reduce-scatter.44
  2030.9 225.7 reduce-scatter.42
  2259.1 225.7 reduce-scatter.46
  2487.6 28.5 reduce-scatter.50
  2519.0 28.3 reduce-scatter.48
  2550.2 21.9 reduce-scatter.56
  2575.1 23.8 reduce-scatter.54
  2601.7 27.7 reduce-scatter.58
  2632.6 27.7 reduce-scatter.52
  2663.3 41.7 reduce-scatter.62
  2708.0 41.7 reduce-scatter.60
  2752.8 41.7 reduce-scatter.64
where the time goes:
time: 2810 us; the launch traced here: 2800 us
  waiting for transfers between devices  1930 us (69%)
  matrix products  451 us (16%)
  other arithmetic  123 us (4%)
  local copies, waits for them, and re-layouts  115 us (4%)
  blocking collectives  109 us (4%)
  loops' own time  35.2 us (1%)
    unnamed x37, waiting for transfers between devices  275 us
    reduce_scatter x1, waiting for transfers between devices, shards(): lax.psum_scatter(grad_down.reshape(grad_down.shape[0], fsdp_count, -1).as...  228 us
    reduce_scatter x1, waiting for transfers between devices, shards(): lax.psum_scatter(grad_gate.reshape(fsdp_count, -1, grad_gate.shape[1]).as...  228 us
    reduce_scatter x1, waiting for transfers between devices, shards(): lax.psum_scatter(grad_up.reshape(fsdp_count, -1, grad_up.shape[1]).astype...  228 us
    all_gather x1, waiting for transfers between devices, shards(): lax.all_gather(sectioned_parts[5], 'seq', axis=1, tiled=True)  187 us
    all_gather x1, waiting for transfers between devices, shards(): lax.all_gather(sectioned_parts[6], 'seq', axis=2, tiled=True)  186 us
    dot_general x18, matrix products, contract(): lax.dot_general(left, right, (((left_dim,), (right_dim,)), ((), ())), pre...  170 us
    dot_general x26, matrix products, block_probs(): jnp.einsum('pdq,dk->pqk', grad_part, keyval_part[HD:], preferred_element_...  96.4 us
  transfers between devices with their start and end apart: 34, of which 28 were waited for; matrix products, arithmetic and copies ran while one was open for 12% of the time, Pallas kernels for 0%

commit v1 on v0

v1 whole, which is shorter than its diff:
```python
import functools

import jax
import jax.numpy as jnp
from jax import lax
from jax.experimental import pallas as pl
from jax.experimental.pallas import tpu as pltpu
from jax.sharding import PartitionSpec as P

HEADS = 32
KV = 4
HD = 64
EPSILON = 1e-05
ROPE_BASE = 10000.0
MASKED = -1e30
GROUP = 4
AXES = ("fsdp", "seq")
BF = jnp.bfloat16
F32 = jnp.float32


def contract(left, right, left_dim, right_dim):
    return lax.dot_general(
        left, right, (((left_dim,), (right_dim,)), ((), ())), preferred_element_type=F32
    )


def doc_first(start_row, places):
    inside = start_row[None, :] <= places[:, None]
    return jnp.max(jnp.where(inside, start_row[None, :], 0), axis=1)


def rotary_tables(offsets):
    half_dim = HD // 2
    frequency = ROPE_BASE ** (-(jnp.arange(half_dim, dtype=F32) / half_dim))
    angles = frequency[:, None] * offsets.astype(F32)[None, :]
    return (jnp.cos(angles), jnp.sin(angles))


def rotate(values, cos_table, sine_table):
    half_dim = HD // 2
    front_half = values[:, :half_dim]
    back_half = values[:, half_dim:]
    return jnp.concatenate(
        [
            front_half * cos_table - back_half * sine_table,
            back_half * cos_table + front_half * sine_table,
        ],
        axis=1,
    )


def unrotate(grads_in, cos_table, sine_table):
    return rotate(grads_in, cos_table, -sine_table)


def swap_pair(flag, pair):
    return [jnp.where(flag == 1, pair[1], pair[0]), jnp.where(flag == 1, pair[0], pair[1])]


def forward_kernel(
    meta, query_ref, keyval_ref, first_ref, out_ref, lse_ref, q_all, top, total, acc, *, rows, heads, pair
):
    cell = pl.program_id(0)
    lowest, highest, key_base, first_most, query_at = (meta[cell, i] for i in range(5))
    for head in range(heads):
        q_all[:, head * rows : (head + 1) * rows] = query_ref[head]
    top[...] = jnp.full_like(top, MASKED)
    total[...] = jnp.zeros_like(total)
    acc[...] = jnp.zeros_like(acc)
    width = pair * rows

    def visit(block, masked):
        start = pl.multiple_of(block * rows, rows)
        keyval = keyval_ref[0, pl.ds(start, rows), :]
        key = keyval[:, :HD]
        value_t = keyval[:, HD:].T
        if masked:
            key_at = key_base + start + lax.broadcasted_iota(jnp.int32, (rows, rows), 0)
            token_at = query_at + lax.broadcasted_iota(jnp.int32, (rows, rows), 1)
            allowed = (key_at <= token_at) & (key_at >= first_ref[0])
            bias = jnp.where(allowed, 0.0, MASKED)
            bias = jnp.concatenate([bias] * pair, axis=1)
        for piece in range(heads // pair):
            cols = slice(piece * width, (piece + 1) * width)
            score = contract(key, q_all[:, cols], 1, 0)
            if masked:
                score = score + bias
            before = top[:, cols]
            now = jnp.maximum(before, jnp.max(score, axis=0, keepdims=True))
            weight = jnp.exp(score - now)
            decay = jnp.exp(before - now)
            top[:, cols] = now
            total[:, cols] = total[:, cols] * decay + jnp.sum(weight, axis=0, keepdims=True)
            acc[:, cols] = acc[:, cols] * decay + contract(value_t, weight.astype(BF), 1, 0)

    def step(block, carry):
        plain = jnp.logical_and(key_base + block * rows >= first_most, block < highest)

        @pl.when(plain)
        def _():
            visit(block, False)

        @pl.when(jnp.logical_not(plain))
        def _():
            visit(block, True)

        return carry

    lax.fori_loop(lowest, highest + 1, step, 0)
    sums = total[...]
    scaled = acc[...] * (1.0 / sums)
    for head in range(heads):
        out_ref[head] = scaled[:, head * rows : (head + 1) * rows].astype(BF)
    lse_ref[0] = top[...] + jnp.log(sums)


def backward_kernel(
    meta,
    query_ref,
    keyval_ref,
    first_ref,
    out_ref,
    lse_ref,
    grad_ref,
    dquery_ref,
    dkeyval_ref,
    q_all,
    g_all,
    delta,
    dq_acc,
    dkv_acc,
    *,
    rows,
    heads,
    pair,
):
    cell = pl.program_id(0)
    lowest, highest, key_base, first_most, query_at = (meta[cell, i] for i in range(5))
    for head in range(heads):
        cols = slice(head * rows, (head + 1) * rows)
        q_all[:, cols] = query_ref[head]
        g_all[:, cols] = grad_ref[head]
        delta[:, cols] = jnp.sum(
            grad_ref[head].astype(F32) * out_ref[head].astype(F32), axis=0, keepdims=True
        )
    dq_acc[...] = jnp.zeros_like(dq_acc)

    @pl.when(cell % 2 == 0)
    def _():
        dkv_acc[...] = jnp.zeros_like(dkv_acc)

    width = pair * rows

    def visit(block, masked):
        start = pl.multiple_of(block * rows, rows)
        keyval = keyval_ref[0, pl.ds(start, rows), :]
        key = keyval[:, :HD]
        value = keyval[:, HD:]
        key_t = key.T
        if masked:
            key_at = key_base + start + lax.broadcasted_iota(jnp.int32, (rows, rows), 0)
            token_at = query_at + lax.broadcasted_iota(jnp.int32, (rows, rows), 1)
            allowed = (key_at <= token_at) & (key_at >= first_ref[0])
            bias = jnp.where(allowed, 0.0, MASKED)
            bias = jnp.concatenate([bias] * pair, axis=1)
        dkey = jnp.zeros((rows, HD), F32)
        dvalue = jnp.zeros((rows, HD), F32)
        for piece in range(heads // pair):
            cols = slice(piece * width, (piece + 1) * width)
            score = contract(key, q_all[:, cols], 1, 0)
            if masked:
                score = score + bias
            weight = jnp.exp(score - lse_ref[0, :, cols])
            dweight = contract(value, g_all[:, cols], 1, 0)
            dscore = (weight * (dweight - delta[:, cols])).astype(BF)
            dq_acc[:, cols] = dq_acc[:, cols] + contract(key_t, dscore, 1, 0)
            dkey = dkey + contract(dscore, q_all[:, cols], 1, 1)
            dvalue = dvalue + contract(weight.astype(BF), g_all[:, cols], 1, 1)
        dkv_acc[pl.ds(start, rows), :] = dkv_acc[pl.ds(start, rows), :] + jnp.concatenate(
            [dkey, dvalue], axis=1
        )

    def step(block, carry):
        plain = jnp.logical_and(key_base + block * rows >= first_most, block < highest)

        @pl.when(plain)
        def _():
            visit(block, False)

        @pl.when(jnp.logical_not(plain))
        def _():
            visit(block, True)

        return carry

    lax.fori_loop(lowest, highest + 1, step, 0)
    scaled = dq_acc[...] * HD ** (-0.5)
    for head in range(heads):
        dquery_ref[head] = scaled[:, head * rows : (head + 1) * rows].astype(BF)

    @pl.when(cell % 2 == 1)
    def _():
        dkeyval_ref[0] = dkv_acc[...].astype(BF)


def attention_specs(rows, heads, keys):
    return dict(
        head=pl.BlockSpec((heads, HD, rows), lambda cell, meta: (0, 0, cell)),
        keyval=pl.BlockSpec((1, keys, 2 * HD), lambda cell, meta: (cell // 2, 0, 0)),
        first=pl.BlockSpec((1, 1, rows), lambda cell, meta: (cell, 0, 0)),
        stat=pl.BlockSpec((1, 1, heads * rows), lambda cell, meta: (cell, 0, 0)),
    )


def attend_forward(meta, query, keyval, first):
    heads, _, tokens = query.shape
    rows = tokens // GROUP
    keys = keyval.shape[1]
    specs = attention_specs(rows, heads, keys)
    wide = heads * rows
    return pl.pallas_call(
        functools.partial(forward_kernel, rows=rows, heads=heads, pair=2),
        grid_spec=pltpu.PrefetchScalarGridSpec(
            num_scalar_prefetch=1,
            grid=(GROUP,),
            in_specs=[specs["head"], specs["keyval"], specs["first"]],
            out_specs=[specs["head"], specs["stat"]],
            scratch_shapes=[
                pltpu.VMEM((HD, wide), BF),
                pltpu.VMEM((1, wide), F32),
                pltpu.VMEM((1, wide), F32),
                pltpu.VMEM((HD, wide), F32),
            ],
        ),
        out_shape=(
            jax.ShapeDtypeStruct(query.shape, BF),
            jax.ShapeDtypeStruct((GROUP, 1, wide), F32),
        ),
        compiler_params=pltpu.CompilerParams(
            dimension_semantics=("arbitrary",), vmem_limit_bytes=48 * 1024 * 1024
        ),
        cost_estimate=pl.CostEstimate(
            flops=40_000_000_000, bytes_accessed=10_000_000, transcendentals=0
        ),
        name="attend_forward",
    )(meta, query, keyval, first)


def attend_backward(meta, query, keyval, first, out, lse, grad):
    heads, _, tokens = query.shape
    rows = tokens // GROUP
    keys = keyval.shape[1]
    specs = attention_specs(rows, heads, keys)
    wide = heads * rows
    return pl.pallas_call(
        functools.partial(backward_kernel, rows=rows, heads=heads, pair=2),
        grid_spec=pltpu.PrefetchScalarGridSpec(
            num_scalar_prefetch=1,
            grid=(GROUP,),
            in_specs=[
                specs["head"],
                specs["keyval"],
                specs["first"],
                specs["head"],
                specs["stat"],
                specs["head"],
            ],
            out_specs=[specs["head"], specs["keyval"]],
            scratch_shapes=[
                pltpu.VMEM((HD, wide), BF),
                pltpu.VMEM((HD, wide), BF),
                pltpu.VMEM((1, wide), F32),
                pltpu.VMEM((HD, wide), F32),
                pltpu.VMEM((keys, 2 * HD), F32),
            ],
        ),
        out_shape=(
            jax.ShapeDtypeStruct(query.shape, BF),
            jax.ShapeDtypeStruct(keyval.shape, BF),
        ),
        compiler_params=pltpu.CompilerParams(
            dimension_semantics=("arbitrary",), vmem_limit_bytes=48 * 1024 * 1024
        ),
        cost_estimate=pl.CostEstimate(
            flops=80_000_000_000, bytes_accessed=16_000_000, transcendentals=0
        ),
        name="attend_backward",
    )(meta, query, keyval, first, out, lse, grad)


def shards(
    tokens,
    starts,
    w_query,
    w_key,
    w_value,
    w_out,
    w_gate,
    w_up,
    w_down,
    norm_attn,
    norm_mlp,
    cotangent,
):
    seq_count = lax.axis_size("seq")
    fsdp_count = lax.axis_size("fsdp")
    deep = seq_count // 2
    wide = fsdp_count // 2
    ring = wide * deep
    half_ring = ring // 2
    f_at, s_at = lax.axis_index("fsdp"), lax.axis_index("seq")
    x_at, y_at, c_at, z_at = f_at % 2, f_at // 2, s_at % 2, s_at // 2
    rows = tokens.shape[1]
    width = tokens.shape[2]
    own_rows = w_query.shape[0]

    def perm_of(move):
        found = []
        for f in range(fsdp_count):
            for s in range(seq_count):
                target = move(f // 2, f % 2, s // 2, s % 2)
                if target is not None:
                    ty, tx, tz, tc = target
                    found.append((f * seq_count + s, (ty * 2 + tx) * seq_count + tz * 2 + tc))
        return found

    def ring_place(position):
        position = position % ring
        row, col = position // deep, position % deep
        return row, col if row % 2 == 0 else deep - 1 - col

    def ring_index(y, z):
        return y * deep + (z if y % 2 == 0 else deep - 1 - z)

    def around(step):
        def move(y, x, z, c):
            ty, tz = ring_place(ring_index(y, z) + step)
            return ty, x, tz, c

        return move

    def along(step):
        return lambda y, x, z, c: (y, x, z + step, c) if 0 <= z + step < deep else None

    core_perm = perm_of(lambda y, x, z, c: (y, x, z, 1 - c))
    x_perm = perm_of(lambda y, x, z, c: (y, 1 - x, z, c))
    cross_perm = perm_of(lambda y, x, z, c: (y, 1 - x, z, 1 - c))
    right_perm, left_perm = perm_of(around(1)), perm_of(around(-1))

    def send(value, perm):
        return lax.ppermute(value, AXES, perm)

    position = y_at * deep + jnp.where(y_at % 2 == 0, z_at, deep - 1 - z_at)

    def place_at(offset):
        index = lax.rem(position + offset + 2 * ring, ring)
        row, col = index // deep, index % deep
        return row, jnp.where(row % 2 == 0, col, deep - 1 - col)

    def gather_group(block):
        near = send(block, core_perm)
        far = send(block, x_perm)
        return jnp.concatenate([block, near, far, send(far, core_perm)], axis=0)

    def to_quarters(pieces):
        return jnp.concatenate(
            [p.reshape(own_rows, GROUP, -1).transpose(1, 0, 2) for p in pieces], axis=2
        )

    def exchange_group(quarters):
        def of(dx, dc):
            return lax.dynamic_index_in_dim(
                quarters, (x_at ^ dx) * 2 + (c_at ^ dc), 0, keepdims=False
            )

        got = [
            [of(0, 0), send(of(0, 1), core_perm)],
            [send(of(1, 0), x_perm), send(of(1, 1), cross_perm)],
        ]
        return got

    def absolute(got):
        rows_of = [swap_pair(c_at, pair) for pair in got]
        ordered = [swap_pair(x_at, [rows_of[0][c], rows_of[1][c]]) for c in range(2)]
        return [[ordered[0][x], ordered[1][x]] for x in range(2)]

    def gather_ring(chunk):
        columns = chunk.shape[2]
        whole = jnp.zeros((wide, 2, deep, chunk.shape[1], columns), chunk.dtype)

        def put(whole, piece, offset, x_from):
            row, col = place_at(offset)
            piece = piece[None, :, None]
            return lax.dynamic_update_slice(whole, piece, (row, x_from, col, 0, 0))

        whole = put(whole, chunk, 0, 0)
        right = left = chunk
        for step in range(1, half_ring):
            right = send(right, right_perm)
            left = send(left, left_perm)
            whole = put(whole, right, -step, 0)
            whole = put(whole, left, step, 0)
        whole = put(whole, send(right[:1], right_perm), half_ring, 0)
        whole = put(whole, send(left[1:], left_perm), half_ring, 1)
        return whole.reshape(-1, columns)

    def scatter_ring(partial):
        columns = partial.shape[1]
        parts = partial.reshape(wide, 2, deep, 2 * own_rows, columns)

        def part(offset, x_from=0, x_count=2):
            row, col = place_at(offset)
            return lax.dynamic_slice(
                parts, (row, x_from, col, 0, 0), (1, x_count, 1, 2 * own_rows, columns)
            ).reshape(x_count, 2 * own_rows, columns)

        right = send(part(half_ring, 0, 1), right_perm)
        left = send(part(half_ring, 1, 1), left_perm)
        for step in range(half_ring - 1, 0, -1):
            to_right, to_left = part(step), part(-step)
            if step == half_ring - 1:
                to_right = jnp.concatenate(
                    [(to_right[:1].astype(F32) + right.astype(F32)).astype(BF), to_right[1:]]
                )
                to_left = jnp.concatenate(
                    [to_left[:1], (to_left[1:].astype(F32) + left.astype(F32)).astype(BF)]
                )
            else:
                to_right = (to_right.astype(F32) + right.astype(F32)).astype(BF)
                to_left = (to_left.astype(F32) + left.astype(F32)).astype(BF)
            right = send(to_right, right_perm)
            left = send(to_left, left_perm)
        own = part(0).astype(F32)
        if half_ring > 1:
            return own + right.astype(F32) + left.astype(F32)
        return own + jnp.concatenate([right, left]).astype(F32)

    def gather_weights(pieces):
        got = absolute(exchange_group(to_quarters(pieces)))
        chunk = jnp.stack([jnp.concatenate(got[x], axis=0) for x in range(2)])
        return gather_ring(chunk)

    def scatter_weights(partial):
        chunk = scatter_ring(partial).astype(BF)
        blocks = [[chunk[x, c * own_rows : (c + 1) * own_rows] for c in range(2)] for x in range(2)]
        relative = absolute(blocks)
        got = [
            [relative[0][0], send(relative[0][1], core_perm)],
            [send(relative[1][0], x_perm), send(relative[1][1], cross_perm)],
        ]
        final = absolute(got)
        return jnp.stack([final[0][0], final[0][1], final[1][0], final[1][1]]).astype(F32)

    def columns_of(quarters):
        return quarters.transpose(1, 0, 2).reshape(own_rows, -1)

    def reduce_group(partial):
        parts = partial.reshape(2, 2, rows, width)
        far = parts[1, 0] + send(parts[1, 1].astype(BF), core_perm).astype(F32)
        near = parts[0, 0] + send(parts[0, 1].astype(BF), core_perm).astype(F32)
        return near + send(far.astype(BF), x_perm).astype(F32)

    own_tokens = tokens[0]
    group_tokens = gather_group(own_tokens)
    weights_attn = gather_weights([w_query, w_key, w_value, w_out.T])
    start_rows = [starts[0], send(starts, x_perm)[0]]
    gains = lax.all_gather(jnp.stack([norm_attn, norm_mlp]), AXES, axis=1, tiled=True)
    gain_attn, gain_mlp = gains[0].astype(F32), gains[1].astype(F32)
    group_cotangent = gather_group(cotangent[0])
    w_gate_q = gather_weights([w_gate])
    w_up_q = gather_weights([w_up])
    w_down_q = gather_weights([w_down.T])

    block_at = [rows * (2 * z_at + (c_at ^ dc)) for dc in range(2)]
    within = jnp.arange(rows, dtype=jnp.int32)
    cells = [(dx, dc) for dx in range(2) for dc in range(2)]
    places = [block_at[dc] + within for dx, dc in cells]
    firsts = [doc_first(start_rows[dx], places[i]) for i, (dx, dc) in enumerate(cells)]
    offsets = jnp.concatenate([p - f for p, f in zip(places, firsts)])
    cos_table, sine_table = rotary_tables(offsets)
    first_rows = jnp.stack(firsts)[:, None, :]
    base_block = 2 * (z_at - deep + 1)
    meta = jnp.stack(
        [
            jnp.stack(
                [
                    firsts[i][0] // rows - base_block,
                    block_at[dc] // rows - base_block,
                    base_block * rows,
                    firsts[i][rows - 1],
                    block_at[dc],
                ]
            )
            for i, (dx, dc) in enumerate(cells)
        ]
    ).astype(jnp.int32)

    per_device = HEADS // GROUP
    q_cols = per_device * HD
    qkv_cols = q_cols + 2 * HD
    group_inputs = group_tokens.astype(F32)
    scale_group = lax.rsqrt(jnp.mean(group_inputs * group_inputs, axis=1, keepdims=True) + EPSILON)
    normed = (group_inputs * scale_group * gain_attn).astype(BF)
    w_qkv, w_out_t = weights_attn[:, :qkv_cols], weights_attn[:, qkv_cols:]
    pre = contract(w_qkv, normed, 0, 1)
    query = (
        rotate(pre[:q_cols].reshape(per_device, HD, -1), cos_table, sine_table) * HD ** (-0.5)
    ).astype(BF)
    key = rotate(pre[q_cols : q_cols + HD][None], cos_table, sine_table)[0].astype(BF)
    keyval = jnp.concatenate([key, pre[q_cols + HD :].astype(BF)], axis=0).T
    keyval = keyval.reshape(2, 2, rows, 2 * HD)
    keyval = jnp.stack([jnp.stack(swap_pair(c_at, [keyval[dx, 0], keyval[dx, 1]])) for dx in range(2)])
    keyval = keyval.reshape(2, 2 * rows, 2 * HD)
    earlier = [send(keyval, perm_of(along(step))) for step in range(deep - 1, 0, -1)]
    keyvals = jnp.concatenate(earlier + [keyval], axis=1)

    attended, lse = attend_forward(meta, query, keyvals, first_rows)
    attended_t = attended.reshape(q_cols, -1)
    middle = own_tokens.astype(F32) + reduce_group(contract(attended_t, w_out_t, 0, 1))

    scale_mlp = lax.rsqrt(jnp.mean(middle * middle, axis=1, keepdims=True) + EPSILON)
    normed_mlp = gather_group((middle * scale_mlp * gain_mlp).astype(BF))
    gate = contract(normed_mlp, w_gate_q, 1, 0)
    up = contract(normed_mlp, w_up_q, 1, 0)
    d_hidden = contract(group_cotangent, w_down_q, 1, 0)
    sigmoid = jax.nn.sigmoid(gate)
    silu = gate * sigmoid
    hidden = (silu * up).astype(BF)
    d_gate = (d_hidden * up * sigmoid * (1.0 + gate * (1.0 - sigmoid))).astype(BF)
    d_up = (d_hidden * silu).astype(BF)
    d_normed_mlp = reduce_group(contract(d_gate, w_gate_q, 1, 1) + contract(d_up, w_up_q, 1, 1))
    result = middle + reduce_group(contract(hidden, w_down_q, 1, 1))
    grad_gate = scatter_weights(contract(normed_mlp, d_gate, 0, 0).astype(BF))
    grad_up = scatter_weights(contract(normed_mlp, d_up, 0, 0).astype(BF))
    grad_down = scatter_weights(contract(group_cotangent, hidden, 0, 0).astype(BF))

    def norm_backward(values, scale_rows, gain, grads_in):
        weighted = grads_in * gain
        gain_grad = jnp.sum(grads_in * values * scale_rows, axis=0)
        inner_mean = jnp.mean(weighted * values, axis=1, keepdims=True)
        cube = scale_rows * scale_rows * scale_rows
        return scale_rows * weighted - values * cube * inner_mean, gain_grad

    d_middle, gain_grad_mlp = norm_backward(middle, scale_mlp, gain_mlp, d_normed_mlp)
    d_middle = d_middle + cotangent[0].astype(F32)

    d_branch = gather_group(d_middle.astype(BF))
    d_attended = contract(w_out_t, d_branch, 0, 1).astype(BF).reshape(query.shape)
    grad_out_t = contract(d_branch, attended_t, 0, 1).astype(BF)
    d_query, d_keyvals = attend_backward(meta, query, keyvals, first_rows, attended, lse, d_attended)
    d_chunks = d_keyvals.reshape(2, deep, 2 * rows, 2 * HD)
    d_keyval = d_chunks[:, deep - 1].astype(F32)
    for step in range(1, deep):
        d_keyval = d_keyval + send(d_chunks[:, deep - 1 - step], perm_of(along(-step))).astype(F32)
    d_keyval = d_keyval.reshape(2, 2, rows, 2 * HD)
    d_keyval = jnp.stack([jnp.stack(swap_pair(c_at, [d_keyval[dx, 0], d_keyval[dx, 1]])) for dx in range(2)])
    d_keyval = d_keyval.reshape(GROUP * rows, 2 * HD).T
    d_query_pre = unrotate(d_query.astype(F32), cos_table, sine_table).astype(BF)
    d_key_pre = unrotate(d_keyval[None, :HD], cos_table, sine_table)[0].astype(BF)
    d_pre = jnp.concatenate(
        [d_query_pre.reshape(q_cols, -1), d_key_pre, d_keyval[HD:].astype(BF)], axis=0
    )
    d_normed = reduce_group(contract(d_pre, w_qkv, 0, 1))
    grad_qkv = contract(normed, d_pre, 0, 1).astype(BF)
    grad_attn = scatter_weights(jnp.concatenate([grad_qkv, grad_out_t], axis=1))
    inputs = own_tokens.astype(F32)
    scale_attn = scale_group[:rows]
    d_inputs, gain_grad_attn = norm_backward(inputs, scale_attn, gain_attn, d_normed)
    d_inputs = d_inputs + d_middle

    gain_grads = lax.psum_scatter(
        jnp.stack([gain_grad_attn, gain_grad_mlp]), AXES, scatter_dimension=1, tiled=True
    )
    return (
        result.astype(BF)[None],
        d_inputs.astype(BF)[None],
        columns_of(grad_attn[:, :, :q_cols]),
        columns_of(grad_attn[:, :, q_cols : q_cols + HD]),
        columns_of(grad_attn[:, :, q_cols + HD : qkv_cols]),
        columns_of(grad_attn[:, :, qkv_cols:]).T,
        columns_of(grad_gate),
        columns_of(grad_up),
        columns_of(grad_down).T,
        gain_grads[0],
        gain_grads[1],
    )


def solution(mesh):
    token_spec = P("fsdp", "seq", None)
    row_spec = P(AXES, None)
    column_spec = P(None, AXES)
    gain_spec = P(AXES)
    return jax.shard_map(
        shards,
        mesh=mesh,
        in_specs=(
            token_spec,
            P("fsdp", None),
            row_spec,
            row_spec,
            row_spec,
            column_spec,
            row_spec,
            row_spec,
            column_spec,
            gain_spec,
            gain_spec,
            token_spec,
        ),
        out_specs=(
            token_spec,
            token_spec,
            row_spec,
            row_spec,
            row_spec,
            column_spec,
            row_spec,
            row_spec,
            column_spec,
            gain_spec,
            gain_spec,
        ),
        check_vma=False,
    )
```

time: 2810 us -> 1300 us (0.46)
  waiting for transfers between devices: 1930 us -> 609 us
  matrix products: 451 us -> 185 us
  starting transfers between devices: 26.3 us -> 148 us
  blocking collectives: 109 us -> 42.1 us
  Pallas kernels: 0 us -> 42.2 us
  loops' own time: 35.2 us -> 0 us
    reduce_scatter x7 -> x0, waiting for transfers between devices: 847 us -> none  [the longest x1 228 us: shards(): lax.psum_scatter(grad_down.reshape(grad_down.shape[0], fsdp_count, -1).as...]
    all_gather x12 -> x0, waiting for transfers between devices: 701 us -> none  [the longest x1 187 us: shards(): lax.all_gather(sectioned_parts[5], 'seq', axis=1, tiled=True)]
    ppermute x0 -> x119, waiting for transfers between devices: none -> 482 us  [send(): return lax.ppermute(value, AXES, perm)]
    dot_general x120 -> x0, matrix products: 281 us -> none  [the longest x26 96.4 us: block_probs(): jnp.einsum('pdq,dk->pqk', grad_part, keyval_part[HD:], preferred_element_...]
    ppermute x0 -> x119, starting transfers between devices: none -> 148 us  [send(): return lax.ppermute(value, AXES, perm)]
    unnamed x37 -> x2, waiting for transfers between devices: 275 us -> 127 us
    all_to_all x6 -> x0, waiting for transfers between devices: 105 us -> none  [the longest x1 37.7 us: shards(): lax.all_to_all(back_attended, 'seq', split_axis=0, concat_axis=2, tiled=T...]
    unnamed x3 -> x12, other arithmetic: 51.8 us -> 1.54 us
  transfers between devices with their start and end apart: 34 -> 120, of which waited for: 28 -> 55; matrix products, arithmetic and copies ran while one was open for 12% -> 23% of each run, Pallas kernels for 0% -> 1%
where the time goes in v1:
time: 1300 us; the launch traced here: 1290 us
  waiting for transfers between devices  609 us (47%)
  matrix products  185 us (14%)
  starting transfers between devices  148 us (11%)
  local copies, waits for them, and re-layouts  128 us (10%)
  other arithmetic  107 us (8%)
  Pallas kernels  42.2 us (3%)
  blocking collectives  42.1 us (3%)
  between operations  24.8 us (2%)
    ppermute x119, waiting for transfers between devices, send(): return lax.ppermute(value, AXES, perm)  482 us
    dot_general x15, matrix products, contract(): lax.dot_general(left, right, (((left_dim,), (right_dim,)), ((), ())), pre...  185 us
    ppermute x119, starting transfers between devices, send(): return lax.ppermute(value, AXES, perm)  148 us
    unnamed x2, waiting for transfers between devices  127 us
    all_gather x1, blocking collectives, shards(): lax.all_gather(jnp.stack([norm_attn, norm_mlp]), AXES, axis=1, tiled=True)  42.1 us
    unnamed x230, local copies, waits for them, and re-layouts  36.7 us
  transfers between devices with their start and end apart: 120, of which 55 were waited for; matrix products, arithmetic and copies ran while one was open for 23% of the time, Pallas kernels for 1%

profile of v1, /device:TPU:0, one launch (start us, length us, event | category | flops | bytes accessed | tf_op | source)
XLA Modules:
  0.0 1285.5 jit_solution(790256379582586470)
XLA Ops:
  20.9 42.1 %all-gather = bf16[32,64,2]{1,2,0:T(2,128)(2,1)S(1)} all-gather(bf16[1,64,2]{1,2,0:T(2,128)(2,1)S(1)} %maximum_bitcast_fusion.13), channel_id=1, replica_groups=mesh['fsdp'=4,'seq'=8] {'fsdp','seq'}, dimensions={0}, use_global_device_ids=true | all-gather | bytes 8448 | tf_op jit(solution)/shard_map/all_gather | solution.py:468
  133.8 14.4 %collective-permute-done.38 = bf16[2,128,1408]{2,1,0:T(8,128)(2,1)S(1)} collective-permute-done((bf16[2,128,1408]{2,1,0:T(8,128)(2,1)S(1)}, bf16[2,128,1408]{2,1,0:T(8,128)(2,1)S(1)}, u32[]{:S(2)}, u32[]{:S(2)}) %collective-permute-start.38) | collective-permute-done | bytes 720928 | tf_op jit(solution)/shard_map/ppermute | solution.py:352
  150.5 14.0 %collective-permute-done.49 = bf16[2,128,1408]{2,1,0:T(8,128)(2,1)S(1)} collective-permute-done((bf16[2,128,1408]{2,1,0:T(8,128)(2,1)S(1)}, bf16[2,128,1408]{2,1,0:T(8,128)(2,1)S(1)}, u32[]{:S(2)}, u32[]{:S(2)}) %collective-permute-start.49) | collective-permute-done | bytes 720928 | tf_op jit(solution)/shard_map/ppermute | solution.py:352
  166.8 13.8 %collective-permute-done.27 = bf16[2,128,1408]{2,1,0:T(8,128)(2,1)S(1)} collective-permute-done((bf16[2,128,1408]{2,1,0:T(8,128)(2,1)S(1)}, bf16[2,128,1408]{2,1,0:T(8,128)(2,1)S(1)}, u32[]{:S(2)}, u32[]{:S(2)}) %collective-permute-start.27) | collective-permute-done | bytes 720928 | tf_op jit(solution)/shard_map/ppermute | solution.py:352
  196.6 14.1 %collective-permute-done.40 = bf16[2,128,1408]{2,1,0:T(8,128)(2,1)} collective-permute-done((bf16[2,128,1408]{2,1,0:T(8,128)(2,1)S(1)}, bf16[2,128,1408]{2,1,0:T(8,128)(2,1)}, u32[]{:S(2)}, u32[]{:S(2)}) %collective-permute-start.40) | collective-permute-done | bytes 720928 | tf_op jit(solution)/shard_map/ppermute | solution.py:352
  230.4 12.9 %collective-permute-done.29 = bf16[2,128,1408]{2,1,0:T(8,128)(2,1)S(1)} collective-permute-done((bf16[2,128,1408]{2,1,0:T(8,128)(2,1)S(1)}, bf16[2,128,1408]{2,1,0:T(8,128)(2,1)S(1)}, u32[]{:S(2)}, u32[]{:S(2)}) %collective-permute-start.29) | collective-permute-done | bytes 720928 | tf_op jit(solution)/shard_map/ppermute | solution.py:352
  296.6 16.5 %collective-permute-start.53 = (bf16[2,128,1408]{2,1,0:T(8,128)(2,1)}, bf16[2,128,1408]{2,1,0:T(8,128)(2,1)}, u32[]{:S(2)}, u32[]{:S(2)}) collective-permute-start(bf16[2,128,1408]{2,1,0:T(8,128)(2,1)} %collective-permute-done.51), channel_id=1, source_target_pairs={{0,2},{1,3},{2,4},{3,5},{4,6},{5,7},{6,22},{7,23},{8,10},{9,11},{1... | collective-permute-start | bytes 2162696 | tf_op jit(solution)/shard_map/ppermute | solution.py:352
  322.9 18.5 %attend_forward.1 = (bf16[8,64,1536]{2,1,0:T(8,128)(2,1)S(1)}, f32[4,1,3072]{2,1,0:T(1,128)S(1)}) custom-call(s32[4,5]{1,0:T(4,128)S(1)} %pad_add_fusion.1.meta, bf16[8,64,1536]{2,1,0:T(8,128)(2,1)S(1)} %fusion.29.query_ref, bf16[2,3072,128]{2,1,0:T(8,128)(2,1)S(1)} %maximum_maximum_fusion.keyval_ref, s32[4,1,384]{2,1,0:T(1,128)S(1)} %broadcast_in_dim.190.first_ref), custom_call_target="tpu_custom_call" | custom-call | flops 40000000000 | bytes 10000000 | tf_op jit(solution)/shard_map/attend_forward/pallas_call | solution.py:222
  353.3 19.0 %collective-permute-start.31 = (bf16[2,128,1408]{2,1,0:T(8,128)(2,1)S(1)}, bf16[2,128,1408]{2,1,0:T(8,128)(2,1)S(1)}, u32[]{:S(2)}, u32[]{:S(2)}) collective-permute-start(bf16[2,128,1408]{2,1,0:T(8,128)(2,1)S(1)} %copy-done.44), channel_id=1, source_target_pairs={{0,2},{1,3},{2,4},{3,5},{4,6},{5,7},{6,22},{7,23},{8,10},{9,11},{1... | collective-permute-start | bytes 2162696 | tf_op jit(solution)/shard_map/ppermute | solution.py:352
  374.3 12.5 collective-permute-done.54
  394.1 27.7 %collective-permute-done.32 = bf16[2,128,1408]{2,1,0:T(8,128)(2,1)S(1)} collective-permute-done((bf16[2,128,1408]{2,1,0:T(8,128)(2,1)S(1)}, bf16[2,128,1408]{2,1,0:T(8,128)(2,1)S(1)}, u32[]{:S(2)}, u32[]{:S(2)}) %collective-permute-start.32) | collective-permute-done | bytes 720928 | tf_op jit(solution)/shard_map/ppermute | solution.py:352
  462.3 19.9 %collective-permute-done.22 = bf16[384,2048]{1,0:T(8,128)(2,1)S(1)} collective-permute-done((bf16[384,2048]{1,0:T(8,128)(2,1)S(1)}, bf16[384,2048]{1,0:T(8,128)(2,1)S(1)}, u32[]{:S(2)}, u32[]{:S(2)}) %collective-permute-start.22) | collective-permute-done | bytes 1572896 | tf_op jit(solution)/shard_map/ppermute | solution.py:352
  482.3 15.8 %fusion.66 = f32[1536,1408]{1,0:T(8,128)} fusion(bf16[2048,1408]{1,0:T(8,128)(2,1)S(1)} %bitcast.752, bf16[384,2048]{1,0:T(8,128)(2,1)} %collective-permute-done.62, bf16[384,2048]{1,0:T(8,128)(2,1)} %collective-permute-done.61, bf16[384,2048]{1,0:T(8,128)(2,1)} %collective-permute-done.60, bf16[384,2048]{1,0:T(8,128)(2,1)S(1)} %bitcast.785), kind=kOutput, calls=%fused_computation.138 | convolution fusion | flops 8883535872 | bytes 20709376 | tf_op jit(solution)/shard_map/dot_general | solution.py:23
  498.1 15.6 %fusion.106 = f32[1536,1408]{1,0:T(8,128)} fusion(bf16[2048,1408]{1,0:T(8,128)(2,1)S(1)} %bitcast.746, bf16[384,2048]{1,0:T(8,128)(2,1)} %collective-permute-done.23, bf16[384,2048]{1,0:T(8,128)(2,1)S(1)} %collective-permute-done.22, bf16[384,2048]{1,0:T(8,128)(2,1)} %collective-permute-done.21, bf16[384,2048]{1,0:T(8,128)(2,1)S(1)} %multiply_convert_fusion.3), kind=kOutput, calls=%fused_computation.450 | convolution fusion | flops 8883535872 | bytes 20709376 | tf_op jit(solution)/shard_map/dot_general | solution.py:23
  513.8 22.7 %multiply_convert_fusion.1 = (bf16[1536,1408]{1,0:T(8,128)(2,1)}, bf16[1536,1408]{1,0:T(8,128)(2,1)}, bf16[1536,1408]{1,0:T(8,128)(2,1)S(1)}) fusion(f32[1536,1408]{1,0:T(8,128)} %fusion.66, f32[1536,1408]{1,0:T(8,128)} %fusion.106, bf16[2048,1408]{1,0:T(8,128)(2,1)} %bitcast.740, bf16[384,2048]{1,0:T(8,128)(2,1)} %collective-permute-done.23, ...), kind=kOutput, calls=%fused_computation.6 | convolution fusion | flops 8915976192 | bytes 42336256 | tf_op jit(solution)/shard_map/dot_general | solution.py:23
  536.5 13.6 %convolution_convert_fusion = bf16[2048,1408]{1,0:T(8,128)(2,1)S(1)} fusion(bf16[1536,1408]{1,0:T(8,128)(2,1)S(1)} %get-tuple-element.63, bf16[384,2048]{1,0:T(8,128)(2,1)} %collective-permute-done.62, bf16[384,2048]{1,0:T(8,128)(2,1)} %collective-permute-done.61, bf16[384,2048]{1,0:T(8,128)(2,1)} %collective-permute-done.60, ...), kind=kOutput, calls=%fused_computation.11 | convolution fusion | flops 8886419456 | bytes 16384000 | tf_op jit(solution)/shard_map/dot_general | solution.py:23
  553.8 13.5 %convolution_convert_fusion.2 = bf16[2048,1408]{1,0:T(8,128)(2,1)S(1)} fusion(bf16[1536,1408]{1,0:T(8,128)(2,1)} %get-tuple-element.61, bf16[384,2048]{1,0:T(8,128)(2,1)} %collective-permute-done.23, bf16[384,2048]{1,0:T(8,128)(2,1)S(1)} %copy-done.82, bf16[384,2048]{1,0:T(8,128)(2,1)} %collective-permute-done.21, ...), kind=kOutput, calls=%fused_computation.13 | convolution fusion | flops 8886419456 | bytes 16384000 | tf_op jit(solution)/shard_map/dot_general | solution.py:23
  570.5 14.5 %fusion.116 = f32[1536,2048]{1,0:T(8,128)} fusion(bf16[1536,1408]{1,0:T(8,128)(2,1)} %get-tuple-element.62, bf16[2048,1408]{1,0:T(8,128)(2,1)S(1)} %bitcast.749), kind=kOutput, calls=%fused_computation.460 | convolution fusion | flops 8858370048 | bytes 22675456 | tf_op jit(solution)/shard_map/dot_general | solution.py:23
  585.1 13.2 %convolution_convert_fusion.1 = bf16[2048,1408]{1,0:T(8,128)(2,1)S(1)} fusion(bf16[1536,1408]{1,0:T(8,128)(2,1)} %get-tuple-element.62, bf16[384,2048]{1,0:T(8,128)(2,1)} %collective-permute-done.23, bf16[384,2048]{1,0:T(8,128)(2,1)S(1)} %copy-done.83, bf16[384,2048]{1,0:T(8,128)(2,1)} %collective-permute-done.21, ...), kind=kOutput, calls=%fused_computation.12 | convolution fusion | flops 8886419456 | bytes 16384000 | tf_op jit(solution)/shard_map/dot_general | solution.py:23
  602.7 16.3 %convolution_add_fusion = f32[1536,2048]{1,0:T(8,128)} fusion(f32[1536,2048]{1,0:T(8,128)} %fusion.116, bf16[1536,1408]{1,0:T(8,128)(2,1)} %get-tuple-element.61, bf16[2048,1408]{1,0:T(8,128)(2,1)S(1)} %bitcast.743), kind=kOutput, calls=%fused_computation.10 | convolution fusion | flops 8861515776 | bytes 35258368 | tf_op jit(solution)/shard_map/dot_general | solution.py:23
  629.3 17.1 %fusion.115 = (bf16[2,2,384,2048]{3,2,1,0:T(8,128)(2,1)}, f32[2,2,384,2048]{3,2,1,0:T(8,128)}) fusion(bf16[2,2,384,1408]{3,2,1,0:T(8,128)(2,1)} %bitcast.831, bf16[2048,1408,1,1]{1,0,3,2:T(8,128)(2,1)} %bitcast.753), kind=kOutput, calls=%fused_computation.459 | convolution fusion | flops 8861515776 | bytes 28966912 | tf_op jit(solution)/shard_map/dot_general | solution.py:23
  676.1 12.4 collective-permute-done.87
  689.8 13.3 %collective-permute-done.98 = bf16[2,128,1408]{2,1,0:T(8,128)(2,1)S(1)} collective-permute-done((bf16[2,128,1408]{2,1,0:T(8,128)(2,1)S(1)}, bf16[2,128,1408]{2,1,0:T(8,128)(2,1)S(1)}, u32[]{:S(2)}, u32[]{:S(2)}) %collective-permute-start.98) | collective-permute-done | bytes 720928 | tf_op jit(solution)/shard_map/ppermute | solution.py:352
  757.8 13.1 %collective-permute-done.92 = bf16[2,128,1408]{2,1,0:T(8,128)(2,1)S(1)} collective-permute-done((bf16[2,128,1408]{2,1,0:T(8,128)(2,1)S(1)}, bf16[2,128,1408]{2,1,0:T(8,128)(2,1)S(1)}, u32[]{:S(2)}, u32[]{:S(2)}) %collective-permute-start.92) | collective-permute-done | bytes 720928 | tf_op jit(solution)/shard_map/ppermute | solution.py:352
  791.8 15.4 %collective-permute-done.59 = bf16[384,2048]{1,0:T(8,128)(2,1)S(1)} collective-permute-done((bf16[384,2048]{1,0:T(8,128)(2,1)}, bf16[384,2048]{1,0:T(8,128)(2,1)S(1)}, u32[]{:S(2)}, u32[]{:S(2)}) %collective-permute-start.59) | collective-permute-done | bytes 1572896 | tf_op jit(solution)/shard_map/ppermute | solution.py:352
  841.2 14.6 %collective-permute-done.116 = bf16[64,1408]{1,0:T(8,128)(2,1)S(1)} collective-permute-done((bf16[64,1408]{1,0:T(8,128)(2,1)S(1)}, bf16[64,1408]{1,0:T(8,128)(2,1)S(1)}, u32[]{:S(2)}, u32[]{:S(2)}) %collective-permute-start.116) | collective-permute-done | bytes 180256 | tf_op jit(solution)/shard_map/ppermute | solution.py:352
  885.3 23.7 %attend_backward.1 = (bf16[8,64,1536]{2,1,0:T(8,128)(2,1)S(1)}, bf16[2,3072,128]{2,1,0:T(8,128)(2,1)S(1)}) custom-call(s32[4,5]{1,0:T(4,128)S(1)} %pad_add_fusion.1.meta, bf16[8,64,1536]{2,1,0:T(8,128)(2,1)S(1)} %copy-done.4, bf16[2,3072,128]{2,1,0:T(8,128)(2,1)} %copy-done.2, s32[4,1,384]{2,1,0:T(1,128)S(1)} %broadcast_in_dim.190.first_ref, ...), custom_call_target="tpu_custom_call" | custom-call | flops 80000000000 | bytes 16000000 | tf_op jit(solution)/shard_map/attend_backward/pallas_call | solution.py:256
  920.5 20.9 %collective-permute-done.69 = bf16[2,768,128]{2,1,0:T(8,128)(2,1)S(1)} collective-permute-done((bf16[2,768,128]{2,1,0:T(8,128)(2,1)S(1)}, bf16[2,768,128]{2,1,0:T(8,128)(2,1)S(1)}, u32[]{:S(2)}, u32[]{:S(2)}) %collective-permute-start.69) | collective-permute-done | bytes 393248 | tf_op jit(solution)/shard_map/ppermute | solution.py:352
  941.4 29.1 %collective-permute-done.71 = bf16[2,768,128]{2,1,0:T(8,128)(2,1)S(1)} collective-permute-done((bf16[2,768,128]{2,1,0:T(8,128)(2,1)S(1)}, bf16[2,768,128]{2,1,0:T(8,128)(2,1)S(1)}, u32[]{:S(2)}, u32[]{:S(2)}) %collective-permute-start.71) | collective-permute-done | bytes 393248 | tf_op jit(solution)/shard_map/ppermute | solution.py:352
  970.5 14.4 %collective-permute-done.70 = bf16[2,768,128]{2,1,0:T(8,128)(2,1)S(1)} collective-permute-done((bf16[2,768,128]{2,1,0:T(8,128)(2,1)S(1)}, bf16[2,768,128]{2,1,0:T(8,128)(2,1)S(1)}, u32[]{:S(2)}, u32[]{:S(2)}) %collective-permute-start.70) | collective-permute-done | bytes 393248 | tf_op jit(solution)/shard_map/ppermute | solution.py:352
  1106.0 25.5 %collective-permute-done.84 = bf16[64,1152]{1,0:T(8,128)(2,1)S(1)} collective-permute-done((bf16[64,1152]{1,0:T(8,128)(2,1)S(1)}, bf16[64,1152]{1,0:T(8,128)(2,1)S(1)}, u32[]{:S(2)}, u32[]{:S(2)}) %collective-permute-start.84) | collective-permute-done | bytes 147488 | tf_op jit(solution)/shard_map/ppermute | solution.py:352
  1148.7 127.4 %reduce-scatter.4.cloned.1.call-done = f32[64,2]{1,0:T(8,128)} async-done(((f32[2048,2]{1,0:T(8,128)}), f32[64,2]{1,0:T(8,128)}) %reduce-scatter.4.cloned.1.call-update) | async-done | bytes 528
  (681 shorter events, 583.2 us)
Async XLA Ops:
  7.2 1268.9 %reduce-scatter.4.cloned.1.call-start = ((), (), s32[]{:S(2)}) async-start(), calls=%async_computation.1 | async-start | bytes 1081344
  7.2 240.3 %collective-permute-start.61 = (bf16[384,2048]{1,0:T(8,128)(2,1)}, bf16[384,2048]{1,0:T(8,128)(2,1)}, u32[]{:S(2)}, u32[]{:S(2)}) collective-permute-start(bf16[384,2048]{1,0:T(8,128)(2,1)} %bitcast.783), channel_id=1, source_target_pairs={{0,8},{1,9},{2,10},{3,11},{4,12},{5,13},{6,14},{7,15},{8,0},{9,1},... | collective-permute-start | bytes 4718600 | tf_op jit(solution)/shard_map/ppermute | solution.py:352
  10.2 472.0 %collective-permute-start.60 = (bf16[384,2048]{1,0:T(8,128)(2,1)}, bf16[384,2048]{1,0:T(8,128)(2,1)}, u32[]{:S(2)}, u32[]{:S(2)}) collective-permute-start(bf16[384,2048]{1,0:T(8,128)(2,1)} %bitcast.784), channel_id=1, source_target_pairs={{0,1},{1,0},{2,3},{3,2},{4,5},{5,4},{6,7},{7,6},{8,9},{9,8},{10,11... | collective-permute-start | bytes 4718600 | tf_op jit(solution)/shard_map/ppermute | solution.py:352
  10.2 65.7 %collective-permute-start = (s32[1,3]{1,0:T(1,128)}, s32[1,3]{1,0:T(1,128)S(1)}, u32[]{:S(2)}, u32[]{:S(2)}) collective-permute-start(s32[1,3]{1,0:T(1,128)} %param.13), channel_id=1, source_target_pairs={{0,8},{1,9},{2,10},{3,11},{4,12},{5,13},{6,14},{7,15},{8,0},{9,1},... | collective-permute-start | bytes 44 | tf_op jit(solution)/shard_map/ppermute | solution.py:352
  18.0 71.9 %collective-permute-start.1 = (bf16[64,1152]{1,0:T(8,128)(2,1)}, bf16[64,1152]{1,0:T(8,128)(2,1)S(1)}, u32[]{:S(2)}, u32[]{:S(2)}) collective-permute-start(bf16[64,1152]{1,0:T(8,128)(2,1)} %bitcast.712), channel_id=1, source_target_pairs={{0,9},{1,8},{2,11},{3,10},{4,13},{5,12},{6,15},{7,14},{8,1},{9,0},... | collective-permute-start | bytes 442376 | tf_op jit(solution)/shard_map/ppermute | solution.py:352
  20.4 69.6 %collective-permute-start.2 = (bf16[64,1152]{1,0:T(8,128)(2,1)}, bf16[64,1152]{1,0:T(8,128)(2,1)}, u32[]{:S(2)}, u32[]{:S(2)}) collective-permute-start(bf16[64,1152]{1,0:T(8,128)(2,1)} %bitcast.711), channel_id=1, source_target_pairs={{0,8},{1,9},{2,10},{3,11},{4,12},{5,13},{6,14},{7,15},{8,0},{9,1},... | collective-permute-start | bytes 442376 | tf_op jit(solution)/shard_map/ppermute | solution.py:352
  112.0 135.6 %collective-permute-start.13 = (bf16[384,2048]{1,0:T(8,128)(2,1)S(1)}, bf16[384,2048]{1,0:T(8,128)(2,1)S(1)}, u32[]{:S(2)}, u32[]{:S(2)}) collective-permute-start(bf16[384,2048]{1,0:T(8,128)(2,1)S(1)} %bitcast.729), channel_id=1, source_target_pairs={{0,8},{1,9},{2,10},{3,11},{4,12},{5,13},{6,14},{7,15},{8,0},{9,1},... | collective-permute-start | bytes 4718600 | tf_op jit(solution)/shard_map/ppermute | solution.py:352
  247.6 234.7 %collective-permute-start.62 = (bf16[384,2048]{1,0:T(8,128)(2,1)}, bf16[384,2048]{1,0:T(8,128)(2,1)}, u32[]{:S(2)}, u32[]{:S(2)}) collective-permute-start(bf16[384,2048]{1,0:T(8,128)(2,1)} %collective-permute-done.61), channel_id=1, source_target_pairs={{0,1},{1,0},{2,3},{3,2},{4,5},{5,4},{6,7},{7,6},{8,9},{9,8},{10,11... | collective-permute-start | bytes 4718600 | tf_op jit(solution)/shard_map/ppermute | solution.py:352
  296.6 56.7 %collective-permute-start.53 = (bf16[2,128,1408]{2,1,0:T(8,128)(2,1)}, bf16[2,128,1408]{2,1,0:T(8,128)(2,1)}, u32[]{:S(2)}, u32[]{:S(2)}) collective-permute-start(bf16[2,128,1408]{2,1,0:T(8,128)(2,1)} %collective-permute-done.51), channel_id=1, source_target_pairs={{0,2},{1,3},{2,4},{3,5},{4,6},{5,7},{6,22},{7,23},{8,10},{9,11},{1... | collective-permute-start | bytes 2162696 | tf_op jit(solution)/shard_map/ppermute | solution.py:352
  313.2 35.8 %collective-permute-start.42 = (bf16[2,128,1408]{2,1,0:T(8,128)(2,1)}, bf16[2,128,1408]{2,1,0:T(8,128)(2,1)}, u32[]{:S(2)}, u32[]{:S(2)}) collective-permute-start(bf16[2,128,1408]{2,1,0:T(8,128)(2,1)} %collective-permute-done.40), channel_id=1, source_target_pairs={{0,2},{1,3},{2,4},{3,5},{4,6},{5,7},{6,22},{7,23},{8,10},{9,11},{1... | collective-permute-start | bytes 2162696 | tf_op jit(solution)/shard_map/ppermute | solution.py:352
  349.0 38.9 %collective-permute-start.19 = (bf16[384,2048]{1,0:T(8,128)(2,1)S(1)}, bf16[384,2048]{1,0:T(8,128)(2,1)S(1)}, u32[]{:S(2)}, u32[]{:S(2)}) collective-permute-start(bf16[384,2048]{1,0:T(8,128)(2,1)S(1)} %get-tuple-element.71), channel_id=1, source_target_pairs={{0,1},{1,0},{2,3},{3,2},{4,5},{5,4},{6,7},{7,6},{8,9},{9,8},{10,11... | collective-permute-start | bytes 4718600 | tf_op jit(solution)/shard_map/ppermute | solution.py:352
  387.8 53.2 %collective-permute-start.18 = (bf16[384,2048]{1,0:T(8,128)(2,1)S(1)}, bf16[384,2048]{1,0:T(8,128)(2,1)S(1)}, u32[]{:S(2)}, u32[]{:S(2)}) collective-permute-start(bf16[384,2048]{1,0:T(8,128)(2,1)S(1)} %get-tuple-element.70), channel_id=1, source_target_pairs={{0,1},{1,0},{2,3},{3,2},{4,5},{5,4},{6,7},{7,6},{8,9},{9,8},{10,11... | collective-permute-start | bytes 4718600 | tf_op jit(solution)/shard_map/ppermute | solution.py:352
  388.4 53.7 %collective-permute-start.20 = (bf16[384,2048]{1,0:T(8,128)(2,1)S(1)}, bf16[384,2048]{1,0:T(8,128)(2,1)S(1)}, u32[]{:S(2)}, u32[]{:S(2)}) collective-permute-start(bf16[384,2048]{1,0:T(8,128)(2,1)S(1)} %fusion.26), channel_id=1, source_target_pairs={{0,8},{1,9},{2,10},{3,11},{4,12},{5,13},{6,14},{7,15},{8,0},{9,1},... | collective-permute-start | bytes 4718600 | tf_op jit(solution)/shard_map/ppermute | solution.py:352
  462.3 35.8 %collective-permute-start.21 = (bf16[384,2048]{1,0:T(8,128)(2,1)S(1)}, bf16[384,2048]{1,0:T(8,128)(2,1)}, u32[]{:S(2)}, u32[]{:S(2)}) collective-permute-start(bf16[384,2048]{1,0:T(8,128)(2,1)S(1)} %multiply_convert_fusion.3), channel_id=1, source_target_pairs={{0,1},{1,0},{2,3},{3,2},{4,5},{5,4},{6,7},{7,6},{8,9},{9,8},{10,11... | collective-permute-start | bytes 4718600 | tf_op jit(solution)/shard_map/ppermute | solution.py:352
  551.3 97.4 %collective-permute-start.108 = (bf16[1,128,1408]{2,1,0:T(8,128)(2,1)}, bf16[1,128,1408]{2,1,0:T(8,128)(2,1)}, u32[]{:S(2)}, u32[]{:S(2)}) collective-permute-start(bf16[1,128,1408]{2,1,0:T(8,128)(2,1)} %get-tuple-element.76), channel_id=1, source_target_pairs={{0,2},{1,3},{2,4},{3,5},{4,6},{5,7},{6,22},{7,23},{8,10},{9,11},{1... | collective-permute-start | bytes 1081352 | tf_op jit(solution)/shard_map/ppermute | solution.py:352
  553.1 95.9 %collective-permute-start.112 = (bf16[1,128,1408]{2,1,0:T(8,128)(2,1)}, bf16[1,128,1408]{2,1,0:T(8,128)(2,1)}, u32[]{:S(2)}, u32[]{:S(2)}) collective-permute-start(bf16[1,128,1408]{2,1,0:T(8,128)(2,1)} %get-tuple-element.79), channel_id=1, source_target_pairs={{0,16},{1,17},{2,0},{3,1},{4,2},{5,3},{6,4},{7,5},{8,24},{9,25},{1... | collective-permute-start | bytes 1081352 | tf_op jit(solution)/shard_map/ppermute | solution.py:352
  568.5 82.9 %collective-permute-start.86 = (bf16[1,128,1408]{2,1,0:T(8,128)(2,1)}, bf16[1,128,1408]{2,1,0:T(8,128)(2,1)}, u32[]{:S(2)}, u32[]{:S(2)}) collective-permute-start(bf16[1,128,1408]{2,1,0:T(8,128)(2,1)} %get-tuple-element.92), channel_id=1, source_target_pairs={{0,2},{1,3},{2,4},{3,5},{4,6},{5,7},{6,22},{7,23},{8,10},{9,11},{1... | collective-permute-start | bytes 1081352 | tf_op jit(solution)/shard_map/ppermute | solution.py:352
  570.3 81.2 %collective-permute-start.90 = (bf16[1,128,1408]{2,1,0:T(8,128)(2,1)}, bf16[1,128,1408]{2,1,0:T(8,128)(2,1)}, u32[]{:S(2)}, u32[]{:S(2)}) collective-permute-start(bf16[1,128,1408]{2,1,0:T(8,128)(2,1)} %get-tuple-element.95), channel_id=1, source_target_pairs={{0,16},{1,17},{2,0},{3,1},{4,2},{5,3},{6,4},{7,5},{8,24},{9,25},{1... | collective-permute-start | bytes 1081352 | tf_op jit(solution)/shard_map/ppermute | solution.py:352
  600.8 53.1 %collective-permute-start.97 = (bf16[1,128,1408]{2,1,0:T(8,128)(2,1)S(1)}, bf16[1,128,1408]{2,1,0:T(8,128)(2,1)}, u32[]{:S(2)}, u32[]{:S(2)}) collective-permute-start(bf16[1,128,1408]{2,1,0:T(8,128)(2,1)S(1)} %get-tuple-element.84), channel_id=1, source_target_pairs={{0,2},{1,3},{2,4},{3,5},{4,6},{5,7},{6,22},{7,23},{8,10},{9,11},{1... | collective-permute-start | bytes 1081352 | tf_op jit(solution)/shard_map/ppermute | solution.py:352
  649.0 137.3 %collective-permute-start.63 = (bf16[384,2048]{1,0:T(8,128)(2,1)S(1)}, bf16[384,2048]{1,0:T(8,128)(2,1)S(1)}, u32[]{:S(2)}, u32[]{:S(2)}) collective-permute-start(bf16[384,2048]{1,0:T(8,128)(2,1)S(1)} %get-tuple-element.66), channel_id=1, source_target_pairs={{0,1},{1,0},{2,3},{3,2},{4,5},{5,4},{6,7},{7,6},{8,9},{9,8},{10,11... | collective-permute-start | bytes 4718600 | tf_op jit(solution)/shard_map/ppermute | solution.py:352
  651.4 52.0 %collective-permute-start.64 = (bf16[384,2048]{1,0:T(8,128)(2,1)S(1)}, bf16[384,2048]{1,0:T(8,128)(2,1)S(1)}, u32[]{:S(2)}, u32[]{:S(2)}) collective-permute-start(bf16[384,2048]{1,0:T(8,128)(2,1)S(1)} %get-tuple-element.67), channel_id=1, source_target_pairs={{0,1},{1,0},{2,3},{3,2},{4,5},{5,4},{6,7},{7,6},{8,9},{9,8},{10,11... | collective-permute-start | bytes 4718600 | tf_op jit(solution)/shard_map/ppermute | solution.py:352
  651.5 54.5 %collective-permute-start.58 = (bf16[384,2048]{1,0:T(8,128)(2,1)S(1)}, bf16[384,2048]{1,0:T(8,128)(2,1)S(1)}, u32[]{:S(2)}, u32[]{:S(2)}) collective-permute-start(bf16[384,2048]{1,0:T(8,128)(2,1)S(1)} %get-tuple-element.69), channel_id=1, source_target_pairs={{0,1},{1,0},{2,3},{3,2},{4,5},{5,4},{6,7},{7,6},{8,9},{9,8},{10,11... | collective-permute-start | bytes 4718600 | tf_op jit(solution)/shard_map/ppermute | solution.py:352
  727.1 64.3 %collective-permute-start.57 = (bf16[384,2048]{1,0:T(8,128)(2,1)S(1)}, bf16[384,2048]{1,0:T(8,128)(2,1)S(1)}, u32[]{:S(2)}, u32[]{:S(2)}) collective-permute-start(bf16[384,2048]{1,0:T(8,128)(2,1)S(1)} %get-tuple-element.68), channel_id=1, source_target_pairs={{0,1},{1,0},{2,3},{3,2},{4,5},{5,4},{6,7},{7,6},{8,9},{9,8},{10,11... | collective-permute-start | bytes 4718600 | tf_op jit(solution)/shard_map/ppermute | solution.py:352
  740.7 47.4 %collective-permute-start.65 = (bf16[384,2048]{1,0:T(8,128)(2,1)S(1)}, bf16[384,2048]{1,0:T(8,128)(2,1)S(1)}, u32[]{:S(2)}, u32[]{:S(2)}) collective-permute-start(bf16[384,2048]{1,0:T(8,128)(2,1)S(1)} %fusion.16), channel_id=1, source_target_pairs={{0,8},{1,9},{2,10},{3,11},{4,12},{5,13},{6,14},{7,15},{8,0},{9,1},... | collective-permute-start | bytes 4718600 | tf_op jit(solution)/shard_map/ppermute | solution.py:352
  770.8 36.4 %collective-permute-start.59 = (bf16[384,2048]{1,0:T(8,128)(2,1)}, bf16[384,2048]{1,0:T(8,128)(2,1)S(1)}, u32[]{:S(2)}, u32[]{:S(2)}) collective-permute-start(bf16[384,2048]{1,0:T(8,128)(2,1)} %fusion.20), channel_id=1, source_target_pairs={{0,8},{1,9},{2,10},{3,11},{4,12},{5,13},{6,14},{7,15},{8,0},{9,1},... | collective-permute-start | bytes 4718600 | tf_op jit(solution)/shard_map/ppermute | solution.py:352
  788.0 42.3 %collective-permute-start.100 = (bf16[2,128,1408]{2,1,0:T(8,128)(2,1)}, bf16[2,128,1408]{2,1,0:T(8,128)(2,1)}, u32[]{:S(2)}, u32[]{:S(2)}) collective-permute-start(bf16[2,128,1408]{2,1,0:T(8,128)(2,1)} %get-tuple-element.80), channel_id=1, source_target_pairs={{0,2},{1,3},{2,4},{3,5},{4,6},{5,7},{6,22},{7,23},{8,10},{9,11},{1... | collective-permute-start | bytes 2162696 | tf_op jit(solution)/shard_map/ppermute | solution.py:352
  817.9 41.5 %collective-permute-start.67 = (bf16[384,2048]{1,0:T(8,128)(2,1)S(1)}, bf16[384,2048]{1,0:T(8,128)(2,1)S(1)}, u32[]{:S(2)}, u32[]{:S(2)}) collective-permute-start(bf16[384,2048]{1,0:T(8,128)(2,1)S(1)} %get-tuple-element.41), channel_id=1, source_target_pairs={{0,8},{1,9},{2,10},{3,11},{4,12},{5,13},{6,14},{7,15},{8,0},{9,1},... | collective-permute-start | bytes 4718600 | tf_op jit(solution)/shard_map/ppermute | solution.py:352
  820.6 53.7 %collective-permute-start.66 = (bf16[384,2048]{1,0:T(8,128)(2,1)S(1)}, bf16[384,2048]{1,0:T(8,128)(2,1)S(1)}, u32[]{:S(2)}, u32[]{:S(2)}) collective-permute-start(bf16[384,2048]{1,0:T(8,128)(2,1)S(1)} %get-tuple-element.41), channel_id=1, source_target_pairs={{0,1},{1,0},{2,3},{3,2},{4,5},{5,4},{6,7},{7,6},{8,9},{9,8},{10,11... | collective-permute-start | bytes 4718600 | tf_op jit(solution)/shard_map/ppermute | solution.py:352
  910.5 59.9 %collective-permute-start.71 = (bf16[2,768,128]{2,1,0:T(8,128)(2,1)S(1)}, bf16[2,768,128]{2,1,0:T(8,128)(2,1)S(1)}, u32[]{:S(2)}, u32[]{:S(2)}) collective-permute-start(bf16[2,768,128]{2,1,0:T(8,128)(2,1)S(1)} %get-tuple-element.113), channel_id=1, source_target_pairs={{6,0},{7,1},{14,8},{15,9},{22,16},{23,17},{30,24},{31,25}} | collective-permute-start | bytes 1179656 | tf_op jit(solution)/shard_map/ppermute | solution.py:352
  911.8 73.0 %collective-permute-start.70 = (bf16[2,768,128]{2,1,0:T(8,128)(2,1)S(1)}, bf16[2,768,128]{2,1,0:T(8,128)(2,1)S(1)}, u32[]{:S(2)}, u32[]{:S(2)}) collective-permute-start(bf16[2,768,128]{2,1,0:T(8,128)(2,1)S(1)} %get-tuple-element.114), channel_id=1, source_target_pairs={{4,0},{5,1},{6,2},{7,3},{12,8},{13,9},{14,10},{15,11},{20,16},{21,... | collective-permute-start | bytes 1179656 | tf_op jit(solution)/shard_map/ppermute | solution.py:352
  1081.5 55.4 %collective-permute-start.72 = (bf16[384,2048]{1,0:T(8,128)(2,1)}, bf16[384,2048]{1,0:T(8,128)(2,1)}, u32[]{:S(2)}, u32[]{:S(2)}) collective-permute-start(bf16[384,2048]{1,0:T(8,128)(2,1)} %get-tuple-element.64), channel_id=1, source_target_pairs={{0,1},{1,0},{2,3},{3,2},{4,5},{5,4},{6,7},{7,6},{8,9},{9,8},{10,11... | collective-permute-start | bytes 4718600 | tf_op jit(solution)/shard_map/ppermute | solution.py:352
  1090.8 46.1 %collective-permute-start.74 = (bf16[384,2048]{1,0:T(8,128)(2,1)}, bf16[384,2048]{1,0:T(8,128)(2,1)}, u32[]{:S(2)}, u32[]{:S(2)}) collective-permute-start(bf16[384,2048]{1,0:T(8,128)(2,1)} %fusion.12), channel_id=1, source_target_pairs={{0,8},{1,9},{2,10},{3,11},{4,12},{5,13},{6,14},{7,15},{8,0},{9,1},... | collective-permute-start | bytes 4718600 | tf_op jit(solution)/shard_map/ppermute | solution.py:352
  (190 other events, 3892.4 us)
Sparse Core Ops, SparseCore 0:
  1142.6 133.4 reduce-scatter.3

commit v2 on v1

--- a/solution.py
+++ b/solution.py
@@ -72,7 +72,7 @@
 
     def visit(block, masked):
         start = pl.multiple_of(block * rows, rows)
-        keyval = keyval_ref[0, pl.ds(start, rows), :]
+        keyval = keyval_ref[pl.ds(start, rows), :]
         key = keyval[:, :HD]
         value_t = keyval[:, HD:].T
         if masked:
@@ -146,7 +146,7 @@
         )
     dq_acc[...] = jnp.zeros_like(dq_acc)
 
-    @pl.when(cell % 2 == 0)
+    @pl.when(cell == 0)
     def _():
         dkv_acc[...] = jnp.zeros_like(dkv_acc)
 
@@ -154,7 +154,7 @@
 
     def visit(block, masked):
         start = pl.multiple_of(block * rows, rows)
-        keyval = keyval_ref[0, pl.ds(start, rows), :]
+        keyval = keyval_ref[pl.ds(start, rows), :]
         key = keyval[:, :HD]
         value = keyval[:, HD:]
         key_t = key.T
@@ -199,15 +199,15 @@
     for head in range(heads):
         dquery_ref[head] = scaled[:, head * rows : (head + 1) * rows].astype(BF)
 
-    @pl.when(cell % 2 == 1)
+    @pl.when(cell == 1)
     def _():
-        dkeyval_ref[0] = dkv_acc[...].astype(BF)
+        dkeyval_ref[...] = dkv_acc[...].astype(BF)
 
 
 def attention_specs(rows, heads, keys):
     return dict(
         head=pl.BlockSpec((heads, HD, rows), lambda cell, meta: (0, 0, cell)),
-        keyval=pl.BlockSpec((1, keys, 2 * HD), lambda cell, meta: (cell // 2, 0, 0)),
+        keyval=pl.BlockSpec((keys, 2 * HD), lambda cell, meta: (0, 0)),
         first=pl.BlockSpec((1, 1, rows), lambda cell, meta: (cell, 0, 0)),
         stat=pl.BlockSpec((1, 1, heads * rows), lambda cell, meta: (cell, 0, 0)),
     )
@@ -215,15 +215,15 @@
 
 def attend_forward(meta, query, keyval, first):
     heads, _, tokens = query.shape
-    rows = tokens // GROUP
-    keys = keyval.shape[1]
+    rows = tokens // 2
+    keys = keyval.shape[0]
     specs = attention_specs(rows, heads, keys)
     wide = heads * rows
     return pl.pallas_call(
         functools.partial(forward_kernel, rows=rows, heads=heads, pair=2),
         grid_spec=pltpu.PrefetchScalarGridSpec(
             num_scalar_prefetch=1,
-            grid=(GROUP,),
+            grid=(2,),
             in_specs=[specs["head"], specs["keyval"], specs["first"]],
             out_specs=[specs["head"], specs["stat"]],
             scratch_shapes=[
@@ -235,7 +235,7 @@
         ),
         out_shape=(
             jax.ShapeDtypeStruct(query.shape, BF),
-            jax.ShapeDtypeStruct((GROUP, 1, wide), F32),
+            jax.ShapeDtypeStruct((2, 1, wide), F32),
         ),
         compiler_params=pltpu.CompilerParams(
             dimension_semantics=("arbitrary",), vmem_limit_bytes=48 * 1024 * 1024
@@ -249,15 +249,15 @@
 
 def attend_backward(meta, query, keyval, first, out, lse, grad):
     heads, _, tokens = query.shape
-    rows = tokens // GROUP
-    keys = keyval.shape[1]
+    rows = tokens // 2
+    keys = keyval.shape[0]
     specs = attention_specs(rows, heads, keys)
     wide = heads * rows
     return pl.pallas_call(
         functools.partial(backward_kernel, rows=rows, heads=heads, pair=2),
         grid_spec=pltpu.PrefetchScalarGridSpec(
             num_scalar_prefetch=1,
-            grid=(GROUP,),
+            grid=(2,),
             in_specs=[
                 specs["head"],
                 specs["keyval"],
@@ -358,10 +358,11 @@
         row, col = index // deep, index % deep
         return row, jnp.where(row % 2 == 0, col, deep - 1 - col)
 
+    def with_core(block):
+        return jnp.concatenate([block, send(block, core_perm)], axis=0)
+
     def gather_group(block):
-        near = send(block, core_perm)
-        far = send(block, x_perm)
-        return jnp.concatenate([block, near, far, send(far, core_perm)], axis=0)
+        return [with_core(block), with_core(send(block, x_perm))]
 
     def to_quarters(pieces):
         return jnp.concatenate(
@@ -385,64 +386,104 @@
         ordered = [swap_pair(x_at, [rows_of[0][c], rows_of[1][c]]) for c in range(2)]
         return [[ordered[0][x], ordered[1][x]] for x in range(2)]
 
-    def gather_ring(chunk):
-        columns = chunk.shape[2]
-        whole = jnp.zeros((wide, 2, deep, chunk.shape[1], columns), chunk.dtype)
-
-        def put(whole, piece, offset, x_from):
-            row, col = place_at(offset)
-            piece = piece[None, :, None]
-            return lax.dynamic_update_slice(whole, piece, (row, x_from, col, 0, 0))
-
-        whole = put(whole, chunk, 0, 0)
-        right = left = chunk
-        for step in range(1, half_ring):
-            right = send(right, right_perm)
-            left = send(left, left_perm)
-            whole = put(whole, right, -step, 0)
-            whole = put(whole, left, step, 0)
-        whole = put(whole, send(right[:1], right_perm), half_ring, 0)
-        whole = put(whole, send(left[1:], left_perm), half_ring, 1)
-        return whole.reshape(-1, columns)
-
-    def scatter_ring(partial):
-        columns = partial.shape[1]
-        parts = partial.reshape(wide, 2, deep, 2 * own_rows, columns)
-
-        def part(offset, x_from=0, x_count=2):
+    class Gather:
+        def __init__(self, chunk):
+            self.right = self.left = chunk
+            self.step, self.got = 0, [(0, 0, chunk)]
+
+        def advance(self, times):
+            for _ in range(min(times, half_ring - self.step)):
+                self.step += 1
+                if self.step < half_ring:
+                    self.right = send(self.right, right_perm)
+                    self.left = send(self.left, left_perm)
+                    self.got += [(-self.step, 0, self.right), (self.step, 0, self.left)]
+                else:
+                    self.got += [
+                        (half_ring, 0, send(self.right[:1], right_perm)),
+                        (half_ring, 1, send(self.left[1:], left_perm)),
+                    ]
+
+        def wait_for(self, value):
+            self.right, self.left = after((self.right, self.left), value)
+
+        def whole(self, cuts):
+            results = []
+            for low, high in zip(cuts[:-1], cuts[1:]):
+                result = jnp.zeros((wide, 2, deep, 2 * own_rows, high - low), BF)
+                for offset, x_from, piece in self.got:
+                    row, col = place_at(offset)
+                    result = lax.dynamic_update_slice(
+                        result, piece[None, :, None, :, low:high], (row, x_from, col, 0, 0)
+                    )
+                results.append(result.reshape(-1, high - low))
+            return results
+
+    class Scatter:
+        def __init__(self, partial):
+            self.parts = partial.reshape(wide, 2, deep, 2 * own_rows, partial.shape[1])
+            self.step, self.right, self.left = 0, None, None
+
+        def part(self, offset, x_from=0, x_count=2):
             row, col = place_at(offset)
             return lax.dynamic_slice(
-                parts, (row, x_from, col, 0, 0), (1, x_count, 1, 2 * own_rows, columns)
-            ).reshape(x_count, 2 * own_rows, columns)
-
-        right = send(part(half_ring, 0, 1), right_perm)
-        left = send(part(half_ring, 1, 1), left_perm)
-        for step in range(half_ring - 1, 0, -1):
-            to_right, to_left = part(step), part(-step)
-            if step == half_ring - 1:
-                to_right = jnp.concatenate(
-                    [(to_right[:1].astype(F32) + right.astype(F32)).astype(BF), to_right[1:]]
-                )
-                to_left = jnp.concatenate(
-                    [to_left[:1], (to_left[1:].astype(F32) + left.astype(F32)).astype(BF)]
-                )
-            else:
-                to_right = (to_right.astype(F32) + right.astype(F32)).astype(BF)
-                to_left = (to_left.astype(F32) + left.astype(F32)).astype(BF)
-            right = send(to_right, right_perm)
-            left = send(to_left, left_perm)
-        own = part(0).astype(F32)
-        if half_ring > 1:
-            return own + right.astype(F32) + left.astype(F32)
-        return own + jnp.concatenate([right, left]).astype(F32)
-
-    def gather_weights(pieces):
+                self.parts,
+                (row, x_from, col, 0, 0),
+                (1, x_count, 1, 2 * own_rows, self.parts.shape[4]),
+            ).reshape(x_count, 2 * own_rows, self.parts.shape[4])
+
+        def advance(self, times):
+            for _ in range(min(times, half_ring - self.step)):
+                self.step += 1
+                offset = half_ring - self.step + 1
+                if self.step == 1:
+                    to_right, to_left = self.part(offset, 0, 1), self.part(-offset, 1, 1)
+                else:
+                    to_right, to_left = self.joined(offset, -offset)
+                self.right = send(to_right, right_perm)
+                self.left = send(to_left, left_perm)
+
+        def joined(self, at_right, at_left):
+            to_right, to_left = self.part(at_right), self.part(at_left)
+            if self.step == 2:
+                to_right = jnp.concatenate([add_low(to_right[:1], self.right), to_right[1:]])
+                to_left = jnp.concatenate([to_left[:1], add_low(to_left[1:], self.left)])
+                return to_right, to_left
+            return add_low(to_right, self.right), add_low(to_left, self.left)
+
+        def wait_for(self, value):
+            self.right, self.left = after((self.right, self.left), value)
+
+        def result(self):
+            self.advance(half_ring)
+            own = self.part(0).astype(F32)
+            if half_ring > 1:
+                return own + self.right.astype(F32) + self.left.astype(F32)
+            return own + jnp.concatenate([self.right, self.left]).astype(F32)
+
+    class Rings:
+        def __init__(self, members):
+            self.members = members
+
+        def wait_for(self, value):
+            for member in self.members:
+                member.wait_for(value)
+
+        def advance(self, times):
+            for member in self.members:
+                member.advance(times)
+
+    def add_low(one, other):
+        return (one.astype(F32) + other.astype(F32)).astype(BF)
+
+    per_window = -(-half_ring // 4)
+
+    def group_chunk(pieces):
         got = absolute(exchange_group(to_quarters(pieces)))
-        chunk = jnp.stack([jnp.concatenate(got[x], axis=0) for x in range(2)])
-        return gather_ring(chunk)
-
-    def scatter_weights(partial):
-        chunk = scatter_ring(partial).astype(BF)
+        return jnp.stack([jnp.concatenate(got[x], axis=0) for x in range(2)])
+
+    def to_owners(scatter):
+        chunk = scatter.result().astype(BF)
         blocks = [[chunk[x, c * own_rows : (c + 1) * own_rows] for c in range(2)] for x in range(2)]
         relative = absolute(blocks)
         got = [
@@ -455,132 +496,213 @@
     def columns_of(quarters):
         return quarters.transpose(1, 0, 2).reshape(own_rows, -1)
 
-    def reduce_group(partial):
-        parts = partial.reshape(2, 2, rows, width)
-        far = parts[1, 0] + send(parts[1, 1].astype(BF), core_perm).astype(F32)
-        near = parts[0, 0] + send(parts[0, 1].astype(BF), core_perm).astype(F32)
-        return near + send(far.astype(BF), x_perm).astype(F32)
-
+    def reduce_core(partial):
+        return partial[:rows].astype(F32) + send(partial[rows:], core_perm).astype(F32)
+
+    def send_far(partial):
+        return send(reduce_core(partial).astype(BF), x_perm).astype(F32)
+
+    index = f_at * seq_count + s_at
+    count = fsdp_count * seq_count
+    doublings = [
+        (bit, [(i, i ^ (1 << bit)) for i in range(count)]) for bit in range(count.bit_length() - 1)
+    ]
+
+    def gather_small(value):
+        bits = len(doublings)
+        x_bit = seq_count.bit_length() - 1
+        order = [x_bit] + [bit for bit in range(bits) if bit != x_bit]
+        for bit in order:
+            _, perm = doublings[bit]
+            pair = swap_pair((index >> bit) & 1, [value, send(value, perm)])
+            value = jnp.stack(pair, axis=1)
+        axes = [1 + order[::-1].index(bit) for bit in range(bits - 1, -1, -1)]
+        value = value.transpose([0] + axes + [bits + 1])
+        return value.reshape(value.shape[0], -1)
+
+    def sum_small(value):
+        for bit, perm in doublings:
+            value = value + send(value, perm)
+        return value
+
+    def after(value, other):
+        return lax.optimization_barrier((value, other))[0]
+
+    q_cols = HEADS // GROUP * HD
+    qkv_cols = q_cols + 2 * HD
+    hidden_cols = w_gate.shape[1] // GROUP
+    gains = gather_small(jnp.stack([norm_attn, norm_mlp])).astype(F32)
+    gain_attn, gain_mlp = gains[0], gains[1]
+    start_rows = [starts[0], send(starts, x_perm)[0]]
+    chunk_attn = group_chunk([w_query, w_key, w_value, w_out.T])
     own_tokens = tokens[0]
-    group_tokens = gather_group(own_tokens)
-    weights_attn = gather_weights([w_query, w_key, w_value, w_out.T])
-    start_rows = [starts[0], send(starts, x_perm)[0]]
-    gains = lax.all_gather(jnp.stack([norm_attn, norm_mlp]), AXES, axis=1, tiled=True)
-    gain_attn, gain_mlp = gains[0].astype(F32), gains[1].astype(F32)
-    group_cotangent = gather_group(cotangent[0])
-    w_gate_q = gather_weights([w_gate])
-    w_up_q = gather_weights([w_up])
-    w_down_q = gather_weights([w_down.T])
+    ring_attn = Gather(chunk_attn)
+    ring_attn.advance(half_ring)
+    group_tokens = gather_group(after(own_tokens, chunk_attn))
+    w_down_in, w_gate_in, w_up_in = after((w_down.T, w_gate, w_up), group_tokens[1])
+    ring_down = Gather(group_chunk([w_down_in]))
+    ring_gate_up = Gather(group_chunk([w_gate_in, w_up_in]))
+    rings = Rings([ring_down, ring_gate_up])
+    w_qkv, w_out_t = ring_attn.whole([0, qkv_cols, chunk_attn.shape[2]])
+    rings.wait_for(w_qkv)
+    rings.advance(per_window)
+    group_cotangent = gather_group(after(cotangent[0], ring_gate_up.right))
 
     block_at = [rows * (2 * z_at + (c_at ^ dc)) for dc in range(2)]
     within = jnp.arange(rows, dtype=jnp.int32)
-    cells = [(dx, dc) for dx in range(2) for dc in range(2)]
-    places = [block_at[dc] + within for dx, dc in cells]
-    firsts = [doc_first(start_rows[dx], places[i]) for i, (dx, dc) in enumerate(cells)]
-    offsets = jnp.concatenate([p - f for p, f in zip(places, firsts)])
-    cos_table, sine_table = rotary_tables(offsets)
-    first_rows = jnp.stack(firsts)[:, None, :]
     base_block = 2 * (z_at - deep + 1)
-    meta = jnp.stack(
-        [
-            jnp.stack(
-                [
-                    firsts[i][0] // rows - base_block,
-                    block_at[dc] // rows - base_block,
-                    base_block * rows,
-                    firsts[i][rows - 1],
-                    block_at[dc],
-                ]
-            )
-            for i, (dx, dc) in enumerate(cells)
+    tables, first_rows, metas = [], [], []
+    for dx in range(2):
+        places = [block_at[dc] + within for dc in range(2)]
+        firsts = [doc_first(start_rows[dx], places[dc]) for dc in range(2)]
+        tables.append(rotary_tables(jnp.concatenate([p - f for p, f in zip(places, firsts)])))
+        first_rows.append(jnp.stack(firsts)[:, None, :])
+        cells = [
+            [
+                firsts[dc][0] // rows - base_block,
+                block_at[dc] // rows - base_block,
+                base_block * rows,
+                firsts[dc][rows - 1],
+                block_at[dc],
+            ]
+            for dc in range(2)
         ]
-    ).astype(jnp.int32)
-
-    per_device = HEADS // GROUP
-    q_cols = per_device * HD
-    qkv_cols = q_cols + 2 * HD
-    group_inputs = group_tokens.astype(F32)
-    scale_group = lax.rsqrt(jnp.mean(group_inputs * group_inputs, axis=1, keepdims=True) + EPSILON)
-    normed = (group_inputs * scale_group * gain_attn).astype(BF)
-    w_qkv, w_out_t = weights_attn[:, :qkv_cols], weights_attn[:, qkv_cols:]
-    pre = contract(w_qkv, normed, 0, 1)
-    query = (
-        rotate(pre[:q_cols].reshape(per_device, HD, -1), cos_table, sine_table) * HD ** (-0.5)
-    ).astype(BF)
-    key = rotate(pre[q_cols : q_cols + HD][None], cos_table, sine_table)[0].astype(BF)
-    keyval = jnp.concatenate([key, pre[q_cols + HD :].astype(BF)], axis=0).T
-    keyval = keyval.reshape(2, 2, rows, 2 * HD)
-    keyval = jnp.stack([jnp.stack(swap_pair(c_at, [keyval[dx, 0], keyval[dx, 1]])) for dx in range(2)])
-    keyval = keyval.reshape(2, 2 * rows, 2 * HD)
-    earlier = [send(keyval, perm_of(along(step))) for step in range(deep - 1, 0, -1)]
-    keyvals = jnp.concatenate(earlier + [keyval], axis=1)
-
-    attended, lse = attend_forward(meta, query, keyvals, first_rows)
-    attended_t = attended.reshape(q_cols, -1)
-    middle = own_tokens.astype(F32) + reduce_group(contract(attended_t, w_out_t, 0, 1))
+        metas.append(jnp.stack([jnp.stack(cell) for cell in cells]).astype(jnp.int32))
+
+    heads = HEADS // GROUP
+    normed, scales, queries, keyvals, attended, lses = ([None, None] for _ in range(6))
+    for dx in (1, 0):
+        group_inputs = group_tokens[dx].astype(F32)
+        scales[dx] = lax.rsqrt(jnp.mean(group_inputs * group_inputs, axis=1, keepdims=True) + EPSILON)
+        normed[dx] = (group_inputs * scales[dx] * gain_attn).astype(BF)
+        pre = contract(w_qkv, normed[dx], 0, 1)
+        turned = rotate(pre[:q_cols].reshape(heads, HD, -1), *tables[dx])
+        queries[dx] = (turned * HD ** (-0.5)).astype(BF)
+        key = rotate(pre[q_cols : q_cols + HD][None], *tables[dx])[0].astype(BF)
+        keyval = jnp.concatenate([key, pre[q_cols + HD :].astype(BF)], axis=0).T
+        keyval = jnp.concatenate(swap_pair(c_at, [keyval[:rows], keyval[rows:]]))
+        earlier = [send(keyval, perm_of(along(step))) for step in range(deep - 1, 0, -1)]
+        keyvals[dx] = jnp.concatenate(earlier + [keyval], axis=0)
+    attended[1], lses[1] = attend_forward(metas[1], queries[1], keyvals[1], first_rows[1])
+    rings.wait_for(attended[1])
+    rings.advance(per_window)
+    far = send_far(contract(attended[1].reshape(q_cols, -1), w_out_t, 0, 1).astype(BF))
+    query_near = after(queries[0], attended[1])
+    attended[0], lses[0] = attend_forward(metas[0], query_near, keyvals[0], first_rows[0])
+    rings.wait_for(attended[0])
+    rings.advance(per_window)
+    near = reduce_core(contract(attended[0].reshape(q_cols, -1), w_out_t, 0, 1).astype(BF))
+    middle = own_tokens.astype(F32) + near + far
+    rings.wait_for(middle)
+    rings.advance(half_ring)
+    attended_t = [a.reshape(q_cols, -1) for a in attended]
 
     scale_mlp = lax.rsqrt(jnp.mean(middle * middle, axis=1, keepdims=True) + EPSILON)
     normed_mlp = gather_group((middle * scale_mlp * gain_mlp).astype(BF))
-    gate = contract(normed_mlp, w_gate_q, 1, 0)
-    up = contract(normed_mlp, w_up_q, 1, 0)
-    d_hidden = contract(group_cotangent, w_down_q, 1, 0)
-    sigmoid = jax.nn.sigmoid(gate)
-    silu = gate * sigmoid
-    hidden = (silu * up).astype(BF)
-    d_gate = (d_hidden * up * sigmoid * (1.0 + gate * (1.0 - sigmoid))).astype(BF)
-    d_up = (d_hidden * silu).astype(BF)
-    d_normed_mlp = reduce_group(contract(d_gate, w_gate_q, 1, 1) + contract(d_up, w_up_q, 1, 1))
-    result = middle + reduce_group(contract(hidden, w_down_q, 1, 1))
-    grad_gate = scatter_weights(contract(normed_mlp, d_gate, 0, 0).astype(BF))
-    grad_up = scatter_weights(contract(normed_mlp, d_up, 0, 0).astype(BF))
-    grad_down = scatter_weights(contract(group_cotangent, hidden, 0, 0).astype(BF))
+    (w_down_t,) = ring_down.whole([0, hidden_cols])
+    (w_gate_up,) = ring_gate_up.whole([0, 2 * hidden_cols])
+    hidden, d_gate_up = [None, None], [None, None]
+    for dx in range(2):
+        d_hidden = contract(group_cotangent[dx], w_down_t, 1, 0)
+        gate_up = contract(normed_mlp[dx], w_gate_up, 1, 0)
+        gate, up = gate_up[:, :hidden_cols], gate_up[:, hidden_cols:]
+        sigmoid = jax.nn.sigmoid(gate)
+        silu = gate * sigmoid
+        hidden[dx] = (silu * up).astype(BF)
+        d_gate = (d_hidden * up * sigmoid * (1.0 + gate * (1.0 - sigmoid))).astype(BF)
+        d_up = (d_hidden * silu).astype(BF)
+        d_gate_up[dx] = jnp.concatenate([d_gate, d_up], axis=1)
+    both_hidden = jnp.concatenate(hidden)
+    both_cotangent = jnp.concatenate(group_cotangent)
+    ring_down = Scatter(contract(both_cotangent, both_hidden, 0, 0).astype(BF))
+    ring_down.advance(per_window)
+    far_part = contract(after(d_gate_up[1], ring_down.parts), w_gate_up, 1, 1).astype(BF)
+    far = send_far(far_part)
+    near = reduce_core(contract(after(d_gate_up[0], far_part), w_gate_up, 1, 1).astype(BF))
+    ring_down.wait_for(near)
+    ring_down.advance(per_window)
+    both_normed = jnp.concatenate(normed_mlp)
+    both_d_gate_up = jnp.concatenate([after(d_gate_up[0], near), d_gate_up[1]])
+    ring_gate_up = Scatter(contract(both_normed, both_d_gate_up, 0, 0).astype(BF))
+    rings = Rings([ring_down, ring_gate_up])
+    ring_gate_up.advance(per_window)
+    d_normed_mlp = near + far
 
     def norm_backward(values, scale_rows, gain, grads_in):
         weighted = grads_in * gain
-        gain_grad = jnp.sum(grads_in * values * scale_rows, axis=0)
         inner_mean = jnp.mean(weighted * values, axis=1, keepdims=True)
         cube = scale_rows * scale_rows * scale_rows
-        return scale_rows * weighted - values * cube * inner_mean, gain_grad
-
-    d_middle, gain_grad_mlp = norm_backward(middle, scale_mlp, gain_mlp, d_normed_mlp)
-    d_middle = d_middle + cotangent[0].astype(F32)
+        return scale_rows * weighted - values * cube * inner_mean
+
+    gain_grad_mlp = jnp.sum(d_normed_mlp * middle * scale_mlp, axis=0)
+    d_middle = norm_backward(middle, scale_mlp, gain_mlp, d_normed_mlp) + cotangent[0].astype(F32)
+    rings.wait_for(d_middle)
+    rings.advance(per_window)
 
     d_branch = gather_group(d_middle.astype(BF))
-    d_attended = contract(w_out_t, d_branch, 0, 1).astype(BF).reshape(query.shape)
-    grad_out_t = contract(d_branch, attended_t, 0, 1).astype(BF)
-    d_query, d_keyvals = attend_backward(meta, query, keyvals, first_rows, attended, lse, d_attended)
-    d_chunks = d_keyvals.reshape(2, deep, 2 * rows, 2 * HD)
-    d_keyval = d_chunks[:, deep - 1].astype(F32)
-    for step in range(1, deep):
-        d_keyval = d_keyval + send(d_chunks[:, deep - 1 - step], perm_of(along(-step))).astype(F32)
-    d_keyval = d_keyval.reshape(2, 2, rows, 2 * HD)
-    d_keyval = jnp.stack([jnp.stack(swap_pair(c_at, [d_keyval[dx, 0], d_keyval[dx, 1]])) for dx in range(2)])
-    d_keyval = d_keyval.reshape(GROUP * rows, 2 * HD).T
-    d_query_pre = unrotate(d_query.astype(F32), cos_table, sine_table).astype(BF)
-    d_key_pre = unrotate(d_keyval[None, :HD], cos_table, sine_table)[0].astype(BF)
-    d_pre = jnp.concatenate(
-        [d_query_pre.reshape(q_cols, -1), d_key_pre, d_keyval[HD:].astype(BF)], axis=0
-    )
-    d_normed = reduce_group(contract(d_pre, w_qkv, 0, 1))
-    grad_qkv = contract(normed, d_pre, 0, 1).astype(BF)
-    grad_attn = scatter_weights(jnp.concatenate([grad_qkv, grad_out_t], axis=1))
-    inputs = own_tokens.astype(F32)
-    scale_attn = scale_group[:rows]
-    d_inputs, gain_grad_attn = norm_backward(inputs, scale_attn, gain_attn, d_normed)
-    d_inputs = d_inputs + d_middle
-
-    gain_grads = lax.psum_scatter(
-        jnp.stack([gain_grad_attn, gain_grad_mlp]), AXES, scatter_dimension=1, tiled=True
-    )
+    d_keyval, d_query = [None, None], [None, None]
+    for dx in range(2):
+        d_attended = contract(w_out_t, d_branch[dx], 0, 1).astype(BF).reshape(queries[dx].shape)
+        if dx == 1:
+            d_attended = after(d_attended, d_query[0])
+        d_query[dx], d_keyvals = attend_backward(
+            metas[dx], queries[dx], keyvals[dx], first_rows[dx], attended[dx], lses[dx], d_attended
+        )
+        rings.wait_for(d_query[dx])
+        rings.advance(per_window)
+        chunks = [d_keyvals[2 * rows * i : 2 * rows * (i + 1)] for i in range(deep)]
+        total = chunks[deep - 1].astype(F32)
+        for step in range(1, deep):
+            total = total + send(chunks[deep - 1 - step], perm_of(along(-step))).astype(F32)
+        d_keyval[dx] = jnp.concatenate(swap_pair(c_at, [total[:rows], total[rows:]])).T
+    rings.advance(half_ring)
+    grad_out_part = contract(d_branch[0], attended_t[0], 0, 1) + contract(
+        after(d_branch[1], d_query[1]), attended_t[1], 0, 1
+    )
+    ring_out = Scatter(grad_out_part.astype(BF))
+    ring_out.advance(half_ring)
+
+    result_far = send_far(contract(after(hidden[1], d_query[1]), w_down_t, 1, 1).astype(BF))
+    result_near = reduce_core(contract(after(hidden[0], d_query[1]), w_down_t, 1, 1).astype(BF))
+    result = middle + result_near + result_far
+
+    d_pre = [None, None]
+    for dx in range(2):
+        d_query_pre = unrotate(d_query[dx].astype(F32), *tables[dx]).astype(BF)
+        d_key_pre = unrotate(d_keyval[dx][None, :HD], *tables[dx])[0].astype(BF)
+        d_value_pre = d_keyval[dx][HD:].astype(BF)
+        d_pre[dx] = jnp.concatenate([d_query_pre.reshape(q_cols, -1), d_key_pre, d_value_pre])
+    near_part = contract(d_pre[0], w_qkv, 0, 1).astype(BF)
+    far_part = contract(d_pre[1], w_qkv, 0, 1).astype(BF)
+    far = send_far(far_part)
+    near = reduce_core(near_part)
+    grad_qkv_part = contract(normed[0], d_pre[0], 0, 1) + contract(
+        normed[1], after(d_pre[1], far_part), 0, 1
+    )
+    ring_qkv = Scatter(grad_qkv_part.astype(BF))
+    ring_qkv.advance(half_ring)
+    gain_grad_attn = sum(
+        jnp.sum(part.astype(F32) * group_tokens[dx].astype(F32) * scales[dx], axis=0)
+        for dx, part in enumerate((near_part, far_part))
+    )
+    gain_grads = lax.dynamic_slice_in_dim(
+        sum_small(jnp.stack([gain_grad_attn, gain_grad_mlp])), index * own_rows, own_rows, 1
+    )
+    grad_down = to_owners(ring_down)
+    grad_gate_up = to_owners(ring_gate_up)
+    grad_out = to_owners(ring_out)
+    d_normed = near + far
+    d_inputs = norm_backward(own_tokens.astype(F32), scales[0][:rows], gain_attn, d_normed) + d_middle
+    grad_qkv = to_owners(ring_qkv)
     return (
         result.astype(BF)[None],
         d_inputs.astype(BF)[None],
-        columns_of(grad_attn[:, :, :q_cols]),
-        columns_of(grad_attn[:, :, q_cols : q_cols + HD]),
-        columns_of(grad_attn[:, :, q_cols + HD : qkv_cols]),
-        columns_of(grad_attn[:, :, qkv_cols:]).T,
-        columns_of(grad_gate),
-        columns_of(grad_up),
+        columns_of(grad_qkv[:, :, :q_cols]),
+        columns_of(grad_qkv[:, :, q_cols : q_cols + HD]),
+        columns_of(grad_qkv[:, :, q_cols + HD :]),
+        columns_of(grad_out).T,
+        columns_of(grad_gate_up[:, :, :hidden_cols]),
+        columns_of(grad_gate_up[:, :, hidden_cols:]),
         columns_of(grad_down).T,
         gain_grads[0],
         gain_grads[1],

time: 1300 us -> 983 us (0.76)
  waiting for transfers between devices: 609 us -> 362 us
  starting transfers between devices: 148 us -> 201 us
  blocking collectives: 42.1 us -> 0 us
  local copies, waits for them, and re-layouts: 128 us -> 100 us
  matrix products: 185 us -> 164 us
    unnamed x2 -> x0, waiting for transfers between devices: 127 us -> none
    ppermute x119 -> x124, waiting for transfers between devices: 482 us -> 362 us  [send(): return lax.ppermute(value, AXES, perm)]
    ppermute x119 -> x124, starting transfers between devices: 148 us -> 201 us  [send(): return lax.ppermute(value, AXES, perm)]
    all_gather x1 -> x0, blocking collectives: 42.1 us -> none  [shards(): lax.all_gather(jnp.stack([norm_attn, norm_mlp]), AXES, axis=1, tiled=True)]
    dot_general x15 -> x22, matrix products: 185 us -> 164 us  [contract(): lax.dot_general(left, right, (((left_dim,), (right_dim,)), ((), ())), pre...]
    concatenate x10 -> x14, other arithmetic: 4.8 us -> 18.7 us  [the longest x2 8.77 us: shards(): d_gate_up[dx] = jnp.concatenate([d_gate, d_up], axis=1)]
    unnamed x230 -> x235, local copies, waits for them, and re-layouts: 36.7 us -> 24.8 us
  transfers between devices with their start and end apart: 120 -> 124, of which waited for: 55 -> 47; matrix products, arithmetic and copies ran while one was open for 23% -> 29% of each run, Pallas kernels for 1% -> 4%
where the time goes in v2:
time: 983 us; the launch traced here: 976 us
  waiting for transfers between devices  362 us (37%)
  starting transfers between devices  201 us (20%)
  matrix products  164 us (17%)
  local copies, waits for them, and re-layouts  100 us (10%)
  other arithmetic  94.5 us (10%)
  Pallas kernels  42.4 us (4%)
  between operations  11.9 us (1%)
    ppermute x124, waiting for transfers between devices, send(): return lax.ppermute(value, AXES, perm)  362 us
    ppermute x124, starting transfers between devices, send(): return lax.ppermute(value, AXES, perm)  201 us
    dot_general x22, matrix products, contract(): lax.dot_general(left, right, (((left_dim,), (right_dim,)), ((), ())), pre...  164 us
    unnamed x235, local copies, waits for them, and re-layouts  24.8 us
    pallas_call x2, Pallas kernels, attend_backward(): pl.pallas_call(functools.partial(backward_kernel, rows=rows, heads=heads,...  23.1 us
    convert_element_type x12, other arithmetic, add_low(): return (one.astype(F32) + other.astype(F32)).astype(BF)  19.9 us
  transfers between devices with their start and end apart: 124, of which 47 were waited for; matrix products, arithmetic and copies ran while one was open for 29% of the time, Pallas kernels for 4%

profile of v2, /device:TPU:0, one launch (start us, length us, event | category | flops | bytes accessed | tf_op | source)
XLA Modules:
  0.0 976.0 jit_solution(16152459839852418500)
XLA Ops:
  48.8 8.9 collective-permute-done.3
  59.9 11.2 %collective-permute-done.5 = bf16[2,128,1152]{2,1,0:T(8,128)(2,1)S(1)} collective-permute-done((bf16[2,128,1152]{2,1,0:T(8,128)(2,1)S(1)}, bf16[2,128,1152]{2,1,0:T(8,128)(2,1)S(1)}, u32[]{:S(2)}, u32[]{:S(2)}) %collective-permute-start.5) | collective-permute-done | bytes 589856 | tf_op jit(solution)/shard_map/ppermute | solution.py:352
  73.3 10.3 %collective-permute-done.18 = bf16[384,2048]{1,0:T(8,128)(2,1)} collective-permute-done((bf16[384,2048]{1,0:T(8,128)(2,1)S(1)}, bf16[384,2048]{1,0:T(8,128)(2,1)}, u32[]{:S(2)}, u32[]{:S(2)}) %collective-permute-start.18) | collective-permute-done | bytes 1572896 | tf_op jit(solution)/shard_map/ppermute | solution.py:352
  165.9 9.5 attend_forward.2
  175.5 9.7 attend_forward.3
  195.5 26.0 %collective-permute-start.33 = (bf16[2,128,2816]{2,1,0:T(8,128)(2,1)}, bf16[2,128,2816]{2,1,0:T(8,128)(2,1)}, u32[]{:S(2)}, u32[]{:S(2)}) collective-permute-start(bf16[2,128,2816]{2,1,0:T(8,128)(2,1)} %pad_maximum_fusion.6), channel_id=1, source_target_pairs={{0,2},{1,3},{2,4},{3,5},{4,6},{5,7},{6,22},{7,23},{8,10},{9,11},{1... | collective-permute-start | bytes 4325384 | tf_op jit(solution)/shard_map/ppermute | solution.py:352
  228.2 25.3 %collective-permute-start.47 = (bf16[2,128,1408]{2,1,0:T(8,128)(2,1)}, bf16[2,128,1408]{2,1,0:T(8,128)(2,1)S(1)}, u32[]{:S(2)}, u32[]{:S(2)}) collective-permute-start(bf16[2,128,1408]{2,1,0:T(8,128)(2,1)} %collective-permute-done.45), channel_id=1, source_target_pairs={{0,2},{1,3},{2,4},{3,5},{4,6},{5,7},{6,22},{7,23},{8,10},{9,11},{1... | collective-permute-start | bytes 2162696 | tf_op jit(solution)/shard_map/ppermute | solution.py:352
  257.6 11.6 %collective-permute-done.47 = bf16[2,128,1408]{2,1,0:T(8,128)(2,1)S(1)} collective-permute-done((bf16[2,128,1408]{2,1,0:T(8,128)(2,1)}, bf16[2,128,1408]{2,1,0:T(8,128)(2,1)S(1)}, u32[]{:S(2)}, u32[]{:S(2)}) %collective-permute-start.47) | collective-permute-done | bytes 720928 | tf_op jit(solution)/shard_map/ppermute | solution.py:352
  272.4 21.3 %collective-permute-start.49 = (bf16[2,128,1408]{2,1,0:T(8,128)(2,1)S(1)}, bf16[2,128,1408]{2,1,0:T(8,128)(2,1)S(1)}, u32[]{:S(2)}, u32[]{:S(2)}) collective-permute-start(bf16[2,128,1408]{2,1,0:T(8,128)(2,1)S(1)} %collective-permute-done.47), channel_id=1, source_target_pairs={{0,2},{1,3},{2,4},{3,5},{4,6},{5,7},{6,22},{7,23},{8,10},{9,11},{1... | collective-permute-start | bytes 2162696 | tf_op jit(solution)/shard_map/ppermute | solution.py:352
  299.0 27.3 %collective-permute-done.34 = bf16[2,128,2816]{2,1,0:T(8,128)(2,1)S(1)} collective-permute-done((bf16[2,128,2816]{2,1,0:T(8,128)(2,1)}, bf16[2,128,2816]{2,1,0:T(8,128)(2,1)S(1)}, u32[]{:S(2)}, u32[]{:S(2)}) %collective-permute-start.34) | collective-permute-done | bytes 1441824 | tf_op jit(solution)/shard_map/ppermute | solution.py:352
  334.3 7.5 collective-permute-done.50
  343.4 13.8 %collective-permute-done.35 = bf16[2,128,2816]{2,1,0:T(8,128)(2,1)} collective-permute-done((bf16[2,128,2816]{2,1,0:T(8,128)(2,1)}, bf16[2,128,2816]{2,1,0:T(8,128)(2,1)}, u32[]{:S(2)}, u32[]{:S(2)}) %collective-permute-start.35) | collective-permute-done | bytes 1441824 | tf_op jit(solution)/shard_map/ppermute | solution.py:352
  357.2 14.1 %collective-permute-done.36 = bf16[2,128,2816]{2,1,0:T(8,128)(2,1)} collective-permute-done((bf16[2,128,2816]{2,1,0:T(8,128)(2,1)S(1)}, bf16[2,128,2816]{2,1,0:T(8,128)(2,1)}, u32[]{:S(2)}, u32[]{:S(2)}) %collective-permute-start.36) | collective-permute-done | bytes 1441824 | tf_op jit(solution)/shard_map/ppermute | solution.py:352
  384.6 26.7 %collective-permute-done.51 = bf16[1,128,1408]{2,1,0:T(8,128)(2,1)S(1)} collective-permute-done((bf16[1,128,1408]{2,1,0:T(8,128)(2,1)S(1)}, bf16[1,128,1408]{2,1,0:T(8,128)(2,1)S(1)}, u32[]{:S(2)}, u32[]{:S(2)}) %collective-permute-start.51) | collective-permute-done | bytes 360480 | tf_op jit(solution)/shard_map/ppermute | solution.py:352
  424.1 29.2 %collective-permute-done.55 = bf16[384,2048]{1,0:T(8,128)(2,1)} collective-permute-done((bf16[384,2048]{1,0:T(8,128)(2,1)S(1)}, bf16[384,2048]{1,0:T(8,128)(2,1)}, u32[]{:S(2)}, u32[]{:S(2)}) %collective-permute-start.55) | collective-permute-done | bytes 1572896 | tf_op jit(solution)/shard_map/ppermute | solution.py:352
  454.0 13.0 %fusion.40 = f32[768,2816]{1,0:T(8,128)} fusion(bf16[2048,2816]{1,0:T(8,128)(2,1)S(1)} %bitcast.665, bf16[384,2048]{1,0:T(8,128)(2,1)S(1)} %collective-permute-done.29, bf16[384,2048]{1,0:T(8,128)(2,1)S(1)} %multiply_convert_fusion.6), kind=kOutput, calls=%fused_computation.72 | convolution fusion | flops 8864661504 | bytes 23330816 | tf_op jit(solution)/shard_map/dot_general | solution.py:23
  468.2 11.3 %multiply_convert_fusion.4 = (bf16[768,1408]{1,0:T(8,128)(2,1)S(1)}, bf16[768,1408]{1,0:T(8,128)(2,1)}, bf16[768,1408]{1,0:T(8,128)(2,1)}) fusion(f32[768,2816]{1,0:T(8,128)} %fusion.40, bf16[2048,1408]{1,0:T(8,128)(2,1)S(1)} %bitcast.671, bf16[384,2048]{1,0:T(8,128)(2,1)} %copy-done.97, bf16[384,2048]{1,0:T(8,128)(2,1)} %bitcast.110), kind=kOutput, calls=%fused_computation.52 | convolution fusion | flops 4451696640 | bytes 24051712 | tf_op jit(solution)/shard_map/dot_general | solution.py:23
  483.6 13.3 %fusion.52 = f32[768,2816]{1,0:T(8,128)} fusion(bf16[2048,2816]{1,0:T(8,128)(2,1)S(1)} %bitcast.666, bf16[384,2048]{1,0:T(8,128)(2,1)} %collective-permute-done.56, bf16[384,2048]{1,0:T(8,128)(2,1)} %collective-permute-done.55), kind=kOutput, calls=%fused_computation.84 | convolution fusion | flops 8864661504 | bytes 23330816 | tf_op jit(solution)/shard_map/dot_general | solution.py:23
  496.9 11.6 %multiply_convert_fusion.2 = (bf16[768,1408]{1,0:T(8,128)(2,1)S(1)}, bf16[768,1408]{1,0:T(8,128)(2,1)}, bf16[768,1408]{1,0:T(8,128)(2,1)}) fusion(f32[768,2816]{1,0:T(8,128)} %fusion.52, bf16[2048,1408]{1,0:T(8,128)(2,1)S(1)} %bitcast.672, bf16[384,2048]{1,0:T(8,128)(2,1)} %collective-permute-done.54, bf16[384,2048]{1,0:T(8,128)(2,1)} %collective-permute-done.53), kind=kOutput, calls=%fused_computation.48 | convolution fusion | flops 4451696640 | bytes 24051712 | tf_op jit(solution)/shard_map/dot_general | solution.py:23
  513.2 15.1 %convolution_convert_fusion.1 = bf16[2048,1408]{1,0:T(8,128)(2,1)} fusion(bf16[384,2048]{1,0:T(8,128)(2,1)} %collective-permute-done.54, bf16[384,2048]{1,0:T(8,128)(2,1)} %collective-permute-done.53, bf16[384,2048]{1,0:T(8,128)(2,1)} %copy-done.97, bf16[384,2048]{1,0:T(8,128)(2,1)} %bitcast.110, bf16[768,1408]{1,0:T(8,128)(2,1)} %get-tuple-element.95, ...), kind=kOutput, calls=%fused_computation.12 | convolution fusion | flops 8895070208 | bytes 16384000 | tf_op jit(solution)/shard_map/dot_general | solution.py:23
  528.3 10.9 %convolution_convert_fusion.9 = bf16[768,2048]{1,0:T(8,128)(2,1)S(1)} fusion(bf16[768,2816]{1,0:T(8,128)(2,1)} %pad_maximum_fusion.1, bf16[2048,2816]{1,0:T(8,128)(2,1)S(1)} %bitcast.667), kind=kOutput, calls=%fused_computation.64 | convolution fusion | flops 8859942912 | bytes 19005440 | tf_op jit(solution)/shard_map/dot_general | solution.py:23
  541.5 10.9 %convolution_convert_fusion.8 = bf16[768,2048]{1,0:T(8,128)(2,1)S(1)} fusion(bf16[768,2816]{1,0:T(8,128)(2,1)} %pad_maximum_fusion, bf16[2048,2816]{1,0:T(8,128)(2,1)S(1)} %bitcast.668), kind=kOutput, calls=%fused_computation.63 | convolution fusion | flops 8859942912 | bytes 19005440 | tf_op jit(solution)/shard_map/dot_general | solution.py:23
  574.4 26.9 %convolution_convert_fusion = bf16[2048,2816]{1,0:T(8,128)(2,1)} fusion(bf16[768,1408]{1,0:T(8,128)(2,1)} %get-tuple-element.154, bf16[768,1408]{1,0:T(8,128)(2,1)} %copy-done.43, bf16[768,2816]{1,0:T(8,128)(2,1)} %pad_maximum_fusion, bf16[384,2048]{1,0:T(8,128)(2,1)} %collective-permute-done.56, bf16[384,2048]{1,0:T(8,128)(2,1)} %collective-permute-done.55, ...), kind=kOutput, calls=%fused_computation | convolution fusion | flops 17773625344 | bytes 26476544 | tf_op jit(solution)/shard_map/dot_general | solution.py:23
  630.6 11.6 %attend_backward.2 = (bf16[8,64,768]{2,1,0:T(8,128)(2,1)S(1)}, bf16[3072,128]{1,0:T(8,128)(2,1)S(1)}) custom-call(s32[2,5]{1,0:T(2,128)S(1)} %get-tuple-element.322.meta, bf16[8,64,768]{2,1,0:T(8,128)(2,1)S(1)} %fusion.66.query_ref, bf16[3072,128]{1,0:T(8,128)(2,1)S(1)} %copy-done.5, s32[2,1,384]{2,1,0:T(1,128)S(1)} %broadcast_in_dim.225.first_ref, ...), custom_call_target="tpu_custom_call" | custom-call | flops 80000000000 | bytes 16000000 | tf_op jit(solution)/shard_map/attend_backward/pallas_call | solution.py:256
  647.4 22.8 %collective-permute-done.100 = bf16[2,128,2816]{2,1,0:T(8,128)(2,1)} collective-permute-done((bf16[2,128,2816]{2,1,0:T(8,128)(2,1)}, bf16[2,128,2816]{2,1,0:T(8,128)(2,1)}, u32[]{:S(2)}, u32[]{:S(2)}) %collective-permute-start.100) | collective-permute-done | bytes 1441824 | tf_op jit(solution)/shard_map/ppermute | solution.py:352
  698.5 11.6 %attend_backward.3 = (bf16[8,64,768]{2,1,0:T(8,128)(2,1)S(1)}, bf16[3072,128]{1,0:T(8,128)(2,1)S(1)}) custom-call(s32[2,5]{1,0:T(2,128)S(1)} %get-tuple-element.323.meta, bf16[8,64,768]{2,1,0:T(8,128)(2,1)S(1)} %copy-done.1, bf16[3072,128]{1,0:T(8,128)(2,1)S(1)} %copy-done.3, s32[2,1,384]{2,1,0:T(1,128)S(1)} %broadcast_in_dim.223.first_ref, ...), custom_call_target="tpu_custom_call" | custom-call | flops 80000000000 | bytes 16000000 | tf_op jit(solution)/shard_map/attend_backward/pallas_call | solution.py:256
  716.5 7.1 collective-permute-done.101
  723.6 16.1 %collective-permute-done.102 = bf16[2,128,2816]{2,1,0:T(8,128)(2,1)} collective-permute-done((bf16[2,128,2816]{2,1,0:T(8,128)(2,1)}, bf16[2,128,2816]{2,1,0:T(8,128)(2,1)}, u32[]{:S(2)}, u32[]{:S(2)}) %collective-permute-start.102) | collective-permute-done | bytes 1441824 | tf_op jit(solution)/shard_map/ppermute | solution.py:352
  770.8 6.8 collective-permute-start.87
  867.5 15.5 %collective-permute-done.103 = bf16[2,128,2816]{2,1,0:T(8,128)(2,1)} collective-permute-done((bf16[2,128,2816]{2,1,0:T(8,128)(2,1)}, bf16[2,128,2816]{2,1,0:T(8,128)(2,1)}, u32[]{:S(2)}, u32[]{:S(2)}) %collective-permute-start.103) | collective-permute-done | bytes 1441824 | tf_op jit(solution)/shard_map/ppermute | solution.py:352
  909.6 28.8 %collective-permute-done.65 = bf16[384,2048]{1,0:T(8,128)(2,1)S(1)} collective-permute-done((bf16[384,2048]{1,0:T(8,128)(2,1)S(1)}, bf16[384,2048]{1,0:T(8,128)(2,1)S(1)}, u32[]{:S(2)}, u32[]{:S(2)}) %collective-permute-start.65) | collective-permute-done | bytes 1572896 | tf_op jit(solution)/shard_map/ppermute | solution.py:352
  942.2 30.0 %collective-permute-done.74 = bf16[384,2048]{1,0:T(8,128)(2,1)S(1)} collective-permute-done((bf16[384,2048]{1,0:T(8,128)(2,1)S(1)}, bf16[384,2048]{1,0:T(8,128)(2,1)S(1)}, u32[]{:S(2)}, u32[]{:S(2)}) %collective-permute-start.74) | collective-permute-done | bytes 1572896 | tf_op jit(solution)/shard_map/ppermute | solution.py:352
  (731 shorter events, 448.0 us)
Async XLA Ops:
  161.4 66.8 %collective-permute-start.45 = (bf16[2,128,1408]{2,1,0:T(8,128)(2,1)}, bf16[2,128,1408]{2,1,0:T(8,128)(2,1)}, u32[]{:S(2)}, u32[]{:S(2)}) collective-permute-start(bf16[2,128,1408]{2,1,0:T(8,128)(2,1)} %pad_maximum_fusion.16), channel_id=1, source_target_pairs={{0,2},{1,3},{2,4},{3,5},{4,6},{5,7},{6,22},{7,23},{8,10},{9,11},{1... | collective-permute-start | bytes 2162696 | tf_op jit(solution)/shard_map/ppermute | solution.py:352
  165.1 63.1 %collective-permute-start.46 = (bf16[2,128,1408]{2,1,0:T(8,128)(2,1)}, bf16[2,128,1408]{2,1,0:T(8,128)(2,1)}, u32[]{:S(2)}, u32[]{:S(2)}) collective-permute-start(bf16[2,128,1408]{2,1,0:T(8,128)(2,1)} %pad_maximum_fusion.16), channel_id=1, source_target_pairs={{0,16},{1,17},{2,0},{3,1},{4,2},{5,3},{6,4},{7,5},{8,24},{9,25},{1... | collective-permute-start | bytes 2162696 | tf_op jit(solution)/shard_map/ppermute | solution.py:352
  193.5 185.4 %collective-permute-start.26 = (bf16[384,2048]{1,0:T(8,128)(2,1)}, bf16[384,2048]{1,0:T(8,128)(2,1)}, u32[]{:S(2)}, u32[]{:S(2)}) collective-permute-start(bf16[384,2048]{1,0:T(8,128)(2,1)} %slice.636), channel_id=1, source_target_pairs={{0,1},{1,0},{2,3},{3,2},{4,5},{5,4},{6,7},{7,6},{8,9},{9,8},{10,11... | collective-permute-start | bytes 4718600 | tf_op jit(solution)/shard_map/ppermute | solution.py:352
  193.5 102.1 %collective-permute-start.27 = (bf16[384,2048]{1,0:T(8,128)(2,1)}, bf16[384,2048]{1,0:T(8,128)(2,1)}, u32[]{:S(2)}, u32[]{:S(2)}) collective-permute-start(bf16[384,2048]{1,0:T(8,128)(2,1)} %slice.638), channel_id=1, source_target_pairs={{0,1},{1,0},{2,3},{3,2},{4,5},{5,4},{6,7},{7,6},{8,9},{9,8},{10,11... | collective-permute-start | bytes 4718600 | tf_op jit(solution)/shard_map/ppermute | solution.py:352
  195.5 103.5 %collective-permute-start.33 = (bf16[2,128,2816]{2,1,0:T(8,128)(2,1)}, bf16[2,128,2816]{2,1,0:T(8,128)(2,1)}, u32[]{:S(2)}, u32[]{:S(2)}) collective-permute-start(bf16[2,128,2816]{2,1,0:T(8,128)(2,1)} %pad_maximum_fusion.6), channel_id=1, source_target_pairs={{0,2},{1,3},{2,4},{3,5},{4,6},{5,7},{6,22},{7,23},{8,10},{9,11},{1... | collective-permute-start | bytes 4325384 | tf_op jit(solution)/shard_map/ppermute | solution.py:352
  269.1 57.2 %collective-permute-start.34 = (bf16[2,128,2816]{2,1,0:T(8,128)(2,1)}, bf16[2,128,2816]{2,1,0:T(8,128)(2,1)S(1)}, u32[]{:S(2)}, u32[]{:S(2)}) collective-permute-start(bf16[2,128,2816]{2,1,0:T(8,128)(2,1)} %pad_maximum_fusion.6), channel_id=1, source_target_pairs={{0,16},{1,17},{2,0},{3,1},{4,2},{5,3},{6,4},{7,5},{8,24},{9,25},{1... | collective-permute-start | bytes 4325384 | tf_op jit(solution)/shard_map/ppermute | solution.py:352
  272.4 60.3 %collective-permute-start.49 = (bf16[2,128,1408]{2,1,0:T(8,128)(2,1)S(1)}, bf16[2,128,1408]{2,1,0:T(8,128)(2,1)S(1)}, u32[]{:S(2)}, u32[]{:S(2)}) collective-permute-start(bf16[2,128,1408]{2,1,0:T(8,128)(2,1)S(1)} %collective-permute-done.47), channel_id=1, source_target_pairs={{0,2},{1,3},{2,4},{3,5},{4,6},{5,7},{6,22},{7,23},{8,10},{9,11},{1... | collective-permute-start | bytes 2162696 | tf_op jit(solution)/shard_map/ppermute | solution.py:352
  295.5 46.3 %collective-permute-start.50 = (bf16[2,128,1408]{2,1,0:T(8,128)(2,1)S(1)}, bf16[2,128,1408]{2,1,0:T(8,128)(2,1)S(1)}, u32[]{:S(2)}, u32[]{:S(2)}) collective-permute-start(bf16[2,128,1408]{2,1,0:T(8,128)(2,1)S(1)} %collective-permute-done.48), channel_id=1, source_target_pairs={{0,16},{1,17},{2,0},{3,1},{4,2},{5,3},{6,4},{7,5},{8,24},{9,25},{1... | collective-permute-start | bytes 2162696 | tf_op jit(solution)/shard_map/ppermute | solution.py:352
  328.7 42.6 %collective-permute-start.36 = (bf16[2,128,2816]{2,1,0:T(8,128)(2,1)S(1)}, bf16[2,128,2816]{2,1,0:T(8,128)(2,1)}, u32[]{:S(2)}, u32[]{:S(2)}) collective-permute-start(bf16[2,128,2816]{2,1,0:T(8,128)(2,1)S(1)} %collective-permute-done.34), channel_id=1, source_target_pairs={{0,16},{1,17},{2,0},{3,1},{4,2},{5,3},{6,4},{7,5},{8,24},{9,25},{1... | collective-permute-start | bytes 4325384 | tf_op jit(solution)/shard_map/ppermute | solution.py:352
  332.7 46.2 %collective-permute-start.28 = (bf16[384,2048]{1,0:T(8,128)(2,1)S(1)}, bf16[384,2048]{1,0:T(8,128)(2,1)S(1)}, u32[]{:S(2)}, u32[]{:S(2)}) collective-permute-start(bf16[384,2048]{1,0:T(8,128)(2,1)S(1)} %add_convert_fusion.6), channel_id=1, source_target_pairs={{0,8},{1,9},{2,10},{3,11},{4,12},{5,13},{6,14},{7,15},{8,0},{9,1},... | collective-permute-start | bytes 4718600 | tf_op jit(solution)/shard_map/ppermute | solution.py:352
  341.8 82.2 %collective-permute-start.53 = (bf16[384,2048]{1,0:T(8,128)(2,1)}, bf16[384,2048]{1,0:T(8,128)(2,1)}, u32[]{:S(2)}, u32[]{:S(2)}) collective-permute-start(bf16[384,2048]{1,0:T(8,128)(2,1)} %bitcast.110), channel_id=1, source_target_pairs={{0,8},{1,9},{2,10},{3,11},{4,12},{5,13},{6,14},{7,15},{8,0},{9,1},... | collective-permute-start | bytes 4718600 | tf_op jit(solution)/shard_map/ppermute | solution.py:352
  371.3 50.2 %collective-permute-start.37 = (bf16[2,128,2816]{2,1,0:T(8,128)(2,1)}, bf16[2,128,2816]{2,1,0:T(8,128)(2,1)S(1)}, u32[]{:S(2)}, u32[]{:S(2)}) collective-permute-start(bf16[2,128,2816]{2,1,0:T(8,128)(2,1)} %collective-permute-done.35), channel_id=1, source_target_pairs={{0,2},{1,3},{2,4},{3,5},{4,6},{5,7},{6,22},{7,23},{8,10},{9,11},{1... | collective-permute-start | bytes 4325384 | tf_op jit(solution)/shard_map/ppermute | solution.py:352
  373.7 47.8 %collective-permute-start.38 = (bf16[2,128,2816]{2,1,0:T(8,128)(2,1)}, bf16[2,128,2816]{2,1,0:T(8,128)(2,1)S(1)}, u32[]{:S(2)}, u32[]{:S(2)}) collective-permute-start(bf16[2,128,2816]{2,1,0:T(8,128)(2,1)} %collective-permute-done.36), channel_id=1, source_target_pairs={{0,16},{1,17},{2,0},{3,1},{4,2},{5,3},{6,4},{7,5},{8,24},{9,25},{1... | collective-permute-start | bytes 4325384 | tf_op jit(solution)/shard_map/ppermute | solution.py:352
  384.5 69.5 %collective-permute-start.29 = (bf16[384,2048]{1,0:T(8,128)(2,1)S(1)}, bf16[384,2048]{1,0:T(8,128)(2,1)S(1)}, u32[]{:S(2)}, u32[]{:S(2)}) collective-permute-start(bf16[384,2048]{1,0:T(8,128)(2,1)S(1)} %multiply_convert_fusion.6), channel_id=1, source_target_pairs={{0,1},{1,0},{2,3},{3,2},{4,5},{5,4},{6,7},{7,6},{8,9},{9,8},{10,11... | collective-permute-start | bytes 4718600 | tf_op jit(solution)/shard_map/ppermute | solution.py:352
  424.0 43.0 %collective-permute-start.41 = (bf16[384,2048]{1,0:T(8,128)(2,1)}, bf16[384,2048]{1,0:T(8,128)(2,1)S(1)}, u32[]{:S(2)}, u32[]{:S(2)}) collective-permute-start(bf16[384,2048]{1,0:T(8,128)(2,1)} %bitcast.110), channel_id=1, source_target_pairs={{0,1},{1,0},{2,3},{3,2},{4,5},{5,4},{6,7},{7,6},{8,9},{9,8},{10,11... | collective-permute-start | bytes 4718600 | tf_op jit(solution)/shard_map/ppermute | solution.py:352
  453.4 43.5 %collective-permute-start.54 = (bf16[384,2048]{1,0:T(8,128)(2,1)}, bf16[384,2048]{1,0:T(8,128)(2,1)}, u32[]{:S(2)}, u32[]{:S(2)}) collective-permute-start(bf16[384,2048]{1,0:T(8,128)(2,1)} %collective-permute-done.53), channel_id=1, source_target_pairs={{0,1},{1,0},{2,3},{3,2},{4,5},{5,4},{6,7},{7,6},{8,9},{9,8},{10,11... | collective-permute-start | bytes 4718600 | tf_op jit(solution)/shard_map/ppermute | solution.py:352
  571.4 42.8 %collective-permute-start.111 = (bf16[2,128,1408]{2,1,0:T(8,128)(2,1)S(1)}, bf16[2,128,1408]{2,1,0:T(8,128)(2,1)}, u32[]{:S(2)}, u32[]{:S(2)}) collective-permute-start(bf16[2,128,1408]{2,1,0:T(8,128)(2,1)S(1)} %pad_maximum_fusion.18), channel_id=1, source_target_pairs={{0,16},{1,17},{2,0},{3,1},{4,2},{5,3},{6,4},{7,5},{8,24},{9,25},{1... | collective-permute-start | bytes 2162696 | tf_op jit(solution)/shard_map/ppermute | solution.py:352
  573.0 42.8 %collective-permute-start.110 = (bf16[2,128,1408]{2,1,0:T(8,128)(2,1)}, bf16[2,128,1408]{2,1,0:T(8,128)(2,1)}, u32[]{:S(2)}, u32[]{:S(2)}) collective-permute-start(bf16[2,128,1408]{2,1,0:T(8,128)(2,1)} %pad_maximum_fusion.17), channel_id=1, source_target_pairs={{0,2},{1,3},{2,4},{3,5},{4,6},{5,7},{6,22},{7,23},{8,10},{9,11},{1... | collective-permute-start | bytes 2162696 | tf_op jit(solution)/shard_map/ppermute | solution.py:352
  614.2 62.0 %collective-permute-start.60 = (bf16[384,2048]{1,0:T(8,128)(2,1)}, bf16[384,2048]{1,0:T(8,128)(2,1)}, u32[]{:S(2)}, u32[]{:S(2)}) collective-permute-start(bf16[384,2048]{1,0:T(8,128)(2,1)} %get-tuple-element.135), channel_id=1, source_target_pairs={{0,8},{1,9},{2,10},{3,11},{4,12},{5,13},{6,14},{7,15},{8,0},{9,1},... | collective-permute-start | bytes 4718600 | tf_op jit(solution)/shard_map/ppermute | solution.py:352
  623.5 46.7 %collective-permute-start.100 = (bf16[2,128,2816]{2,1,0:T(8,128)(2,1)}, bf16[2,128,2816]{2,1,0:T(8,128)(2,1)}, u32[]{:S(2)}, u32[]{:S(2)}) collective-permute-start(bf16[2,128,2816]{2,1,0:T(8,128)(2,1)} %pad_maximum_fusion.8), channel_id=1, source_target_pairs={{0,16},{1,17},{2,0},{3,1},{4,2},{5,3},{6,4},{7,5},{8,24},{9,25},{1... | collective-permute-start | bytes 4325384 | tf_op jit(solution)/shard_map/ppermute | solution.py:352
  626.3 45.2 %collective-permute-start.99 = (bf16[2,128,2816]{2,1,0:T(8,128)(2,1)}, bf16[2,128,2816]{2,1,0:T(8,128)(2,1)S(1)}, u32[]{:S(2)}, u32[]{:S(2)}) collective-permute-start(bf16[2,128,2816]{2,1,0:T(8,128)(2,1)} %pad_maximum_fusion.7), channel_id=1, source_target_pairs={{0,2},{1,3},{2,4},{3,5},{4,6},{5,7},{6,22},{7,23},{8,10},{9,11},{1... | collective-permute-start | bytes 4325384 | tf_op jit(solution)/shard_map/ppermute | solution.py:352
  642.3 43.5 %collective-permute-start.66 = (bf16[768,128]{1,0:T(8,128)(2,1)S(1)}, bf16[768,128]{1,0:T(8,128)(2,1)S(1)}, u32[]{:S(2)}, u32[]{:S(2)}) collective-permute-start(bf16[768,128]{1,0:T(8,128)(2,1)S(1)} %get-tuple-element.225), channel_id=1, source_target_pairs={{2,0},{3,1},{4,2},{5,3},{6,4},{7,5},{10,8},{11,9},{12,10},{13,11},... | collective-permute-start | bytes 589832 | tf_op jit(solution)/shard_map/ppermute | solution.py:352
  643.6 45.7 %collective-permute-start.67 = (bf16[768,128]{1,0:T(8,128)(2,1)S(1)}, bf16[768,128]{1,0:T(8,128)(2,1)S(1)}, u32[]{:S(2)}, u32[]{:S(2)}) collective-permute-start(bf16[768,128]{1,0:T(8,128)(2,1)S(1)} %get-tuple-element.227), channel_id=1, source_target_pairs={{4,0},{5,1},{6,2},{7,3},{12,8},{13,9},{14,10},{15,11},{20,16},{21,... | collective-permute-start | bytes 589832 | tf_op jit(solution)/shard_map/ppermute | solution.py:352
  691.8 47.9 %collective-permute-start.102 = (bf16[2,128,2816]{2,1,0:T(8,128)(2,1)}, bf16[2,128,2816]{2,1,0:T(8,128)(2,1)}, u32[]{:S(2)}, u32[]{:S(2)}) collective-permute-start(bf16[2,128,2816]{2,1,0:T(8,128)(2,1)} %get-tuple-element.157), channel_id=1, source_target_pairs={{0,16},{1,17},{2,0},{3,1},{4,2},{5,3},{6,4},{7,5},{8,24},{9,25},{1... | collective-permute-start | bytes 4325384 | tf_op jit(solution)/shard_map/ppermute | solution.py:352
  710.3 68.9 %collective-permute-start.70 = (bf16[768,128]{1,0:T(8,128)(2,1)S(1)}, bf16[768,128]{1,0:T(8,128)(2,1)S(1)}, u32[]{:S(2)}, u32[]{:S(2)}) collective-permute-start(bf16[768,128]{1,0:T(8,128)(2,1)S(1)} %get-tuple-element.228), channel_id=1, source_target_pairs={{2,0},{3,1},{4,2},{5,3},{6,4},{7,5},{10,8},{11,9},{12,10},{13,11},... | collective-permute-start | bytes 589832 | tf_op jit(solution)/shard_map/ppermute | solution.py:352
  711.8 67.3 %collective-permute-start.71 = (bf16[768,128]{1,0:T(8,128)(2,1)S(1)}, bf16[768,128]{1,0:T(8,128)(2,1)S(1)}, u32[]{:S(2)}, u32[]{:S(2)}) collective-permute-start(bf16[768,128]{1,0:T(8,128)(2,1)S(1)} %get-tuple-element.230), channel_id=1, source_target_pairs={{4,0},{5,1},{6,2},{7,3},{12,8},{13,9},{14,10},{15,11},{20,16},{21,... | collective-permute-start | bytes 589832 | tf_op jit(solution)/shard_map/ppermute | solution.py:352
  715.2 52.4 %collective-permute-start.116 = (bf16[64,1408]{1,0:T(8,128)(2,1)S(1)}, bf16[64,1408]{1,0:T(8,128)(2,1)S(1)}, u32[]{:S(2)}, u32[]{:S(2)}) collective-permute-start(bf16[64,1408]{1,0:T(8,128)(2,1)S(1)} %get-tuple-element.234), channel_id=1, source_target_pairs={{0,9},{1,8},{2,11},{3,10},{4,13},{5,12},{6,15},{7,14},{8,1},{9,0},... | collective-permute-start | bytes 540680 | tf_op jit(solution)/shard_map/ppermute | solution.py:352
  770.8 45.6 %collective-permute-start.91 = (bf16[2,128,512]{2,1,0:T(8,128)(2,1)}, bf16[2,128,512]{2,1,0:T(8,128)(2,1)}, u32[]{:S(2)}, u32[]{:S(2)}) collective-permute-start(bf16[2,128,512]{2,1,0:T(8,128)(2,1)} %pad_maximum_fusion.24), channel_id=1, source_target_pairs={{0,16},{1,17},{2,0},{3,1},{4,2},{5,3},{6,4},{7,5},{8,24},{9,25},{1... | collective-permute-start | bytes 786440 | tf_op jit(solution)/shard_map/ppermute | solution.py:352
  770.8 45.6 %collective-permute-start.87 = (bf16[2,128,512]{2,1,0:T(8,128)(2,1)}, bf16[2,128,512]{2,1,0:T(8,128)(2,1)}, u32[]{:S(2)}, u32[]{:S(2)}) collective-permute-start(bf16[2,128,512]{2,1,0:T(8,128)(2,1)} %pad_maximum_fusion.23), channel_id=1, source_target_pairs={{0,2},{1,3},{2,4},{3,5},{4,6},{5,7},{6,22},{7,23},{8,10},{9,11},{1... | collective-permute-start | bytes 786440 | tf_op jit(solution)/shard_map/ppermute | solution.py:352
  861.2 48.4 %collective-permute-start.63 = (bf16[384,2048]{1,0:T(8,128)(2,1)}, bf16[384,2048]{1,0:T(8,128)(2,1)}, u32[]{:S(2)}, u32[]{:S(2)}) collective-permute-start(bf16[384,2048]{1,0:T(8,128)(2,1)} %slice.649), channel_id=1, source_target_pairs={{0,1},{1,0},{2,3},{3,2},{4,5},{5,4},{6,7},{7,6},{8,9},{9,8},{10,11... | collective-permute-start | bytes 4718600 | tf_op jit(solution)/shard_map/ppermute | solution.py:352
  862.8 79.3 %collective-permute-start.69 = (bf16[384,2048]{1,0:T(8,128)(2,1)}, bf16[384,2048]{1,0:T(8,128)(2,1)S(1)}, u32[]{:S(2)}, u32[]{:S(2)}) collective-permute-start(bf16[384,2048]{1,0:T(8,128)(2,1)} %slice.661), channel_id=1, source_target_pairs={{0,1},{1,0},{2,3},{3,2},{4,5},{5,4},{6,7},{7,6},{8,9},{9,8},{10,11... | collective-permute-start | bytes 4718600 | tf_op jit(solution)/shard_map/ppermute | solution.py:352
  904.8 67.4 %collective-permute-start.74 = (bf16[384,2048]{1,0:T(8,128)(2,1)S(1)}, bf16[384,2048]{1,0:T(8,128)(2,1)S(1)}, u32[]{:S(2)}, u32[]{:S(2)}) collective-permute-start(bf16[384,2048]{1,0:T(8,128)(2,1)S(1)} %add_convert_fusion.2), channel_id=1, source_target_pairs={{0,8},{1,9},{2,10},{3,11},{4,12},{5,13},{6,14},{7,15},{8,0},{9,1},... | collective-permute-start | bytes 4718600 | tf_op jit(solution)/shard_map/ppermute | solution.py:352
  (198 other events, 2977.3 us)

commit v3 on v2

--- a/solution.py
+++ b/solution.py
@@ -289,6 +289,192 @@
     )(meta, query, keyval, first, out, lse, grad)
 
 
+def opening_kernel(
+    tokens,
+    quarters_attn,
+    quarters_down,
+    quarters_gate_up,
+    group,
+    whole_attn,
+    whole_down,
+    chunk_gate_up,
+    local_sem,
+    near_send,
+    near_recv,
+    swap_send,
+    swap_recv,
+    hop_send,
+    hop_recv,
+    *,
+    wide,
+    deep,
+    own_rows,
+):
+    ring, half_ring = wide * deep, wide * deep // 2
+    f_at, s_at = lax.axis_index("fsdp"), lax.axis_index("seq")
+    y_at, x_at, z_at, c_at = f_at // 2, lax.rem(f_at, 2), s_at // 2, lax.rem(s_at, 2)
+    here = y_at * deep + jnp.where(lax.rem(y_at, 2) == 0, z_at, deep - 1 - z_at)
+
+    def ring_place(offset):
+        index = lax.rem(here + offset + 2 * ring, ring)
+        row, col = index // deep, lax.rem(index, deep)
+        return row, jnp.where(lax.rem(row, 2) == 0, col, deep - 1 - col)
+
+    def ring_device(offset):
+        row, col = ring_place(offset)
+        return row * 2 + x_at, col * 2 + c_at
+
+    moves = ((0, 1), (1, 0), (1, 1))
+
+    def other(dx, dc):
+        return lax.rem(x_at + dx, 2), lax.rem(c_at + dc, 2)
+
+    def group_device(dx, dc):
+        x, c = other(dx, dc)
+        return y_at * 2 + x, z_at * 2 + c
+
+    def remote(source, target, send, recv, device):
+        return pltpu.make_async_remote_copy(
+            src_ref=source,
+            dst_ref=target,
+            send_sem=send,
+            recv_sem=recv,
+            device_id=device,
+            device_id_type=pl.DeviceIdType.MESH,
+        )
+
+    barrier = pltpu.get_barrier_semaphore()
+    partners = [group_device(*move) for move in moves] + [ring_device(1), ring_device(-1)]
+    for device in partners:
+        pl.semaphore_signal(barrier, inc=1, device_id=device, device_id_type=pl.DeviceIdType.MESH)
+    pl.semaphore_wait(barrier, len(partners))
+
+    my_rows = pl.ds(pl.multiple_of(c_at * own_rows, own_rows), own_rows)
+    targets = (
+        whole_attn.at[y_at, x_at, z_at, my_rows],
+        whole_down.at[y_at, x_at, z_at, my_rows],
+        chunk_gate_up.at[x_at, my_rows],
+    )
+    quarters = (quarters_attn, quarters_down, quarters_gate_up)
+    locals_ = [
+        pltpu.make_async_copy(quarters[i].at[x_at * 2 + c_at], targets[i], local_sem.at[i])
+        for i in range(3)
+    ] + [pltpu.make_async_copy(tokens, group.at[0], local_sem.at[3])]
+
+    def swaps(i):
+        copies = []
+        for j, (dx, dc) in enumerate(moves):
+            x, c = other(dx, dc)
+            copies.append(
+                remote(
+                    quarters[i].at[x * 2 + c],
+                    targets[i],
+                    swap_send.at[i, j],
+                    swap_recv.at[i, j],
+                    group_device(dx, dc),
+                )
+            )
+        return copies
+
+    swap = [swaps(i) for i in range(3)]
+    to_core = remote(tokens, group.at[1], near_send.at[0], near_recv.at[0], group_device(0, 1))
+    to_x = remote(tokens, group.at[2], near_send.at[1], near_recv.at[1], group_device(1, 0))
+    far_to_core = remote(
+        group.at[2], group.at[3], near_send.at[2], near_recv.at[2], group_device(0, 1)
+    )
+    wholes = (whole_attn, whole_down)
+
+    def hop(i, direction, step):
+        row, col = ring_place(-direction * (step - 1))
+        if step < half_ring:
+            part = wholes[i].at[row, :, col]
+        else:
+            part = wholes[i].at[row, 0 if direction == 1 else 1, col]
+        side = 0 if direction == 1 else 1
+        return remote(
+            part,
+            part,
+            hop_send.at[i, side, step - 1],
+            hop_recv.at[i, side, step - 1],
+            ring_device(direction),
+        )
+
+    hops = [
+        [[hop(i, direction, step) for direction in (1, -1)] for step in range(1, half_ring + 1)]
+        for i in range(2)
+    ]
+
+    for copy in locals_:
+        copy.start()
+    for copy in swap[0]:
+        copy.start()
+    for copy in swap[1]:
+        copy.start()
+    to_core.start()
+    to_x.start()
+    for copy in swap[2]:
+        copy.start()
+    for i in range(2):
+        locals_[i].wait()
+        for copy in swap[i]:
+            copy.wait_recv()
+    for i in range(2):
+        for step in range(half_ring):
+            if i == 0 or step > 0:
+                for copy in hops[i][step]:
+                    copy.start()
+            if i == 0 and step == half_ring - 1:
+                for copy in hops[1][0]:
+                    copy.start()
+            for copy in hops[i][step]:
+                copy.wait_recv()
+            if i == 0 and step == half_ring - 1:
+                to_x.wait_recv()
+                far_to_core.start()
+    for copy in locals_[2:]:
+        copy.wait()
+    for copy in swap[2] + [to_core, far_to_core]:
+        copy.wait_recv()
+    for copy in swap[0] + swap[1] + swap[2] + [to_core, to_x, far_to_core]:
+        copy.wait_send()
+    for i in range(2):
+        for pair in hops[i]:
+            for copy in pair:
+                copy.wait_send()
+
+
+def opening(tokens, quarters_attn, quarters_down, quarters_gate_up, wide, deep):
+    own_rows = quarters_attn.shape[1]
+    half_ring = wide * deep // 2
+
+    def whole(quarters):
+        return jax.ShapeDtypeStruct((wide, 2, deep, 2 * own_rows, quarters.shape[2]), BF)
+
+    anywhere = pl.BlockSpec(memory_space=pl.ANY)
+    return pl.pallas_call(
+        functools.partial(opening_kernel, wide=wide, deep=deep, own_rows=own_rows),
+        out_shape=(
+            jax.ShapeDtypeStruct((GROUP, *tokens.shape), BF),
+            whole(quarters_attn),
+            whole(quarters_down),
+            jax.ShapeDtypeStruct((2, 2 * own_rows, quarters_gate_up.shape[2]), BF),
+        ),
+        in_specs=[anywhere] * 4,
+        out_specs=(anywhere,) * 4,
+        scratch_shapes=[
+            pltpu.SemaphoreType.DMA((4,)),
+            pltpu.SemaphoreType.DMA((3,)),
+            pltpu.SemaphoreType.DMA((3,)),
+            pltpu.SemaphoreType.DMA((3, 3)),
+            pltpu.SemaphoreType.DMA((3, 3)),
+            pltpu.SemaphoreType.DMA((2, 2, half_ring)),
+            pltpu.SemaphoreType.DMA((2, 2, half_ring)),
+        ],
+        compiler_params=pltpu.CompilerParams(collective_id=0, has_side_effects=True),
+        name="opening",
+    )(tokens, quarters_attn, quarters_down, quarters_gate_up)
+
+
 def shards(
     tokens,
     starts,
@@ -369,18 +555,6 @@
             [p.reshape(own_rows, GROUP, -1).transpose(1, 0, 2) for p in pieces], axis=2
         )
 
-    def exchange_group(quarters):
-        def of(dx, dc):
-            return lax.dynamic_index_in_dim(
-                quarters, (x_at ^ dx) * 2 + (c_at ^ dc), 0, keepdims=False
-            )
-
-        got = [
-            [of(0, 0), send(of(0, 1), core_perm)],
-            [send(of(1, 0), x_perm), send(of(1, 1), cross_perm)],
-        ]
-        return got
-
     def absolute(got):
         rows_of = [swap_pair(c_at, pair) for pair in got]
         ordered = [swap_pair(x_at, [rows_of[0][c], rows_of[1][c]]) for c in range(2)]
@@ -461,26 +635,17 @@
                 return own + self.right.astype(F32) + self.left.astype(F32)
             return own + jnp.concatenate([self.right, self.left]).astype(F32)
 
-    class Rings:
-        def __init__(self, members):
-            self.members = members
-
-        def wait_for(self, value):
-            for member in self.members:
-                member.wait_for(value)
-
-        def advance(self, times):
-            for member in self.members:
-                member.advance(times)
+    def stage(moving, values):
+        ends = [(member.right, member.left) for member in moving]
+        ends, values = lax.optimization_barrier((ends, values))
+        for member, (right, left) in zip(moving, ends):
+            member.right, member.left = right, left
+        return values
 
     def add_low(one, other):
         return (one.astype(F32) + other.astype(F32)).astype(BF)
 
     per_window = -(-half_ring // 4)
-
-    def group_chunk(pieces):
-        got = absolute(exchange_group(to_quarters(pieces)))
-        return jnp.stack([jnp.concatenate(got[x], axis=0) for x in range(2)])
 
     def to_owners(scatter):
         chunk = scatter.result().astype(BF)
@@ -508,18 +673,6 @@
         (bit, [(i, i ^ (1 << bit)) for i in range(count)]) for bit in range(count.bit_length() - 1)
     ]
 
-    def gather_small(value):
-        bits = len(doublings)
-        x_bit = seq_count.bit_length() - 1
-        order = [x_bit] + [bit for bit in range(bits) if bit != x_bit]
-        for bit in order:
-            _, perm = doublings[bit]
-            pair = swap_pair((index >> bit) & 1, [value, send(value, perm)])
-            value = jnp.stack(pair, axis=1)
-        axes = [1 + order[::-1].index(bit) for bit in range(bits - 1, -1, -1)]
-        value = value.transpose([0] + axes + [bits + 1])
-        return value.reshape(value.shape[0], -1)
-
     def sum_small(value):
         for bit, perm in doublings:
             value = value + send(value, perm)
@@ -531,22 +684,33 @@
     q_cols = HEADS // GROUP * HD
     qkv_cols = q_cols + 2 * HD
     hidden_cols = w_gate.shape[1] // GROUP
-    gains = gather_small(jnp.stack([norm_attn, norm_mlp])).astype(F32)
+    start_rows = [starts[0], send(starts, x_perm)[0]]
+    gain_columns = jnp.pad(jnp.stack([norm_attn, norm_mlp], axis=1), ((0, 0), (0, 126)))
+    own_tokens = tokens[0]
+    group_blocks, whole_attn, whole_down, chunk_gate_up = opening(
+        own_tokens,
+        to_quarters([w_query, w_key, w_value, w_out.T, jnp.tile(gain_columns, (1, GROUP))]),
+        to_quarters([w_down.T]),
+        to_quarters([w_gate, w_up]),
+        wide,
+        deep,
+    )
+    group_tokens = [group_blocks[2 * dx : 2 * dx + 2].reshape(2 * rows, width) for dx in range(2)]
+    whole_attn = whole_attn.reshape(width, -1)
+    w_down_t = whole_down.reshape(width, -1)
+    w_qkv = whole_attn[:, :qkv_cols]
+    w_out_t = whole_attn[:, qkv_cols : qkv_cols + q_cols]
+    gains = whole_attn[:, qkv_cols + q_cols :].T.astype(F32)
     gain_attn, gain_mlp = gains[0], gains[1]
-    start_rows = [starts[0], send(starts, x_perm)[0]]
-    chunk_attn = group_chunk([w_query, w_key, w_value, w_out.T])
-    own_tokens = tokens[0]
-    ring_attn = Gather(chunk_attn)
-    ring_attn.advance(half_ring)
-    group_tokens = gather_group(after(own_tokens, chunk_attn))
-    w_down_in, w_gate_in, w_up_in = after((w_down.T, w_gate, w_up), group_tokens[1])
-    ring_down = Gather(group_chunk([w_down_in]))
-    ring_gate_up = Gather(group_chunk([w_gate_in, w_up_in]))
-    rings = Rings([ring_down, ring_gate_up])
-    w_qkv, w_out_t = ring_attn.whole([0, qkv_cols, chunk_attn.shape[2]])
-    rings.wait_for(w_qkv)
-    rings.advance(per_window)
-    group_cotangent = gather_group(after(cotangent[0], ring_gate_up.right))
+    ring_gate_up = Gather(chunk_gate_up)
+    rings = [ring_gate_up]
+
+    def advance(members, times=per_window):
+        for member in members:
+            member.advance(times)
+
+    advance(rings)
+    group_cotangent = gather_group(cotangent[0])
 
     block_at = [rows * (2 * z_at + (c_at ^ dc)) for dc in range(2)]
     within = jnp.arange(rows, dtype=jnp.int32)
@@ -583,23 +747,23 @@
         keyval = jnp.concatenate(swap_pair(c_at, [keyval[:rows], keyval[rows:]]))
         earlier = [send(keyval, perm_of(along(step))) for step in range(deep - 1, 0, -1)]
         keyvals[dx] = jnp.concatenate(earlier + [keyval], axis=0)
+    keyvals[1] = stage(rings, keyvals[1])
+    advance(rings)
     attended[1], lses[1] = attend_forward(metas[1], queries[1], keyvals[1], first_rows[1])
-    rings.wait_for(attended[1])
-    rings.advance(per_window)
-    far = send_far(contract(attended[1].reshape(q_cols, -1), w_out_t, 0, 1).astype(BF))
-    query_near = after(queries[0], attended[1])
+    attended[1] = stage(rings, attended[1])
+    advance(rings)
+    far_sum = reduce_core(contract(attended[1].reshape(q_cols, -1), w_out_t, 0, 1).astype(BF)).astype(BF)
+    far = send(far_sum, x_perm).astype(F32)
+    query_near = after(queries[0], far_sum)
     attended[0], lses[0] = attend_forward(metas[0], query_near, keyvals[0], first_rows[0])
-    rings.wait_for(attended[0])
-    rings.advance(per_window)
+    attended[0], far = stage(rings, (attended[0], far))
+    advance(rings, half_ring)
     near = reduce_core(contract(attended[0].reshape(q_cols, -1), w_out_t, 0, 1).astype(BF))
     middle = own_tokens.astype(F32) + near + far
-    rings.wait_for(middle)
-    rings.advance(half_ring)
     attended_t = [a.reshape(q_cols, -1) for a in attended]
 
     scale_mlp = lax.rsqrt(jnp.mean(middle * middle, axis=1, keepdims=True) + EPSILON)
     normed_mlp = gather_group((middle * scale_mlp * gain_mlp).astype(BF))
-    (w_down_t,) = ring_down.whole([0, hidden_cols])
     (w_gate_up,) = ring_gate_up.whole([0, 2 * hidden_cols])
     hidden, d_gate_up = [None, None], [None, None]
     for dx in range(2):
@@ -614,18 +778,18 @@
         d_gate_up[dx] = jnp.concatenate([d_gate, d_up], axis=1)
     both_hidden = jnp.concatenate(hidden)
     both_cotangent = jnp.concatenate(group_cotangent)
-    ring_down = Scatter(contract(both_cotangent, both_hidden, 0, 0).astype(BF))
+    both_normed = jnp.concatenate(normed_mlp)
+    both_d_gate_up = jnp.concatenate(d_gate_up)
+    ring_gate_up = Scatter(contract(both_normed, both_d_gate_up, 0, 0).astype(BF))
+    ring_gate_up.advance(per_window)
+    far_part = contract(after(d_gate_up[1], ring_gate_up.parts), w_gate_up, 1, 1).astype(BF)
+    far = send_far(far_part)
+    near_part = contract(after(d_gate_up[0], far_part), w_gate_up, 1, 1).astype(BF)
+    near_part = stage([ring_gate_up], near_part)
+    ring_gate_up.advance(per_window)
+    near = reduce_core(near_part)
+    ring_down = Scatter(contract(both_cotangent, after(both_hidden, near_part), 0, 0).astype(BF))
     ring_down.advance(per_window)
-    far_part = contract(after(d_gate_up[1], ring_down.parts), w_gate_up, 1, 1).astype(BF)
-    far = send_far(far_part)
-    near = reduce_core(contract(after(d_gate_up[0], far_part), w_gate_up, 1, 1).astype(BF))
-    ring_down.wait_for(near)
-    ring_down.advance(per_window)
-    both_normed = jnp.concatenate(normed_mlp)
-    both_d_gate_up = jnp.concatenate([after(d_gate_up[0], near), d_gate_up[1]])
-    ring_gate_up = Scatter(contract(both_normed, both_d_gate_up, 0, 0).astype(BF))
-    rings = Rings([ring_down, ring_gate_up])
-    ring_gate_up.advance(per_window)
     d_normed_mlp = near + far
 
     def norm_backward(values, scale_rows, gain, grads_in):
@@ -636,33 +800,48 @@
 
     gain_grad_mlp = jnp.sum(d_normed_mlp * middle * scale_mlp, axis=0)
     d_middle = norm_backward(middle, scale_mlp, gain_mlp, d_normed_mlp) + cotangent[0].astype(F32)
-    rings.wait_for(d_middle)
-    rings.advance(per_window)
+    rings = [ring_gate_up, ring_down]
+    d_middle = stage(rings, d_middle)
+    for member in rings:
+        member.advance(per_window)
 
     d_branch = gather_group(d_middle.astype(BF))
-    d_keyval, d_query = [None, None], [None, None]
+    d_keyval, d_query, d_attended = [None, None], [None, None], [None, None]
     for dx in range(2):
-        d_attended = contract(w_out_t, d_branch[dx], 0, 1).astype(BF).reshape(queries[dx].shape)
-        if dx == 1:
-            d_attended = after(d_attended, d_query[0])
-        d_query[dx], d_keyvals = attend_backward(
-            metas[dx], queries[dx], keyvals[dx], first_rows[dx], attended[dx], lses[dx], d_attended
-        )
-        rings.wait_for(d_query[dx])
-        rings.advance(per_window)
+        part = contract(w_out_t, d_branch[dx], 0, 1).astype(BF)
+        d_attended[dx] = part.reshape(queries[dx].shape)
+
+    def keyval_home(d_keyvals):
         chunks = [d_keyvals[2 * rows * i : 2 * rows * (i + 1)] for i in range(deep)]
         total = chunks[deep - 1].astype(F32)
         for step in range(1, deep):
             total = total + send(chunks[deep - 1 - step], perm_of(along(-step))).astype(F32)
-        d_keyval[dx] = jnp.concatenate(swap_pair(c_at, [total[:rows], total[rows:]])).T
-    rings.advance(half_ring)
+        return jnp.concatenate(swap_pair(c_at, [total[:rows], total[rows:]])).T
+
+    d_query[0], d_keyvals = attend_backward(
+        metas[0], queries[0], keyvals[0], first_rows[0], attended[0], lses[0], d_attended[0]
+    )
+    d_query[0], d_keyvals = stage(rings, (d_query[0], d_keyvals))
+    for member in rings:
+        member.advance(per_window)
+    d_keyval[0] = keyval_home(d_keyvals)
+    result_part = contract(after(hidden[1], d_query[0]), w_down_t, 1, 1).astype(BF)
+    result_far = send_far(result_part)
+    d_attended[1] = after(d_attended[1], (d_query[0], result_part))
+    d_query[1], d_keyvals = attend_backward(
+        metas[1], queries[1], keyvals[1], first_rows[1], attended[1], lses[1], d_attended[1]
+    )
+    d_query[1], d_keyvals, d_keyval[0], result_far = stage(
+        rings, (d_query[1], d_keyvals, d_keyval[0], result_far)
+    )
+    for member in rings:
+        member.advance(half_ring)
+    d_keyval[1] = keyval_home(d_keyvals)
     grad_out_part = contract(d_branch[0], attended_t[0], 0, 1) + contract(
         after(d_branch[1], d_query[1]), attended_t[1], 0, 1
     )
     ring_out = Scatter(grad_out_part.astype(BF))
     ring_out.advance(half_ring)
-
-    result_far = send_far(contract(after(hidden[1], d_query[1]), w_down_t, 1, 1).astype(BF))
     result_near = reduce_core(contract(after(hidden[0], d_query[1]), w_down_t, 1, 1).astype(BF))
     result = middle + result_near + result_far
 
@@ -675,11 +854,13 @@
     near_part = contract(d_pre[0], w_qkv, 0, 1).astype(BF)
     far_part = contract(d_pre[1], w_qkv, 0, 1).astype(BF)
     far = send_far(far_part)
-    near = reduce_core(near_part)
     grad_qkv_part = contract(normed[0], d_pre[0], 0, 1) + contract(
         normed[1], after(d_pre[1], far_part), 0, 1
     )
     ring_qkv = Scatter(grad_qkv_part.astype(BF))
+    ring_qkv.advance(half_ring - per_window)
+    near = reduce_core(near_part)
+    near, far = stage([ring_qkv], (near, far))
     ring_qkv.advance(half_ring)
     gain_grad_attn = sum(
         jnp.sum(part.astype(F32) * group_tokens[dx].astype(F32) * scales[dx], axis=0)

time: 983 us -> 890 us (0.905)
  Pallas kernels: 42.4 us -> 179 us
  waiting for transfers between devices: 362 us -> 242 us
  starting transfers between devices: 201 us -> 104 us
  local copies, waits for them, and re-layouts: 100 us -> 61.6 us
  matrix products: 164 us -> 185 us
    pallas_call x0 -> x1, Pallas kernels: none -> 137 us  [opening(): pl.pallas_call(functools.partial(opening_kernel, wide=wide, deep=deep, ow...]
    ppermute x124 -> x91, waiting for transfers between devices: 362 us -> 242 us  [send(): return lax.ppermute(value, AXES, perm)]
    ppermute x124 -> x91, starting transfers between devices: 201 us -> 104 us  [send(): return lax.ppermute(value, AXES, perm)]
    dot_general x22, matrix products: 164 us -> 185 us  [contract(): lax.dot_general(left, right, (((left_dim,), (right_dim,)), ((), ())), pre...]
    dynamic_update_slice x32 -> x9, local copies, waits for them, and re-layouts: 19.4 us -> 7.36 us  [whole(): lax.dynamic_update_slice(result, piece[None, :, None, :, low:high], (row,...]
    unnamed x235 -> x257, local copies, waits for them, and re-layouts: 24.8 us -> 15.8 us
  transfers between devices with their start and end apart: 124 -> 91, of which waited for: 47 -> 35; matrix products, arithmetic and copies ran while one was open for 29% -> 30% of each run, Pallas kernels for 4% -> 5%
where the time goes in v3:
time: 890 us; the launch traced here: 879 us
  waiting for transfers between devices  242 us (27%)
  matrix products  185 us (21%)
  Pallas kernels  179 us (20%)
  starting transfers between devices  104 us (12%)
  other arithmetic  95.5 us (11%)
  local copies, waits for them, and re-layouts  61.6 us (7%)
  between operations  11.7 us (1%)
    ppermute x91, waiting for transfers between devices, send(): return lax.ppermute(value, AXES, perm)  242 us
    dot_general x22, matrix products, contract(): lax.dot_general(left, right, (((left_dim,), (right_dim,)), ((), ())), pre...  185 us
    pallas_call x1, Pallas kernels, opening(): pl.pallas_call(functools.partial(opening_kernel, wide=wide, deep=deep, ow...  137 us
    ppermute x91, starting transfers between devices, send(): return lax.ppermute(value, AXES, perm)  104 us
    pallas_call x2, Pallas kernels, attend_backward(): pl.pallas_call(functools.partial(backward_kernel, rows=rows, heads=heads,...  23.6 us
    pallas_call x2, Pallas kernels, attend_forward(): pl.pallas_call(functools.partial(forward_kernel, rows=rows, heads=heads,...  19 us
    convert_element_type x12, other arithmetic, add_low(): return (one.astype(F32) + other.astype(F32)).astype(BF)  17.8 us
  transfers between devices with their start and end apart: 91, of which 35 were waited for; matrix products, arithmetic and copies ran while one was open for 30% of the time, Pallas kernels for 5%

profile of v3, /device:TPU:0, one launch (start us, length us, event | category | flops | bytes accessed | tf_op | source)
XLA Modules:
  0.0 879.0 jit_solution(1825180049167192361)
XLA Ops:
  8.8 136.7 %opening.1 = (bf16[4,384,2048]{2,1,0:T(8,128)(2,1)}, bf16[2,2,4,128,1280]{4,3,2,1,0:T(8,128)(2,1)}, bf16[2,2,4,128,1408]{4,3,2,1,0:T(8,128)(2,1)}, bf16[2,128,2816]{2,1,0:T(8,128)(2,1)}) custom-call(bf16[384,2048]{1,0:T(8,128)(2,1)} %bitcast.498, bf16[4,64,1280]{2,1,0:T(8,128)(2,1)} %concatenate.144.quarters_attn, bf16[4,64,1408]{2,1,0:T(8,128)(2,1)} %bitcast.523, ...), custom_call_target="tpu_custom_call" | custom-call | tf_op jit(solution)/shard_map/opening/pallas_call | solution.py:454
  159.4 5.1 fusion.67
  164.9 5.3 fusion.65
  174.1 5.4 broadcast_in_dim.63
  224.0 5.2 collective-permute-start.12
  229.3 7.6 collective-permute-start.13
  244.6 9.5 %attend_forward.2 = (bf16[8,64,768]{2,1,0:T(8,128)(2,1)S(1)}, f32[2,1,3072]{2,1,0:T(1,128)S(1)}) custom-call(s32[2,5]{1,0:T(2,128)S(1)} %get-tuple-element.287.meta, bf16[8,64,768]{2,1,0:T(8,128)(2,1)S(1)} %fusion.71.query_ref, bf16[3072,128]{1,0:T(8,128)(2,1)S(1)} %constant_dynamic-update-slice_fusion.keyval_ref, s32[2,1,384]{2,1,0:T(1,128)S(1)} %broadcast_in_dim.60.first_ref), custom_call_target="tpu_custom_call" | custom-call | flops 40000000000 | bytes 10000000 | tf_op jit(solution)/shard_map/attend_forward/pallas_call | solution.py:222
  254.2 17.4 %collective-permute-done.6 = bf16[2,128,2816]{2,1,0:T(8,128)(2,1)S(1)} collective-permute-done((bf16[2,128,2816]{2,1,0:T(8,128)(2,1)}, bf16[2,128,2816]{2,1,0:T(8,128)(2,1)S(1)}, u32[]{:S(2)}, u32[]{:S(2)}) %collective-permute-start.6) | collective-permute-done | bytes 1441824 | tf_op jit(solution)/shard_map/ppermute | solution.py:538
  287.1 9.5 %attend_forward.3 = (bf16[8,64,768]{2,1,0:T(8,128)(2,1)S(1)}, f32[2,1,3072]{2,1,0:T(1,128)S(1)}) custom-call(s32[2,5]{1,0:T(2,128)S(1)} %get-tuple-element.288.meta, bf16[8,64,768]{2,1,0:T(8,128)(2,1)S(1)} %fusion.72.query_ref, bf16[3072,128]{1,0:T(8,128)(2,1)S(1)} %constant_dynamic-update-slice_fusion.5.keyval_ref, s32[2,1,384]{2,1,0:T(1,128)S(1)} %broadcast_in_dim.62.first_ref), custom_call_target="tpu_custom_call" | custom-call | flops 40000000000 | bytes 10000000 | tf_op jit(solution)/shard_map/attend_forward/pallas_call | solution.py:222
  296.6 25.8 %collective-permute-done.14 = bf16[384,2048]{1,0:T(8,128)(2,1)S(1)} collective-permute-done((bf16[384,2048]{1,0:T(8,128)(2,1)S(1)}, bf16[384,2048]{1,0:T(8,128)(2,1)S(1)}, u32[]{:S(2)}, u32[]{:S(2)}) %collective-permute-start.14) | collective-permute-done | bytes 1572896 | tf_op jit(solution)/shard_map/ppermute | solution.py:538
  337.4 10.0 %collective-permute-done.17 = bf16[1,128,2816]{2,1,0:T(8,128)(2,1)S(1)} collective-permute-done((bf16[1,128,2816]{2,1,0:T(8,128)(2,1)S(1)}, bf16[1,128,2816]{2,1,0:T(8,128)(2,1)S(1)}, u32[]{:S(2)}, u32[]{:S(2)}) %collective-permute-start.17) | collective-permute-done | bytes 720928 | tf_op jit(solution)/shard_map/ppermute | solution.py:538
  349.8 20.6 %collective-permute-done.19 = bf16[384,2048]{1,0:T(8,128)(2,1)} collective-permute-done((bf16[384,2048]{1,0:T(8,128)(2,1)S(1)}, bf16[384,2048]{1,0:T(8,128)(2,1)}, u32[]{:S(2)}, u32[]{:S(2)}) %collective-permute-start.19) | collective-permute-done | bytes 1572896 | tf_op jit(solution)/shard_map/ppermute | solution.py:538
  370.5 12.6 %fusion.39 = f32[768,2816]{1,0:T(8,128)} fusion(bf16[2048,2816]{1,0:T(8,128)(2,1)S(1)} %bitcast.504, bf16[384,2048]{1,0:T(8,128)(2,1)S(1)} %collective-permute-done.16, bf16[384,2048]{1,0:T(8,128)(2,1)S(1)} %multiply_convert_fusion.6), kind=kOutput, calls=%fused_computation.71 | convolution fusion | flops 8864661504 | bytes 23330816 | tf_op jit(solution)/shard_map/dot_general | solution.py:23
  383.1 12.6 %multiply_convert_fusion.4 = (bf16[768,1408]{1,0:T(8,128)(2,1)S(1)}, bf16[768,1408]{1,0:T(8,128)(2,1)S(1)}, bf16[768,1408]{1,0:T(8,128)(2,1)}) fusion(f32[768,2816]{1,0:T(8,128)} %fusion.39, bf16[2048,1408]{1,0:T(8,128)(2,1)} %bitcast.573, bf16[384,2048]{1,0:T(8,128)(2,1)S(1)} %collective-permute-done.21, bf16[384,2048]{1,0:T(8,128)(2,1)} %bitcast.68), kind=kOutput, calls=%fused_computation.52 | convolution fusion | flops 4451696640 | bytes 24051712 | tf_op jit(solution)/shard_map/dot_general | solution.py:23
  398.5 14.0 %fusion.51 = f32[768,2816]{1,0:T(8,128)} fusion(bf16[2048,2816]{1,0:T(8,128)(2,1)S(1)} %bitcast.506, bf16[384,2048]{1,0:T(8,128)(2,1)S(1)} %collective-permute-done.20, bf16[384,2048]{1,0:T(8,128)(2,1)} %collective-permute-done.19), kind=kOutput, calls=%fused_computation.83 | convolution fusion | flops 8864661504 | bytes 23330816 | tf_op jit(solution)/shard_map/dot_general | solution.py:23
  412.5 12.6 %multiply_convert_fusion.2 = (bf16[768,1408]{1,0:T(8,128)(2,1)S(1)}, bf16[768,1408]{1,0:T(8,128)(2,1)S(1)}, bf16[768,1408]{1,0:T(8,128)(2,1)}) fusion(f32[768,2816]{1,0:T(8,128)} %fusion.51, bf16[2048,1408]{1,0:T(8,128)(2,1)} %bitcast.574, bf16[384,2048]{1,0:T(8,128)(2,1)S(1)} %collective-permute-done.23, bf16[384,2048]{1,0:T(8,128)(2,1)} %collective-permute-done.22), kind=kOutput, calls=%fused_computation.48 | convolution fusion | flops 4451696640 | bytes 24051712 | tf_op jit(solution)/shard_map/dot_general | solution.py:23
  429.5 29.0 %convolution_convert_fusion = bf16[2048,2816]{1,0:T(8,128)(2,1)} fusion(bf16[768,1408]{1,0:T(8,128)(2,1)} %copy-done.47, bf16[768,1408]{1,0:T(8,128)(2,1)} %copy-done.46, bf16[768,1408]{1,0:T(8,128)(2,1)} %copy-done.45, bf16[768,1408]{1,0:T(8,128)(2,1)S(1)} %get-tuple-element.151, bf16[384,2048]{1,0:T(8,128)(2,1)} %copy-done.112, ...), kind=kOutput, calls=%fused_computation | convolution fusion | flops 17782276096 | bytes 26476544 | tf_op jit(solution)/shard_map/dot_general | solution.py:23
  464.5 13.6 %convolution_convert_fusion.9 = bf16[768,2048]{1,0:T(8,128)(2,1)S(1)} fusion(bf16[768,2816]{1,0:T(8,128)(2,1)} %pad_maximum_fusion.1, bf16[2048,2816]{1,0:T(8,128)(2,1)} %bitcast.505), kind=kOutput, calls=%fused_computation.64 | convolution fusion | flops 8859942912 | bytes 19005440 | tf_op jit(solution)/shard_map/dot_general | solution.py:23
  478.1 9.3 %convolution_convert_fusion.8 = bf16[768,2048]{1,0:T(8,128)(2,1)S(1)} fusion(bf16[768,2816]{1,0:T(8,128)(2,1)S(1)} %bitcast.518, bf16[2048,2816]{1,0:T(8,128)(2,1)S(1)} %bitcast.509), kind=kOutput, calls=%fused_computation.63 | convolution fusion | flops 8859942912 | bytes 19005440 | tf_op jit(solution)/shard_map/dot_general | solution.py:23
  504.6 13.8 %convolution_convert_fusion.1 = bf16[2048,1408]{1,0:T(8,128)(2,1)S(1)} fusion(bf16[1536,1408]{1,0:T(8,128)(2,1)} %pad_maximum_fusion.2, bf16[384,2048]{1,0:T(8,128)(2,1)} %copy-done.108, bf16[384,2048]{1,0:T(8,128)(2,1)} %collective-permute-done.22, bf16[384,2048]{1,0:T(8,128)(2,1)} %copy-done.107, bf16[384,2048]{1,0:T(8,128)(2,1)} %bitcast.68), kind=kOutput, calls=%fused_computation.8 | convolution fusion | flops 8886419456 | bytes 16384000 | tf_op jit(solution)/shard_map/dot_general | solution.py:23
  520.8 19.0 %collective-permute-done.32 = bf16[384,2048]{1,0:T(8,128)(2,1)S(1)} collective-permute-done((bf16[384,2048]{1,0:T(8,128)(2,1)}, bf16[384,2048]{1,0:T(8,128)(2,1)S(1)}, u32[]{:S(2)}, u32[]{:S(2)}) %collective-permute-start.32) | collective-permute-done | bytes 1572896 | tf_op jit(solution)/shard_map/ppermute | solution.py:538
  561.8 12.0 %attend_backward.2 = (bf16[8,64,768]{2,1,0:T(8,128)(2,1)S(1)}, bf16[3072,128]{1,0:T(8,128)(2,1)S(1)}) custom-call(s32[2,5]{1,0:T(2,128)S(1)} %copy-done.13, bf16[8,64,768]{2,1,0:T(8,128)(2,1)S(1)} %copy-done.3, bf16[3072,128]{1,0:T(8,128)(2,1)S(1)} %copy-done.5, s32[2,1,384]{2,1,0:T(1,128)S(1)} %broadcast_in_dim.62.first_ref, ...), custom_call_target="tpu_custom_call" | custom-call | flops 80000000000 | bytes 16000000 | tf_op jit(solution)/shard_map/attend_backward/pallas_call | solution.py:256
  573.8 26.8 %collective-permute-done.35 = bf16[2,128,1408]{2,1,0:T(8,128)(2,1)} collective-permute-done((bf16[2,128,1408]{2,1,0:T(8,128)(2,1)}, bf16[2,128,1408]{2,1,0:T(8,128)(2,1)}, u32[]{:S(2)}, u32[]{:S(2)}) %collective-permute-start.35) | collective-permute-done | bytes 720928 | tf_op jit(solution)/shard_map/ppermute | solution.py:538
  603.6 7.9 convolution_convert_fusion.7
  641.7 11.6 %attend_backward.3 = (bf16[8,64,768]{2,1,0:T(8,128)(2,1)S(1)}, bf16[3072,128]{1,0:T(8,128)(2,1)S(1)}) custom-call(s32[2,5]{1,0:T(2,128)S(1)} %copy-done.11, bf16[8,64,768]{2,1,0:T(8,128)(2,1)S(1)} %copy-done.1, bf16[3072,128]{1,0:T(8,128)(2,1)S(1)} %copy-done.7, s32[2,1,384]{2,1,0:T(1,128)S(1)} %copy-done.9, bf16[8,64,768]{2,1,0:T(8,128)(2,1)S(1)} %copy-done.15, ...), custom_call_target="tpu_custom_call" | custom-call | flops 80000000000 | bytes 16000000 | tf_op jit(solution)/shard_map/attend_backward/pallas_call | solution.py:256
  653.2 23.6 %collective-permute-done.48 = bf16[384,2048]{1,0:T(8,128)(2,1)S(1)} collective-permute-done((bf16[384,2048]{1,0:T(8,128)(2,1)S(1)}, bf16[384,2048]{1,0:T(8,128)(2,1)S(1)}, u32[]{:S(2)}, u32[]{:S(2)}) %collective-permute-start.48) | collective-permute-done | bytes 1572896 | tf_op jit(solution)/shard_map/ppermute | solution.py:538
  681.3 7.9 convolution_convert_fusion.6
  695.8 5.0 add_convert_fusion.1
  733.7 6.3 fusion.30
  771.4 17.1 %collective-permute-done.68 = bf16[2,128,512]{2,1,0:T(8,128)(2,1)S(1)} collective-permute-done((bf16[2,128,512]{2,1,0:T(8,128)(2,1)S(1)}, bf16[2,128,512]{2,1,0:T(8,128)(2,1)S(1)}, u32[]{:S(2)}, u32[]{:S(2)}) %collective-permute-start.68) | collective-permute-done | bytes 262176 | tf_op jit(solution)/shard_map/ppermute | solution.py:538
  831.0 29.4 %collective-permute-done.61 = bf16[384,2048]{1,0:T(8,128)(2,1)S(1)} collective-permute-done((bf16[384,2048]{1,0:T(8,128)(2,1)S(1)}, bf16[384,2048]{1,0:T(8,128)(2,1)S(1)}, u32[]{:S(2)}, u32[]{:S(2)}) %collective-permute-start.61) | collective-permute-done | bytes 1572896 | tf_op jit(solution)/shard_map/ppermute | solution.py:538
  863.7 5.8 collective-permute-done.63
  (637 shorter events, 319.4 us)
Async XLA Ops:
  145.5 95.0 %collective-permute-start = (bf16[2,128,2816]{2,1,0:T(8,128)(2,1)}, bf16[2,128,2816]{2,1,0:T(8,128)(2,1)}, u32[]{:S(2)}, u32[]{:S(2)}) collective-permute-start(bf16[2,128,2816]{2,1,0:T(8,128)(2,1)} %get-tuple-element.68), channel_id=1, source_target_pairs={{0,2},{1,3},{2,4},{3,5},{4,6},{5,7},{6,22},{7,23},{8,10},{9,11},{1... | collective-permute-start | bytes 4325384 | tf_op jit(solution)/shard_map/ppermute | solution.py:538
  146.3 94.2 %collective-permute-start.1 = (bf16[2,128,2816]{2,1,0:T(8,128)(2,1)}, bf16[2,128,2816]{2,1,0:T(8,128)(2,1)}, u32[]{:S(2)}, u32[]{:S(2)}) collective-permute-start(bf16[2,128,2816]{2,1,0:T(8,128)(2,1)} %get-tuple-element.68), channel_id=1, source_target_pairs={{0,16},{1,17},{2,0},{3,1},{4,2},{5,3},{6,4},{7,5},{8,24},{9,25},{1... | collective-permute-start | bytes 4325384 | tf_op jit(solution)/shard_map/ppermute | solution.py:538
  147.6 33.2 %collective-permute-start.2 = (s32[1,3]{1,0:T(1,128)S(1)}, s32[1,3]{1,0:T(1,128)S(1)}, u32[]{:S(2)}, u32[]{:S(2)}) collective-permute-start(s32[1,3]{1,0:T(1,128)S(1)} %copy-done.106), channel_id=1, source_target_pairs={{0,8},{1,9},{2,10},{3,11},{4,12},{5,13},{6,14},{7,15},{8,0},{9,1},... | collective-permute-start | bytes 44 | tf_op jit(solution)/shard_map/ppermute | solution.py:538
  147.6 189.3 %collective-permute-start.22 = (bf16[384,2048]{1,0:T(8,128)(2,1)}, bf16[384,2048]{1,0:T(8,128)(2,1)}, u32[]{:S(2)}, u32[]{:S(2)}) collective-permute-start(bf16[384,2048]{1,0:T(8,128)(2,1)} %bitcast.68), channel_id=1, source_target_pairs={{0,8},{1,9},{2,10},{3,11},{4,12},{5,13},{6,14},{7,15},{8,0},{9,1},... | collective-permute-start | bytes 4718600 | tf_op jit(solution)/shard_map/ppermute | solution.py:538
  283.8 38.9 %collective-permute-start.8 = (bf16[2,128,2816]{2,1,0:T(8,128)(2,1)S(1)}, bf16[2,128,2816]{2,1,0:T(8,128)(2,1)S(1)}, u32[]{:S(2)}, u32[]{:S(2)}) collective-permute-start(bf16[2,128,2816]{2,1,0:T(8,128)(2,1)S(1)} %collective-permute-done.6), channel_id=1, source_target_pairs={{0,2},{1,3},{2,4},{3,5},{4,6},{5,7},{6,22},{7,23},{8,10},{9,11},{1... | collective-permute-start | bytes 4325384 | tf_op jit(solution)/shard_map/ppermute | solution.py:538
  285.6 37.2 %collective-permute-start.9 = (bf16[2,128,2816]{2,1,0:T(8,128)(2,1)S(1)}, bf16[2,128,2816]{2,1,0:T(8,128)(2,1)S(1)}, u32[]{:S(2)}, u32[]{:S(2)}) collective-permute-start(bf16[2,128,2816]{2,1,0:T(8,128)(2,1)S(1)} %collective-permute-done.7), channel_id=1, source_target_pairs={{0,16},{1,17},{2,0},{3,1},{4,2},{5,3},{6,4},{7,5},{8,24},{9,25},{1... | collective-permute-start | bytes 4325384 | tf_op jit(solution)/shard_map/ppermute | solution.py:538
  286.7 35.7 %collective-permute-start.14 = (bf16[384,2048]{1,0:T(8,128)(2,1)S(1)}, bf16[384,2048]{1,0:T(8,128)(2,1)S(1)}, u32[]{:S(2)}, u32[]{:S(2)}) collective-permute-start(bf16[384,2048]{1,0:T(8,128)(2,1)S(1)} %add_convert_fusion.6), channel_id=1, source_target_pairs={{0,8},{1,9},{2,10},{3,11},{4,12},{5,13},{6,14},{7,15},{8,0},{9,1},... | collective-permute-start | bytes 4718600 | tf_op jit(solution)/shard_map/ppermute | solution.py:538
  334.9 35.6 %collective-permute-start.19 = (bf16[384,2048]{1,0:T(8,128)(2,1)S(1)}, bf16[384,2048]{1,0:T(8,128)(2,1)}, u32[]{:S(2)}, u32[]{:S(2)}) collective-permute-start(bf16[384,2048]{1,0:T(8,128)(2,1)S(1)} %multiply_convert_fusion.6), channel_id=1, source_target_pairs={{0,8},{1,9},{2,10},{3,11},{4,12},{5,13},{6,14},{7,15},{8,0},{9,1},... | collective-permute-start | bytes 4718600 | tf_op jit(solution)/shard_map/ppermute | solution.py:538
  336.7 33.8 %collective-permute-start.16 = (bf16[384,2048]{1,0:T(8,128)(2,1)S(1)}, bf16[384,2048]{1,0:T(8,128)(2,1)S(1)}, u32[]{:S(2)}, u32[]{:S(2)}) collective-permute-start(bf16[384,2048]{1,0:T(8,128)(2,1)S(1)} %multiply_convert_fusion.6), channel_id=1, source_target_pairs={{0,1},{1,0},{2,3},{3,2},{4,5},{5,4},{6,7},{7,6},{8,9},{9,8},{10,11... | collective-permute-start | bytes 4718600 | tf_op jit(solution)/shard_map/ppermute | solution.py:538
  336.9 46.3 %collective-permute-start.21 = (bf16[384,2048]{1,0:T(8,128)(2,1)}, bf16[384,2048]{1,0:T(8,128)(2,1)S(1)}, u32[]{:S(2)}, u32[]{:S(2)}) collective-permute-start(bf16[384,2048]{1,0:T(8,128)(2,1)} %bitcast.68), channel_id=1, source_target_pairs={{0,1},{1,0},{2,3},{3,2},{4,5},{5,4},{6,7},{7,6},{8,9},{9,8},{10,11... | collective-permute-start | bytes 4718600 | tf_op jit(solution)/shard_map/ppermute | solution.py:538
  347.5 65.1 %collective-permute-start.23 = (bf16[384,2048]{1,0:T(8,128)(2,1)}, bf16[384,2048]{1,0:T(8,128)(2,1)S(1)}, u32[]{:S(2)}, u32[]{:S(2)}) collective-permute-start(bf16[384,2048]{1,0:T(8,128)(2,1)} %collective-permute-done.22), channel_id=1, source_target_pairs={{0,1},{1,0},{2,3},{3,2},{4,5},{5,4},{6,7},{7,6},{8,9},{9,8},{10,11... | collective-permute-start | bytes 4718600 | tf_op jit(solution)/shard_map/ppermute | solution.py:538
  496.5 48.1 %collective-permute-start.26 = (bf16[2,128,2816]{2,1,0:T(8,128)(2,1)}, bf16[2,128,2816]{2,1,0:T(8,128)(2,1)}, u32[]{:S(2)}, u32[]{:S(2)}) collective-permute-start(bf16[2,128,2816]{2,1,0:T(8,128)(2,1)} %pad_maximum_fusion.7), channel_id=1, source_target_pairs={{0,2},{1,3},{2,4},{3,5},{4,6},{5,7},{6,22},{7,23},{8,10},{9,11},{1... | collective-permute-start | bytes 4325384 | tf_op jit(solution)/shard_map/ppermute | solution.py:538
  499.8 44.8 %collective-permute-start.27 = (bf16[2,128,2816]{2,1,0:T(8,128)(2,1)}, bf16[2,128,2816]{2,1,0:T(8,128)(2,1)}, u32[]{:S(2)}, u32[]{:S(2)}) collective-permute-start(bf16[2,128,2816]{2,1,0:T(8,128)(2,1)} %pad_maximum_fusion.8), channel_id=1, source_target_pairs={{0,16},{1,17},{2,0},{3,1},{4,2},{5,3},{6,4},{7,5},{8,24},{9,25},{1... | collective-permute-start | bytes 4325384 | tf_op jit(solution)/shard_map/ppermute | solution.py:538
  502.8 37.0 %collective-permute-start.32 = (bf16[384,2048]{1,0:T(8,128)(2,1)}, bf16[384,2048]{1,0:T(8,128)(2,1)S(1)}, u32[]{:S(2)}, u32[]{:S(2)}) collective-permute-start(bf16[384,2048]{1,0:T(8,128)(2,1)} %add_convert_fusion.5), channel_id=1, source_target_pairs={{0,8},{1,9},{2,10},{3,11},{4,12},{5,13},{6,14},{7,15},{8,0},{9,1},... | collective-permute-start | bytes 4718600 | tf_op jit(solution)/shard_map/ppermute | solution.py:538
  544.9 78.7 %collective-permute-start.42 = (bf16[384,2048]{1,0:T(8,128)(2,1)S(1)}, bf16[384,2048]{1,0:T(8,128)(2,1)S(1)}, u32[]{:S(2)}, u32[]{:S(2)}) collective-permute-start(bf16[384,2048]{1,0:T(8,128)(2,1)S(1)} %convert_element_type.760), channel_id=1, source_target_pairs={{0,8},{1,9},{2,10},{3,11},{4,12},{5,13},{6,14},{7,15},{8,0},{9,1},... | collective-permute-start | bytes 4718600 | tf_op jit(solution)/shard_map/ppermute | solution.py:538
  551.1 51.4 %collective-permute-start.33 = (bf16[2,128,2816]{2,1,0:T(8,128)(2,1)}, bf16[2,128,2816]{2,1,0:T(8,128)(2,1)S(1)}, u32[]{:S(2)}, u32[]{:S(2)}) collective-permute-start(bf16[2,128,2816]{2,1,0:T(8,128)(2,1)} %get-tuple-element.158), channel_id=1, source_target_pairs={{0,2},{1,3},{2,4},{3,5},{4,6},{5,7},{6,22},{7,23},{8,10},{9,11},{1... | collective-permute-start | bytes 4325384 | tf_op jit(solution)/shard_map/ppermute | solution.py:538
  553.4 49.1 %collective-permute-start.34 = (bf16[2,128,2816]{2,1,0:T(8,128)(2,1)S(1)}, bf16[2,128,2816]{2,1,0:T(8,128)(2,1)S(1)}, u32[]{:S(2)}, u32[]{:S(2)}) collective-permute-start(bf16[2,128,2816]{2,1,0:T(8,128)(2,1)S(1)} %get-tuple-element.157), channel_id=1, source_target_pairs={{0,16},{1,17},{2,0},{3,1},{4,2},{5,3},{6,4},{7,5},{8,24},{9,25},{1... | collective-permute-start | bytes 4325384 | tf_op jit(solution)/shard_map/ppermute | solution.py:538
  554.6 46.0 %collective-permute-start.35 = (bf16[2,128,1408]{2,1,0:T(8,128)(2,1)}, bf16[2,128,1408]{2,1,0:T(8,128)(2,1)}, u32[]{:S(2)}, u32[]{:S(2)}) collective-permute-start(bf16[2,128,1408]{2,1,0:T(8,128)(2,1)} %pad_maximum_fusion.15), channel_id=1, source_target_pairs={{0,2},{1,3},{2,4},{3,5},{4,6},{5,7},{6,22},{7,23},{8,10},{9,11},{1... | collective-permute-start | bytes 2162696 | tf_op jit(solution)/shard_map/ppermute | solution.py:538
  557.5 44.9 %collective-permute-start.36 = (bf16[2,128,1408]{2,1,0:T(8,128)(2,1)}, bf16[2,128,1408]{2,1,0:T(8,128)(2,1)S(1)}, u32[]{:S(2)}, u32[]{:S(2)}) collective-permute-start(bf16[2,128,1408]{2,1,0:T(8,128)(2,1)} %pad_maximum_fusion.16), channel_id=1, source_target_pairs={{0,16},{1,17},{2,0},{3,1},{4,2},{5,3},{6,4},{7,5},{8,24},{9,25},{1... | collective-permute-start | bytes 2162696 | tf_op jit(solution)/shard_map/ppermute | solution.py:538
  628.4 51.7 %collective-permute-start.38 = (bf16[2,128,2816]{2,1,0:T(8,128)(2,1)}, bf16[2,128,2816]{2,1,0:T(8,128)(2,1)S(1)}, u32[]{:S(2)}, u32[]{:S(2)}) collective-permute-start(bf16[2,128,2816]{2,1,0:T(8,128)(2,1)} %get-tuple-element.156), channel_id=1, source_target_pairs={{0,2},{1,3},{2,4},{3,5},{4,6},{5,7},{6,22},{7,23},{8,10},{9,11},{1... | collective-permute-start | bytes 4325384 | tf_op jit(solution)/shard_map/ppermute | solution.py:538
  631.0 49.0 %collective-permute-start.39 = (bf16[2,128,2816]{2,1,0:T(8,128)(2,1)S(1)}, bf16[2,128,2816]{2,1,0:T(8,128)(2,1)}, u32[]{:S(2)}, u32[]{:S(2)}) collective-permute-start(bf16[2,128,2816]{2,1,0:T(8,128)(2,1)S(1)} %get-tuple-element.155), channel_id=1, source_target_pairs={{0,16},{1,17},{2,0},{3,1},{4,2},{5,3},{6,4},{7,5},{8,24},{9,25},{1... | collective-permute-start | bytes 4325384 | tf_op jit(solution)/shard_map/ppermute | solution.py:538
  631.0 47.8 %collective-permute-start.40 = (bf16[2,128,1408]{2,1,0:T(8,128)(2,1)}, bf16[2,128,1408]{2,1,0:T(8,128)(2,1)S(1)}, u32[]{:S(2)}, u32[]{:S(2)}) collective-permute-start(bf16[2,128,1408]{2,1,0:T(8,128)(2,1)} %get-tuple-element.172), channel_id=1, source_target_pairs={{0,2},{1,3},{2,4},{3,5},{4,6},{5,7},{6,22},{7,23},{8,10},{9,11},{1... | collective-permute-start | bytes 2162696 | tf_op jit(solution)/shard_map/ppermute | solution.py:538
  635.3 44.8 %collective-permute-start.41 = (bf16[2,128,1408]{2,1,0:T(8,128)(2,1)}, bf16[2,128,1408]{2,1,0:T(8,128)(2,1)S(1)}, u32[]{:S(2)}, u32[]{:S(2)}) collective-permute-start(bf16[2,128,1408]{2,1,0:T(8,128)(2,1)} %get-tuple-element.171), channel_id=1, source_target_pairs={{0,16},{1,17},{2,0},{3,1},{4,2},{5,3},{6,4},{7,5},{8,24},{9,25},{1... | collective-permute-start | bytes 2162696 | tf_op jit(solution)/shard_map/ppermute | solution.py:538
  640.7 36.1 %collective-permute-start.48 = (bf16[384,2048]{1,0:T(8,128)(2,1)S(1)}, bf16[384,2048]{1,0:T(8,128)(2,1)S(1)}, u32[]{:S(2)}, u32[]{:S(2)}) collective-permute-start(bf16[384,2048]{1,0:T(8,128)(2,1)S(1)} %add_convert_fusion.4), channel_id=1, source_target_pairs={{0,8},{1,9},{2,10},{3,11},{4,12},{5,13},{6,14},{7,15},{8,0},{9,1},... | collective-permute-start | bytes 4718600 | tf_op jit(solution)/shard_map/ppermute | solution.py:538
  692.2 134.5 %collective-permute-start.49 = (bf16[384,2048]{1,0:T(8,128)(2,1)}, bf16[384,2048]{1,0:T(8,128)(2,1)}, u32[]{:S(2)}, u32[]{:S(2)}) collective-permute-start(bf16[384,2048]{1,0:T(8,128)(2,1)} %slice.562), channel_id=1, source_target_pairs={{0,1},{1,0},{2,3},{3,2},{4,5},{5,4},{6,7},{7,6},{8,9},{9,8},{10,11... | collective-permute-start | bytes 4718600 | tf_op jit(solution)/shard_map/ppermute | solution.py:538
  712.2 55.2 %collective-permute-start.78 = (bf16[64,2816]{1,0:T(8,128)(2,1)}, bf16[64,2816]{1,0:T(8,128)(2,1)}, u32[]{:S(2)}, u32[]{:S(2)}) collective-permute-start(bf16[64,2816]{1,0:T(8,128)(2,1)} %get-tuple-element.214), channel_id=1, source_target_pairs={{0,9},{1,8},{2,11},{3,10},{4,13},{5,12},{6,15},{7,14},{8,1},{9,0},... | collective-permute-start | bytes 1081352 | tf_op jit(solution)/shard_map/ppermute | solution.py:538
  715.1 52.6 %collective-permute-start.79 = (bf16[64,2816]{1,0:T(8,128)(2,1)}, bf16[64,2816]{1,0:T(8,128)(2,1)}, u32[]{:S(2)}, u32[]{:S(2)}) collective-permute-start(bf16[64,2816]{1,0:T(8,128)(2,1)} %get-tuple-element.140), channel_id=1, source_target_pairs={{0,8},{1,9},{2,10},{3,11},{4,12},{5,13},{6,14},{7,15},{8,0},{9,1},... | collective-permute-start | bytes 1081352 | tf_op jit(solution)/shard_map/ppermute | solution.py:538
  765.2 32.0 %collective-permute-start.82 = (bf16[2,128,1408]{2,1,0:T(8,128)(2,1)S(1)}, bf16[2,128,1408]{2,1,0:T(8,128)(2,1)S(1)}, u32[]{:S(2)}, u32[]{:S(2)}) collective-permute-start(bf16[2,128,1408]{2,1,0:T(8,128)(2,1)S(1)} %copy-done.72), channel_id=1, source_target_pairs={{0,16},{1,17},{2,0},{3,1},{4,2},{5,3},{6,4},{7,5},{8,24},{9,25},{1... | collective-permute-start | bytes 2162696 | tf_op jit(solution)/shard_map/ppermute | solution.py:538
  767.5 31.5 %collective-permute-start.81 = (bf16[2,128,1408]{2,1,0:T(8,128)(2,1)S(1)}, bf16[2,128,1408]{2,1,0:T(8,128)(2,1)S(1)}, u32[]{:S(2)}, u32[]{:S(2)}) collective-permute-start(bf16[2,128,1408]{2,1,0:T(8,128)(2,1)S(1)} %copy-done.71), channel_id=1, source_target_pairs={{0,2},{1,3},{2,4},{3,5},{4,6},{5,7},{6,22},{7,23},{8,10},{9,11},{1... | collective-permute-start | bytes 2162696 | tf_op jit(solution)/shard_map/ppermute | solution.py:538
  823.0 37.9 %collective-permute-start.55 = (bf16[2,128,640]{2,1,0:T(8,128)(2,1)S(1)}, bf16[2,128,640]{2,1,0:T(8,128)(2,1)S(1)}, u32[]{:S(2)}, u32[]{:S(2)}) collective-permute-start(bf16[2,128,640]{2,1,0:T(8,128)(2,1)S(1)} %get-tuple-element.184), channel_id=1, source_target_pairs={{0,2},{1,3},{2,4},{3,5},{4,6},{5,7},{6,22},{7,23},{8,10},{9,11},{1... | collective-permute-start | bytes 983048 | tf_op jit(solution)/shard_map/ppermute | solution.py:538
  823.9 36.9 %collective-permute-start.58 = (bf16[2,128,640]{2,1,0:T(8,128)(2,1)S(1)}, bf16[2,128,640]{2,1,0:T(8,128)(2,1)S(1)}, u32[]{:S(2)}, u32[]{:S(2)}) collective-permute-start(bf16[2,128,640]{2,1,0:T(8,128)(2,1)S(1)} %get-tuple-element.183), channel_id=1, source_target_pairs={{0,16},{1,17},{2,0},{3,1},{4,2},{5,3},{6,4},{7,5},{8,24},{9,25},{1... | collective-permute-start | bytes 983048 | tf_op jit(solution)/shard_map/ppermute | solution.py:538
  825.0 35.5 %collective-permute-start.61 = (bf16[384,2048]{1,0:T(8,128)(2,1)S(1)}, bf16[384,2048]{1,0:T(8,128)(2,1)S(1)}, u32[]{:S(2)}, u32[]{:S(2)}) collective-permute-start(bf16[384,2048]{1,0:T(8,128)(2,1)S(1)} %add_convert_fusion.2), channel_id=1, source_target_pairs={{0,8},{1,9},{2,10},{3,11},{4,12},{5,13},{6,14},{7,15},{8,0},{9,1},... | collective-permute-start | bytes 4718600 | tf_op jit(solution)/shard_map/ppermute | solution.py:538
  (182 other events, 2588.1 us)

commit v4 on v3

--- a/solution.py
+++ b/solution.py
@@ -289,6 +289,62 @@
     )(meta, query, keyval, first, out, lse, grad)
 
 
+def feed_kernel(normed, cotangent, w_gate_up, w_down_t, *rest, columns):
+    hidden, d_gate_up = rest[-2:]
+    step = 256
+    for low in range(0, columns, step):
+        high = min(low + step, columns)
+        gate = contract(normed[...], w_gate_up[:, low:high], 1, 0)
+        up = contract(normed[...], w_gate_up[:, columns + low : columns + high], 1, 0)
+        d_hidden = contract(cotangent[...], w_down_t[:, low:high], 1, 0)
+        sigmoid = 1.0 / (1.0 + jnp.exp(-gate))
+        silu = gate * sigmoid
+        hidden[:, low:high] = (silu * up).astype(BF)
+        d_gate_up[:, low:high] = (
+            d_hidden * up * sigmoid * (1.0 + gate * (1.0 - sigmoid))
+        ).astype(BF)
+        d_gate_up[:, columns + low : columns + high] = (d_hidden * silu).astype(BF)
+
+
+def feed_forward(normed, cotangent, w_gate_up, w_down_t, half, before=()):
+    tokens, width = normed.shape
+    columns = w_down_t.shape[1]
+    tile = min(256, tokens)
+    shift = half * (tokens // tile)
+    token_spec = pl.BlockSpec((tile, width), lambda i: (i, 0))
+
+    def weight_spec(wide):
+        return pl.BlockSpec((width, wide), lambda i: (0, 0), pipeline_mode=pl.Buffered(1))
+
+    def out_spec(wide):
+        return pl.BlockSpec((tile, wide), lambda i: (i + shift, 0))
+
+    return pl.pallas_call(
+        functools.partial(feed_kernel, columns=columns),
+        grid=(tokens // tile,),
+        in_specs=[
+            token_spec,
+            token_spec,
+            weight_spec(2 * columns),
+            weight_spec(columns),
+            *[pl.BlockSpec(memory_space=pl.ANY) for _ in before],
+        ],
+        out_specs=(out_spec(columns), out_spec(2 * columns)),
+        out_shape=(
+            jax.ShapeDtypeStruct((2 * tokens, columns), BF),
+            jax.ShapeDtypeStruct((2 * tokens, 2 * columns), BF),
+        ),
+        input_output_aliases={4 + i: i for i in range(len(before))},
+        compiler_params=pltpu.CompilerParams(
+            dimension_semantics=("arbitrary",), vmem_limit_bytes=56 * 1024 * 1024
+        ),
+        cost_estimate=pl.CostEstimate(
+            flops=6 * tokens * width * columns, bytes_accessed=6 * width * columns, transcendentals=0
+        ),
+        name="feed_forward",
+    )(normed, cotangent, w_gate_up, w_down_t, *before)
+
+
 def opening_kernel(
     tokens,
     quarters_attn,
@@ -297,7 +353,7 @@
     group,
     whole_attn,
     whole_down,
-    chunk_gate_up,
+    whole_gate_up,
     local_sem,
     near_send,
     near_recv,
@@ -353,7 +409,7 @@
     targets = (
         whole_attn.at[y_at, x_at, z_at, my_rows],
         whole_down.at[y_at, x_at, z_at, my_rows],
-        chunk_gate_up.at[x_at, my_rows],
+        whole_gate_up.at[y_at, x_at, z_at, my_rows],
     )
     quarters = (quarters_attn, quarters_down, quarters_gate_up)
     locals_ = [
@@ -457,7 +513,7 @@
             jax.ShapeDtypeStruct((GROUP, *tokens.shape), BF),
             whole(quarters_attn),
             whole(quarters_down),
-            jax.ShapeDtypeStruct((2, 2 * own_rows, quarters_gate_up.shape[2]), BF),
+            whole(quarters_gate_up),
         ),
         in_specs=[anywhere] * 4,
         out_specs=(anywhere,) * 4,
@@ -473,6 +529,214 @@
         compiler_params=pltpu.CompilerParams(collective_id=0, has_side_effects=True),
         name="opening",
     )(tokens, quarters_attn, quarters_down, quarters_gate_up)
+
+
+def closing_kernel(
+    partial,
+    near_part,
+    far_part,
+    chunk_gate_up,
+    chunk_down,
+    d_normed,
+    owned_attn,
+    owned_gate_up,
+    owned_down,
+    land,
+    chunk_attn,
+    core_land,
+    x_stage,
+    x_land,
+    local_sem,
+    near_send,
+    near_recv,
+    swap_send,
+    swap_recv,
+    hop_send,
+    hop_recv,
+    *,
+    wide,
+    deep,
+    own_rows,
+):
+    ring, half_ring = wide * deep, wide * deep // 2
+    f_at, s_at = lax.axis_index("fsdp"), lax.axis_index("seq")
+    y_at, x_at, z_at, c_at = f_at // 2, lax.rem(f_at, 2), s_at // 2, lax.rem(s_at, 2)
+    here = y_at * deep + jnp.where(lax.rem(y_at, 2) == 0, z_at, deep - 1 - z_at)
+
+    def ring_place(offset):
+        index = lax.rem(here + offset + 2 * ring, ring)
+        row, col = index // deep, lax.rem(index, deep)
+        return row, jnp.where(lax.rem(row, 2) == 0, col, deep - 1 - col)
+
+    def ring_device(offset):
+        row, col = ring_place(offset)
+        return row * 2 + x_at, col * 2 + c_at
+
+    moves = ((0, 1), (1, 0), (1, 1))
+
+    def other(dx, dc):
+        return lax.rem(x_at + dx, 2), lax.rem(c_at + dc, 2)
+
+    def group_device(dx, dc):
+        x, c = other(dx, dc)
+        return y_at * 2 + x, z_at * 2 + c
+
+    def remote(source, target, send, recv, device):
+        return pltpu.make_async_remote_copy(
+            src_ref=source,
+            dst_ref=target,
+            send_sem=send,
+            recv_sem=recv,
+            device_id=device,
+            device_id_type=pl.DeviceIdType.MESH,
+        )
+
+    barrier = pltpu.get_barrier_semaphore()
+    partners = [group_device(*move) for move in moves] + [ring_device(1), ring_device(-1)]
+    for device in partners:
+        pl.semaphore_signal(barrier, inc=1, device_id=device, device_id_type=pl.DeviceIdType.MESH)
+    pl.semaphore_wait(barrier, len(partners))
+
+    rows = x_land.shape[0]
+    far_core = remote(
+        far_part.at[rows:], core_land.at[0], near_send.at[0], near_recv.at[0], group_device(0, 1)
+    )
+    near_core = remote(
+        near_part.at[rows:], core_land.at[1], near_send.at[1], near_recv.at[1], group_device(0, 1)
+    )
+    far_x = remote(x_stage, x_land, near_send.at[2], near_recv.at[2], group_device(1, 0))
+
+    def hop(side, step):
+        direction = 1 - 2 * side
+        if step == 1:
+            row, col = ring_place(direction * half_ring)
+            source, target = partial.at[row, side, col], land.at[side, 0, side]
+        else:
+            source, target = land.at[side, step - 2], land.at[side, step - 1]
+        return remote(
+            source,
+            target,
+            hop_send.at[side, step - 1],
+            hop_recv.at[side, step - 1],
+            ring_device(direction),
+        )
+
+    chunks = (chunk_attn, chunk_gate_up, chunk_down)
+    owned = (owned_attn, owned_gate_up, owned_down)
+
+    def piece(i, x, c):
+        return chunks[i].at[x, pl.ds(pl.multiple_of(c * own_rows, own_rows), own_rows)]
+
+    def swaps(i):
+        copies = []
+        for j, (dx, dc) in enumerate(moves):
+            copies.append(
+                remote(
+                    piece(i, *other(dx, dc)),
+                    owned[i].at[x_at * 2 + c_at],
+                    swap_send.at[i, j],
+                    swap_recv.at[i, j],
+                    group_device(dx, dc),
+                )
+            )
+        return copies
+
+    swap = [swaps(i) for i in range(3)]
+    keep = [
+        pltpu.make_async_copy(piece(i, x_at, c_at), owned[i].at[x_at * 2 + c_at], local_sem.at[i])
+        for i in range(3)
+    ]
+
+    far_core.start()
+    near_core.start()
+    for side in range(2):
+        hop(side, 1).start()
+    far_core.wait_recv()
+    x_stage[...] = (far_part[:rows].astype(F32) + core_land[0].astype(F32)).astype(BF)
+    far_x.start()
+    for i in (1, 2):
+        for copy in swap[i]:
+            copy.start()
+        keep[i].start()
+    for step in range(2, half_ring + 1):
+        for side in range(2):
+            hop(side, step - 1).wait_recv()
+            row, col = ring_place((1 - 2 * side) * (half_ring - step + 1))
+            if step == 2:
+                mine = partial[row, side, col].astype(F32) + land[side, 0, side].astype(F32)
+                land[side, 0, side] = mine.astype(BF)
+                land[side, 0, 1 - side] = partial[row, 1 - side, col]
+            else:
+                for half in range(2):
+                    mine = partial[row, half, col].astype(F32)
+                    mine = mine + land[side, step - 2, half].astype(F32)
+                    land[side, step - 2, half] = mine.astype(BF)
+            hop(side, step).start()
+    near_core.wait_recv()
+    for side in range(2):
+        hop(side, half_ring).wait_recv()
+    for half in range(2):
+        total = partial[y_at, half, z_at].astype(F32) + land[0, half_ring - 1, half].astype(F32)
+        total = total + land[1, half_ring - 1, half].astype(F32)
+        chunk_attn[half] = total.astype(BF)
+    for copy in swap[0]:
+        copy.start()
+    keep[0].start()
+    far_x.wait_recv()
+    d_normed[...] = (
+        near_part[:rows].astype(F32) + core_land[1].astype(F32) + x_land[...].astype(F32)
+    )
+    for i in (1, 2, 0):
+        keep[i].wait()
+        for copy in swap[i]:
+            copy.wait_recv()
+    for copy in swap[0] + swap[1] + swap[2] + [far_core, near_core, far_x]:
+        copy.wait_send()
+    for side in range(2):
+        for step in range(1, half_ring + 1):
+            hop(side, step).wait_send()
+
+
+def closing(partial, near_part, far_part, chunk_gate_up, chunk_down, wide, deep):
+    own_rows = partial.shape[3] // 2
+    half_ring = wide * deep // 2
+    rows, width = near_part.shape[0] // 2, near_part.shape[1]
+    columns = partial.shape[4]
+    anywhere = pl.BlockSpec(memory_space=pl.ANY)
+    vmem = pl.BlockSpec(memory_space=pltpu.VMEM)
+
+    def quarters(wanted):
+        return jax.ShapeDtypeStruct((GROUP, own_rows, wanted), BF)
+
+    return pl.pallas_call(
+        functools.partial(closing_kernel, wide=wide, deep=deep, own_rows=own_rows),
+        out_shape=(
+            jax.ShapeDtypeStruct((rows, width), F32),
+            quarters(columns),
+            quarters(chunk_gate_up.shape[2]),
+            quarters(chunk_down.shape[2]),
+        ),
+        in_specs=[vmem, vmem, vmem, anywhere, anywhere],
+        out_specs=(vmem, anywhere, anywhere, anywhere),
+        scratch_shapes=[
+            pltpu.VMEM((2, half_ring, 2, 2 * own_rows, columns), BF),
+            pltpu.VMEM((2, 2 * own_rows, columns), BF),
+            pltpu.VMEM((2, rows, width), BF),
+            pltpu.VMEM((rows, width), BF),
+            pltpu.VMEM((rows, width), BF),
+            pltpu.SemaphoreType.DMA((3,)),
+            pltpu.SemaphoreType.DMA((3,)),
+            pltpu.SemaphoreType.DMA((3,)),
+            pltpu.SemaphoreType.DMA((3, 3)),
+            pltpu.SemaphoreType.DMA((3, 3)),
+            pltpu.SemaphoreType.DMA((2, half_ring)),
+            pltpu.SemaphoreType.DMA((2, half_ring)),
+        ],
+        compiler_params=pltpu.CompilerParams(
+            collective_id=1, has_side_effects=True, vmem_limit_bytes=56 * 1024 * 1024
+        ),
+        name="closing",
+    )(partial, near_part, far_part, chunk_gate_up, chunk_down)
 
 
 def shards(
@@ -561,9 +825,13 @@
         return [[ordered[0][x], ordered[1][x]] for x in range(2)]
 
     class Gather:
-        def __init__(self, chunk):
+        def __init__(self, room):
+            self.room = room
+            row, col = place_at(0)
+            size = (1, 2, 1, *room.shape[3:])
+            chunk = lax.dynamic_slice(room, (row, 0, col, 0, 0), size).reshape(2, *room.shape[3:])
             self.right = self.left = chunk
-            self.step, self.got = 0, [(0, 0, chunk)]
+            self.step, self.got = 0, []
 
         def advance(self, times):
             for _ in range(min(times, half_ring - self.step)):
@@ -581,17 +849,14 @@
         def wait_for(self, value):
             self.right, self.left = after((self.right, self.left), value)
 
-        def whole(self, cuts):
-            results = []
-            for low, high in zip(cuts[:-1], cuts[1:]):
-                result = jnp.zeros((wide, 2, deep, 2 * own_rows, high - low), BF)
-                for offset, x_from, piece in self.got:
-                    row, col = place_at(offset)
-                    result = lax.dynamic_update_slice(
-                        result, piece[None, :, None, :, low:high], (row, x_from, col, 0, 0)
-                    )
-                results.append(result.reshape(-1, high - low))
-            return results
+        def whole(self):
+            result = self.room
+            for offset, x_from, piece in self.got:
+                row, col = place_at(offset)
+                result = lax.dynamic_update_slice(
+                    result, piece[None, :, None], (row, x_from, col, 0, 0)
+                )
+            return result.reshape(-1, result.shape[4])
 
     class Scatter:
         def __init__(self, partial):
@@ -647,17 +912,6 @@
 
     per_window = -(-half_ring // 4)
 
-    def to_owners(scatter):
-        chunk = scatter.result().astype(BF)
-        blocks = [[chunk[x, c * own_rows : (c + 1) * own_rows] for c in range(2)] for x in range(2)]
-        relative = absolute(blocks)
-        got = [
-            [relative[0][0], send(relative[0][1], core_perm)],
-            [send(relative[1][0], x_perm), send(relative[1][1], cross_perm)],
-        ]
-        final = absolute(got)
-        return jnp.stack([final[0][0], final[0][1], final[1][0], final[1][1]]).astype(F32)
-
     def columns_of(quarters):
         return quarters.transpose(1, 0, 2).reshape(own_rows, -1)
 
@@ -685,33 +939,6 @@
     qkv_cols = q_cols + 2 * HD
     hidden_cols = w_gate.shape[1] // GROUP
     start_rows = [starts[0], send(starts, x_perm)[0]]
-    gain_columns = jnp.pad(jnp.stack([norm_attn, norm_mlp], axis=1), ((0, 0), (0, 126)))
-    own_tokens = tokens[0]
-    group_blocks, whole_attn, whole_down, chunk_gate_up = opening(
-        own_tokens,
-        to_quarters([w_query, w_key, w_value, w_out.T, jnp.tile(gain_columns, (1, GROUP))]),
-        to_quarters([w_down.T]),
-        to_quarters([w_gate, w_up]),
-        wide,
-        deep,
-    )
-    group_tokens = [group_blocks[2 * dx : 2 * dx + 2].reshape(2 * rows, width) for dx in range(2)]
-    whole_attn = whole_attn.reshape(width, -1)
-    w_down_t = whole_down.reshape(width, -1)
-    w_qkv = whole_attn[:, :qkv_cols]
-    w_out_t = whole_attn[:, qkv_cols : qkv_cols + q_cols]
-    gains = whole_attn[:, qkv_cols + q_cols :].T.astype(F32)
-    gain_attn, gain_mlp = gains[0], gains[1]
-    ring_gate_up = Gather(chunk_gate_up)
-    rings = [ring_gate_up]
-
-    def advance(members, times=per_window):
-        for member in members:
-            member.advance(times)
-
-    advance(rings)
-    group_cotangent = gather_group(cotangent[0])
-
     block_at = [rows * (2 * z_at + (c_at ^ dc)) for dc in range(2)]
     within = jnp.arange(rows, dtype=jnp.int32)
     base_block = 2 * (z_at - deep + 1)
@@ -732,6 +959,34 @@
             for dc in range(2)
         ]
         metas.append(jnp.stack([jnp.stack(cell) for cell in cells]).astype(jnp.int32))
+
+    gain_columns = jnp.pad(jnp.stack([norm_attn, norm_mlp], axis=1), ((0, 0), (0, 126)))
+    own_tokens, tables, first_rows, metas = after((tokens[0], tables, first_rows, metas), start_rows[1])
+    own_tokens = after(own_tokens, (tables, first_rows, metas))
+    group_blocks, whole_attn, whole_down, whole_gate_up = opening(
+        own_tokens,
+        to_quarters([w_query, w_key, w_value, w_out.T, jnp.tile(gain_columns, (1, GROUP))]),
+        to_quarters([w_down.T]),
+        to_quarters([w_gate, w_up]),
+        wide,
+        deep,
+    )
+    group_tokens = [group_blocks[2 * dx : 2 * dx + 2].reshape(2 * rows, width) for dx in range(2)]
+    whole_attn = whole_attn.reshape(width, -1)
+    w_down_t = whole_down.reshape(width, -1)
+    w_qkv = whole_attn[:, :qkv_cols]
+    w_out_t = whole_attn[:, qkv_cols : qkv_cols + q_cols]
+    gains = whole_attn[:, qkv_cols + q_cols :].T.astype(F32)
+    gain_attn, gain_mlp = gains[0], gains[1]
+    ring_gate_up = Gather(whole_gate_up)
+    rings = [ring_gate_up]
+
+    def advance(members, times=per_window):
+        for member in members:
+            member.advance(times)
+
+    advance(rings)
+    group_cotangent = gather_group(after(cotangent[0], group_blocks))
 
     heads = HEADS // GROUP
     normed, scales, queries, keyvals, attended, lses = ([None, None] for _ in range(6))
@@ -763,33 +1018,32 @@
     attended_t = [a.reshape(q_cols, -1) for a in attended]
 
     scale_mlp = lax.rsqrt(jnp.mean(middle * middle, axis=1, keepdims=True) + EPSILON)
-    normed_mlp = gather_group((middle * scale_mlp * gain_mlp).astype(BF))
-    (w_gate_up,) = ring_gate_up.whole([0, 2 * hidden_cols])
-    hidden, d_gate_up = [None, None], [None, None]
-    for dx in range(2):
-        d_hidden = contract(group_cotangent[dx], w_down_t, 1, 0)
-        gate_up = contract(normed_mlp[dx], w_gate_up, 1, 0)
-        gate, up = gate_up[:, :hidden_cols], gate_up[:, hidden_cols:]
-        sigmoid = jax.nn.sigmoid(gate)
-        silu = gate * sigmoid
-        hidden[dx] = (silu * up).astype(BF)
-        d_gate = (d_hidden * up * sigmoid * (1.0 + gate * (1.0 - sigmoid))).astype(BF)
-        d_up = (d_hidden * silu).astype(BF)
-        d_gate_up[dx] = jnp.concatenate([d_gate, d_up], axis=1)
-    both_hidden = jnp.concatenate(hidden)
+    normed_own = (middle * scale_mlp * gain_mlp).astype(BF)
+    normed_far = send(normed_own, x_perm)
+    normed_mlp = [with_core(normed_own), None]
+    w_gate_up = ring_gate_up.whole()
+    both = feed_forward(normed_mlp[0], group_cotangent[0], w_gate_up, w_down_t, 0)
+    normed_far, both = stage([], (normed_far, both))
+    normed_mlp[1] = with_core(normed_far)
+    both = feed_forward(normed_mlp[1], group_cotangent[1], w_gate_up, w_down_t, 1, both)
+    both_hidden, both_d_gate_up = both
+    hidden = [both_hidden[: 2 * rows], both_hidden[2 * rows :]]
+    d_gate_up = [both_d_gate_up[: 2 * rows], both_d_gate_up[2 * rows :]]
     both_cotangent = jnp.concatenate(group_cotangent)
     both_normed = jnp.concatenate(normed_mlp)
-    both_d_gate_up = jnp.concatenate(d_gate_up)
+    far_part = contract(d_gate_up[1], w_gate_up, 1, 1).astype(BF)
+    far_sum = reduce_core(far_part).astype(BF)
+    far = send(far_sum, x_perm)
+    near_part = contract(after(d_gate_up[0], far_part), w_gate_up, 1, 1).astype(BF)
+    near = reduce_core(near_part)
+    both_hidden = after(both_hidden, (near_part, far_sum))
+    ring_down = Scatter(contract(both_cotangent, both_hidden, 0, 0).astype(BF))
+    ring_down.advance(per_window)
+    both_d_gate_up = after(both_d_gate_up, ring_down.parts)
     ring_gate_up = Scatter(contract(both_normed, both_d_gate_up, 0, 0).astype(BF))
+    far, ring_gate_up.parts = stage([ring_down], (far, ring_gate_up.parts))
+    far = far.astype(F32)
     ring_gate_up.advance(per_window)
-    far_part = contract(after(d_gate_up[1], ring_gate_up.parts), w_gate_up, 1, 1).astype(BF)
-    far = send_far(far_part)
-    near_part = contract(after(d_gate_up[0], far_part), w_gate_up, 1, 1).astype(BF)
-    near_part = stage([ring_gate_up], near_part)
-    ring_gate_up.advance(per_window)
-    near = reduce_core(near_part)
-    ring_down = Scatter(contract(both_cotangent, after(both_hidden, near_part), 0, 0).astype(BF))
-    ring_down.advance(per_window)
     d_normed_mlp = near + far
 
     def norm_backward(values, scale_rows, gain, grads_in):
@@ -801,15 +1055,14 @@
     gain_grad_mlp = jnp.sum(d_normed_mlp * middle * scale_mlp, axis=0)
     d_middle = norm_backward(middle, scale_mlp, gain_mlp, d_normed_mlp) + cotangent[0].astype(F32)
     rings = [ring_gate_up, ring_down]
-    d_middle = stage(rings, d_middle)
-    for member in rings:
-        member.advance(per_window)
-
-    d_branch = gather_group(d_middle.astype(BF))
-    d_keyval, d_query, d_attended = [None, None], [None, None], [None, None]
-    for dx in range(2):
-        part = contract(w_out_t, d_branch[dx], 0, 1).astype(BF)
-        d_attended[dx] = part.reshape(queries[dx].shape)
+
+    branch_own = d_middle.astype(BF)
+    branch_far = send(branch_own, x_perm)
+    d_branch = [with_core(branch_own), None]
+    d_keyval, d_query = [None, None], [None, None]
+
+    def d_attended(dx):
+        return contract(w_out_t, d_branch[dx], 0, 1).astype(BF).reshape(queries[dx].shape)
 
     def keyval_home(d_keyvals):
         chunks = [d_keyvals[2 * rows * i : 2 * rows * (i + 1)] for i in range(deep)]
@@ -818,18 +1071,21 @@
             total = total + send(chunks[deep - 1 - step], perm_of(along(-step))).astype(F32)
         return jnp.concatenate(swap_pair(c_at, [total[:rows], total[rows:]])).T
 
+    d_near = stage([ring_gate_up], d_attended(0))
+    advance(rings)
     d_query[0], d_keyvals = attend_backward(
-        metas[0], queries[0], keyvals[0], first_rows[0], attended[0], lses[0], d_attended[0]
-    )
-    d_query[0], d_keyvals = stage(rings, (d_query[0], d_keyvals))
-    for member in rings:
-        member.advance(per_window)
+        metas[0], queries[0], keyvals[0], first_rows[0], attended[0], lses[0], d_near
+    )
+    d_query[0], d_keyvals, branch_far = stage(rings, (d_query[0], d_keyvals, branch_far))
+    advance(rings)
     d_keyval[0] = keyval_home(d_keyvals)
+    d_branch[1] = with_core(branch_far)
     result_part = contract(after(hidden[1], d_query[0]), w_down_t, 1, 1).astype(BF)
-    result_far = send_far(result_part)
-    d_attended[1] = after(d_attended[1], (d_query[0], result_part))
+    result_sum = reduce_core(result_part).astype(BF)
+    result_far = send(result_sum, x_perm).astype(F32)
+    d_far = after(d_attended(1), (d_query[0], result_sum))
     d_query[1], d_keyvals = attend_backward(
-        metas[1], queries[1], keyvals[1], first_rows[1], attended[1], lses[1], d_attended[1]
+        metas[1], queries[1], keyvals[1], first_rows[1], attended[1], lses[1], d_far
     )
     d_query[1], d_keyvals, d_keyval[0], result_far = stage(
         rings, (d_query[1], d_keyvals, d_keyval[0], result_far)
@@ -840,8 +1096,6 @@
     grad_out_part = contract(d_branch[0], attended_t[0], 0, 1) + contract(
         after(d_branch[1], d_query[1]), attended_t[1], 0, 1
     )
-    ring_out = Scatter(grad_out_part.astype(BF))
-    ring_out.advance(half_ring)
     result_near = reduce_core(contract(after(hidden[0], d_query[1]), w_down_t, 1, 1).astype(BF))
     result = middle + result_near + result_far
 
@@ -853,35 +1107,34 @@
         d_pre[dx] = jnp.concatenate([d_query_pre.reshape(q_cols, -1), d_key_pre, d_value_pre])
     near_part = contract(d_pre[0], w_qkv, 0, 1).astype(BF)
     far_part = contract(d_pre[1], w_qkv, 0, 1).astype(BF)
-    far = send_far(far_part)
-    grad_qkv_part = contract(normed[0], d_pre[0], 0, 1) + contract(
-        normed[1], after(d_pre[1], far_part), 0, 1
-    )
-    ring_qkv = Scatter(grad_qkv_part.astype(BF))
-    ring_qkv.advance(half_ring - per_window)
-    near = reduce_core(near_part)
-    near, far = stage([ring_qkv], (near, far))
-    ring_qkv.advance(half_ring)
+    grad_qkv_part = contract(normed[0], d_pre[0], 0, 1) + contract(normed[1], d_pre[1], 0, 1)
     gain_grad_attn = sum(
         jnp.sum(part.astype(F32) * group_tokens[dx].astype(F32) * scales[dx], axis=0)
         for dx, part in enumerate((near_part, far_part))
     )
-    gain_grads = lax.dynamic_slice_in_dim(
-        sum_small(jnp.stack([gain_grad_attn, gain_grad_mlp])), index * own_rows, own_rows, 1
-    )
-    grad_down = to_owners(ring_down)
-    grad_gate_up = to_owners(ring_gate_up)
-    grad_out = to_owners(ring_out)
-    d_normed = near + far
+    gain_partial = jnp.pad(jnp.stack([gain_grad_attn, gain_grad_mlp], axis=1), ((0, 0), (0, 126)))
+    partial = jnp.concatenate([grad_qkv_part, gain_partial, grad_out_part], axis=1).astype(BF)
+    d_normed, grad_attn, grad_gate_up, grad_down = closing(
+        partial.reshape(wide, 2, deep, 2 * own_rows, -1),
+        near_part,
+        far_part,
+        ring_gate_up.result().astype(BF),
+        ring_down.result().astype(BF),
+        wide,
+        deep,
+    )
+    grad_attn, grad_gate_up, grad_down = (
+        grads.astype(F32) for grads in (grad_attn, grad_gate_up, grad_down)
+    )
+    gain_grads = jnp.sum(grad_attn[:, :, qkv_cols : qkv_cols + 2], axis=0).T
     d_inputs = norm_backward(own_tokens.astype(F32), scales[0][:rows], gain_attn, d_normed) + d_middle
-    grad_qkv = to_owners(ring_qkv)
     return (
         result.astype(BF)[None],
         d_inputs.astype(BF)[None],
-        columns_of(grad_qkv[:, :, :q_cols]),
-        columns_of(grad_qkv[:, :, q_cols : q_cols + HD]),
-        columns_of(grad_qkv[:, :, q_cols + HD :]),
-        columns_of(grad_out).T,
+        columns_of(grad_attn[:, :, :q_cols]),
+        columns_of(grad_attn[:, :, q_cols : q_cols + HD]),
+        columns_of(grad_attn[:, :, q_cols + HD : qkv_cols]),
+        columns_of(grad_attn[:, :, qkv_cols + 128 :]).T,
         columns_of(grad_gate_up[:, :, :hidden_cols]),
         columns_of(grad_gate_up[:, :, hidden_cols:]),
         columns_of(grad_down).T,

time: 890 us -> 854 us (0.960)
  Pallas kernels: 179 us -> 299 us
  waiting for transfers between devices: 242 us -> 139 us
  matrix products: 185 us -> 136 us
  starting transfers between devices: 104 us -> 78.9 us
  local copies, waits for them, and re-layouts: 61.6 us -> 76 us
  other arithmetic: 95.5 us -> 106 us
    pallas_call x0 -> x3, Pallas kernels: none -> 124 us  [the longest x1 76.8 us: closing(): pl.pallas_call(functools.partial(closing_kernel, wide=wide, deep=deep, ow...]
    ppermute x91 -> x55, waiting for transfers between devices: 242 us -> 139 us  [send(): return lax.ppermute(value, AXES, perm)]
    dot_general x22 -> x18, matrix products: 185 us -> 136 us  [contract(): lax.dot_general(left, right, (((left_dim,), (right_dim,)), ((), ())), pre...]
    ppermute x91 -> x55, starting transfers between devices: 104 us -> 78.9 us  [send(): return lax.ppermute(value, AXES, perm)]
    convert_element_type x13 -> x9, other arithmetic: 10.2 us -> 20.2 us  [the longest x1 4.48 us: shards(): branch_own = d_middle.astype(BF)]
    convert_element_type x12 -> x7, other arithmetic: 17.8 us -> 20.9 us  [add_low(): return (one.astype(F32) + other.astype(F32)).astype(BF)]
  transfers between devices with their start and end apart: 91 -> 55, of which waited for: 35 -> 14; matrix products, arithmetic and copies ran while one was open for 30% -> 28% of each run, Pallas kernels for 5% -> 17%
where the time goes in v4:
time: 854 us; the launch traced here: 846 us
  Pallas kernels  299 us (35%)
  waiting for transfers between devices  139 us (16%)
  matrix products  136 us (16%)
  other arithmetic  106 us (12%)
  starting transfers between devices  78.9 us (9%)
  local copies, waits for them, and re-layouts  76 us (9%)
  between operations  11.1 us (1%)
    ppermute x55, waiting for transfers between devices, send(): return lax.ppermute(value, AXES, perm)  139 us
    dot_general x18, matrix products, contract(): lax.dot_general(left, right, (((left_dim,), (right_dim,)), ((), ())), pre...  136 us
    pallas_call x1, Pallas kernels, opening(): pl.pallas_call(functools.partial(opening_kernel, wide=wide, deep=deep, ow...  133 us
    ppermute x55, starting transfers between devices, send(): return lax.ppermute(value, AXES, perm)  78.9 us
    pallas_call x1, Pallas kernels, closing(): pl.pallas_call(functools.partial(closing_kernel, wide=wide, deep=deep, ow...  76.8 us
    pallas_call x2, Pallas kernels, feed_forward(): pl.pallas_call(functools.partial(feed_kernel, columns=columns), grid=(tok...  46.7 us
    pallas_call x2, Pallas kernels, attend_backward(): pl.pallas_call(functools.partial(backward_kernel, rows=rows, heads=heads,...  23.7 us
    convert_element_type x7, other arithmetic, add_low(): return (one.astype(F32) + other.astype(F32)).astype(BF)  20.9 us
  transfers between devices with their start and end apart: 55, of which 14 were waited for; matrix products, arithmetic and copies ran while one was open for 28% of the time, Pallas kernels for 17%

profile of v4, /device:TPU:0, one launch (start us, length us, event | category | flops | bytes accessed | tf_op | source)
XLA Modules:
  0.0 846.2 jit_solution(7336066637835908430)
XLA Ops:
  28.8 132.7 %opening.1 = (bf16[4,384,2048]{2,1,0:T(8,128)(2,1)}, bf16[2,2,4,128,1280]{4,3,2,1,0:T(8,128)(2,1)}, bf16[2,2,4,128,1408]{4,3,2,1,0:T(8,128)(2,1)}, bf16[2,2,4,128,2816]{4,3,2,1,0:T(8,128)(2,1)}) custom-call(bf16[384,2048]{1,0:T(8,128)(2,1)} %bitcast.358, bf16[4,64,1280]{2,1,0:T(8,128)(2,1)} %concatenate.133.quarters_attn, bf16[4,64,1408]{2,1,0:T(8,128)(2,1)} %bitcast.385, ...), custom_call_target="tpu_custom_call" | custom-call | tf_op jit(solution)/shard_map/opening/pallas_call | solution.py:510
  176.0 5.1 fusion.46
  213.5 7.4 collective-permute-start.13
  228.2 9.5 %attend_forward.2 = (bf16[8,64,768]{2,1,0:T(8,128)(2,1)S(1)}, f32[2,1,3072]{2,1,0:T(1,128)S(1)}) custom-call(s32[2,5]{1,0:T(2,128)S(1)} %get-tuple-element.93.meta, bf16[8,64,768]{2,1,0:T(8,128)(2,1)S(1)} %fusion.50.query_ref, bf16[3072,128]{1,0:T(8,128)(2,1)S(1)} %constant_dynamic-update-slice_fusion.keyval_ref, s32[2,1,384]{2,1,0:T(1,128)S(1)} %broadcast_in_dim.68.first_ref), custom_call_target="tpu_custom_call" | custom-call | flops 40000000000 | bytes 10000000 | tf_op jit(solution)/shard_map/attend_forward/pallas_call | solution.py:222
  237.8 20.6 %collective-permute-done.6 = bf16[2,128,2816]{2,1,0:T(8,128)(2,1)} collective-permute-done((bf16[2,128,2816]{2,1,0:T(8,128)(2,1)}, bf16[2,128,2816]{2,1,0:T(8,128)(2,1)}, u32[]{:S(2)}, u32[]{:S(2)}) %collective-permute-start.6) | collective-permute-done | bytes 1441824 | tf_op jit(solution)/shard_map/ppermute | solution.py:802
  278.9 9.5 %attend_forward.3 = (bf16[8,64,768]{2,1,0:T(8,128)(2,1)S(1)}, f32[2,1,3072]{2,1,0:T(1,128)S(1)}) custom-call(s32[2,5]{1,0:T(2,128)S(1)} %get-tuple-element.99.meta, bf16[8,64,768]{2,1,0:T(8,128)(2,1)S(1)} %fusion.51.query_ref, bf16[3072,128]{1,0:T(8,128)(2,1)S(1)} %constant_dynamic-update-slice_fusion.5.keyval_ref, s32[2,1,384]{2,1,0:T(1,128)S(1)} %broadcast_in_dim.67.first_ref), custom_call_target="tpu_custom_call" | custom-call | flops 40000000000 | bytes 10000000 | tf_op jit(solution)/shard_map/attend_forward/pallas_call | solution.py:222
  288.4 24.5 %collective-permute-done.14 = bf16[384,2048]{1,0:T(8,128)(2,1)S(1)} collective-permute-done((bf16[384,2048]{1,0:T(8,128)(2,1)S(1)}, bf16[384,2048]{1,0:T(8,128)(2,1)S(1)}, u32[]{:S(2)}, u32[]{:S(2)}) %collective-permute-start.14) | collective-permute-done | bytes 1572896 | tf_op jit(solution)/shard_map/ppermute | solution.py:802
  328.9 13.1 %collective-permute-done.19 = bf16[1,128,2816]{2,1,0:T(8,128)(2,1)S(1)} collective-permute-done((bf16[1,128,2816]{2,1,0:T(8,128)(2,1)S(1)}, bf16[1,128,2816]{2,1,0:T(8,128)(2,1)S(1)}, u32[]{:S(2)}, u32[]{:S(2)}) %collective-permute-start.19) | collective-permute-done | bytes 720928 | tf_op jit(solution)/shard_map/ppermute | solution.py:802
  347.8 23.5 %feed_forward.2 = (bf16[1536,1408]{1,0:T(8,128)(2,1)}, bf16[1536,2816]{1,0:T(8,128)(2,1)}) custom-call(bf16[768,2048]{1,0:T(8,128)(2,1)} %pad_maximum_fusion.1.normed, bf16[768,2048]{1,0:T(8,128)(2,1)} %pad_maximum_fusion.2.cotangent, bf16[2048,2816]{1,0:T(8,128)(2,1)} %bitcast.404, bf16[2048,1408]{1,0:T(8,128)(2,1)} %bitcast.429), custom_call_target="tpu_custom_call" | custom-call | flops 13287555072 | bytes 17301504 | tf_op jit(solution)/shard_map/feed_forward/pallas_call | solution.py:322
  371.3 7.7 collective-permute-done.16
  391.6 23.2 %feed_forward.3 = (bf16[1536,1408]{1,0:T(8,128)(2,1)}, bf16[1536,2816]{1,0:T(8,128)(2,1)}) custom-call(bf16[768,2048]{1,0:T(8,128)(2,1)} %pad_maximum_fusion.3.normed, bf16[768,2048]{1,0:T(8,128)(2,1)} %pad_maximum_fusion.4.cotangent, bf16[2048,2816]{1,0:T(8,128)(2,1)} %bitcast.405, ...), custom_call_target="tpu_custom_call", output_to_operand_aliasing={{0}: (4, {}), {1}: (5, {})} | custom-call | flops 13287555072 | bytes 17301504 | tf_op jit(solution)/shard_map/feed_forward/pallas_call | solution.py:322
  414.8 13.7 %fusion.26 = bf16[768,2048]{1,0:T(8,128)(2,1)S(1)} fusion(bf16[2048,2816]{1,0:T(8,128)(2,1)} %bitcast.406, bf16[1536,2816]{1,0:T(8,128)(2,1)} %get-tuple-element.121), kind=kOutput, calls=%fused_computation.44 | convolution fusion | flops 8859942912 | bytes 19005440 | tf_op jit(solution)/shard_map/dot_general | solution.py:23
  431.7 12.3 %convolution_convert_fusion.8 = bf16[768,2048]{1,0:T(8,128)(2,1)S(1)} fusion(bf16[768,2816]{1,0:T(8,128)(2,1)S(1)} %slice.342, bf16[2048,2816]{1,0:T(8,128)(2,1)} %bitcast.407), kind=kOutput, calls=%fused_computation.47 | convolution fusion | flops 8859942912 | bytes 19005440 | tf_op jit(solution)/shard_map/dot_general | solution.py:23
  450.6 12.1 %convolution_convert_fusion.1 = bf16[2048,1408]{1,0:T(8,128)(2,1)S(1)} fusion(bf16[1536,1408]{1,0:T(8,128)(2,1)S(1)} %bitcast.380, bf16[384,2048]{1,0:T(8,128)(2,1)} %collective-permute-done.23, bf16[384,2048]{1,0:T(8,128)(2,1)} %collective-permute-done.22, bf16[384,2048]{1,0:T(8,128)(2,1)} %copy-done.35, bf16[384,2048]{1,0:T(8,128)(2,1)S(1)} %bitcast.373), kind=kOutput, calls=%fused_computation.1 | convolution fusion | flops 8886419456 | bytes 16384000 | tf_op jit(solution)/shard_map/dot_general | solution.py:23
  468.2 25.7 %convolution_convert_fusion = bf16[2048,2816]{1,0:T(8,128)(2,1)} fusion(bf16[1536,2816]{1,0:T(8,128)(2,1)} %get-tuple-element.121, bf16[384,2048]{1,0:T(8,128)(2,1)} %collective-permute-done.21, bf16[384,2048]{1,0:T(8,128)(2,1)} %collective-permute-done.16, bf16[384,2048]{1,0:T(8,128)(2,1)} %copy-done.36, bf16[384,2048]{1,0:T(8,128)(2,1)} %copy-done.21), kind=kOutput, calls=%fused_computation | convolution fusion | flops 17747673088 | bytes 26476544 | tf_op jit(solution)/shard_map/dot_general | solution.py:23
  519.4 7.8 collective-permute-done.28
  534.9 12.0 %attend_backward.2 = (bf16[8,64,768]{2,1,0:T(8,128)(2,1)S(1)}, bf16[3072,128]{1,0:T(8,128)(2,1)S(1)}) custom-call(s32[2,5]{1,0:T(2,128)S(1)} %get-tuple-element.99.meta, bf16[8,64,768]{2,1,0:T(8,128)(2,1)S(1)} %fusion.51.query_ref, bf16[3072,128]{1,0:T(8,128)(2,1)S(1)} %constant_dynamic-update-slice_fusion.5.keyval_ref, ...), custom_call_target="tpu_custom_call" | custom-call | flops 80000000000 | bytes 16000000 | tf_op jit(solution)/shard_map/attend_backward/pallas_call | solution.py:256
  547.0 27.0 %collective-permute-done.33 = bf16[2,128,2816]{2,1,0:T(8,128)(2,1)S(1)} collective-permute-done((bf16[2,128,2816]{2,1,0:T(8,128)(2,1)}, bf16[2,128,2816]{2,1,0:T(8,128)(2,1)S(1)}, u32[]{:S(2)}, u32[]{:S(2)}) %collective-permute-start.33) | collective-permute-done | bytes 1441824 | tf_op jit(solution)/shard_map/ppermute | solution.py:802
  575.5 7.9 convolution_convert_fusion.7
  600.1 6.3 collective-permute-done.44
  618.7 11.7 %attend_backward.3 = (bf16[8,64,768]{2,1,0:T(8,128)(2,1)S(1)}, bf16[3072,128]{1,0:T(8,128)(2,1)S(1)}) custom-call(s32[2,5]{1,0:T(2,128)S(1)} %get-tuple-element.93.meta, bf16[8,64,768]{2,1,0:T(8,128)(2,1)S(1)} %copy-done.1, bf16[3072,128]{1,0:T(8,128)(2,1)S(1)} %copy-done.3, s32[2,1,384]{2,1,0:T(1,128)S(1)} %broadcast_in_dim.68.first_ref, ...), custom_call_target="tpu_custom_call" | custom-call | flops 80000000000 | bytes 16000000 | tf_op jit(solution)/shard_map/attend_backward/pallas_call | solution.py:256
  630.5 16.4 %collective-permute-done.46 = bf16[384,2048]{1,0:T(8,128)(2,1)S(1)} collective-permute-done((bf16[384,2048]{1,0:T(8,128)(2,1)}, bf16[384,2048]{1,0:T(8,128)(2,1)S(1)}, u32[]{:S(2)}, u32[]{:S(2)}) %collective-permute-start.46) | collective-permute-done | bytes 1572896 | tf_op jit(solution)/shard_map/ppermute | solution.py:802
  648.9 6.3 collective-permute-done.38
  658.3 7.2 fusion.67
  665.5 5.8 convolution_convert_fusion.5.near_part
  683.2 5.3 convolution_convert_fusion.6
  688.6 5.6 fusion.36
  700.0 9.9 %collective-permute-start.51 = (bf16[2,128,2816]{2,1,0:T(8,128)(2,1)}, bf16[2,128,2816]{2,1,0:T(8,128)(2,1)}, u32[]{:S(2)}, u32[]{:S(2)}) collective-permute-start(bf16[2,128,2816]{2,1,0:T(8,128)(2,1)} %get-tuple-element.176), channel_id=1, source_target_pairs={{0,2},{1,3},{2,4},{3,5},{4,6},{5,7},{6,22},{7,23},{8,10},{9,11},{1... | collective-permute-start | bytes 4325384 | tf_op jit(solution)/shard_map/ppermute | solution.py:802
  718.9 8.1 add_convert_fusion
  727.1 7.7 fusion.23
  735.2 5.2 pad_maximum_fusion.partial
  747.2 76.8 %closing.1 = (f32[384,2048]{1,0:T(8,128)}, bf16[4,64,1280]{2,1,0:T(8,128)(2,1)}, bf16[4,64,2816]{2,1,0:T(8,128)(2,1)}, bf16[4,64,1408]{2,1,0:T(8,128)(2,1)}) custom-call(bf16[2,2,4,128,1280]{4,3,2,1,0:T(8,128)(2,1)} %pad_maximum_fusion.partial, bf16[768,2048]{1,0:T(8,128)(2,1)} %convolution_convert_fusion.5.near_part, ...), custom_call_target="tpu_custom_call" | custom-call | tf_op jit(solution)/shard_map/closing/pallas_call | solution.py:711
  (476 shorter events, 267.4 us)
Async XLA Ops:
  164.1 60.2 %collective-permute-start.1 = (bf16[2,128,2816]{2,1,0:T(8,128)(2,1)}, bf16[2,128,2816]{2,1,0:T(8,128)(2,1)}, u32[]{:S(2)}, u32[]{:S(2)}) collective-permute-start(bf16[2,128,2816]{2,1,0:T(8,128)(2,1)} %dynamic-slice_bitcast_fusion), channel_id=1, source_target_pairs={{0,2},{1,3},{2,4},{3,5},{4,6},{5,7},{6,22},{7,23},{8,10},{9,11},{1... | collective-permute-start | bytes 4325384 | tf_op jit(solution)/shard_map/ppermute | solution.py:802
  165.1 59.2 %collective-permute-start.2 = (bf16[2,128,2816]{2,1,0:T(8,128)(2,1)}, bf16[2,128,2816]{2,1,0:T(8,128)(2,1)}, u32[]{:S(2)}, u32[]{:S(2)}) collective-permute-start(bf16[2,128,2816]{2,1,0:T(8,128)(2,1)} %dynamic-slice_bitcast_fusion), channel_id=1, source_target_pairs={{0,16},{1,17},{2,0},{3,1},{4,2},{5,3},{6,4},{7,5},{8,24},{9,25},{1... | collective-permute-start | bytes 4325384 | tf_op jit(solution)/shard_map/ppermute | solution.py:802
  221.9 48.2 %collective-permute-start.18 = (bf16[384,2048]{1,0:T(8,128)(2,1)S(1)}, bf16[384,2048]{1,0:T(8,128)(2,1)S(1)}, u32[]{:S(2)}, u32[]{:S(2)}) collective-permute-start(bf16[384,2048]{1,0:T(8,128)(2,1)S(1)} %bitcast.370), channel_id=1, source_target_pairs={{0,1},{1,0},{2,3},{3,2},{4,5},{5,4},{6,7},{7,6},{8,9},{9,8},{10,11... | collective-permute-start | bytes 4718600 | tf_op jit(solution)/shard_map/ppermute | solution.py:802
  222.1 47.5 %collective-permute-start.22 = (bf16[384,2048]{1,0:T(8,128)(2,1)S(1)}, bf16[384,2048]{1,0:T(8,128)(2,1)}, u32[]{:S(2)}, u32[]{:S(2)}) collective-permute-start(bf16[384,2048]{1,0:T(8,128)(2,1)S(1)} %bitcast.371), channel_id=1, source_target_pairs={{0,8},{1,9},{2,10},{3,11},{4,12},{5,13},{6,14},{7,15},{8,0},{9,1},... | collective-permute-start | bytes 4718600 | tf_op jit(solution)/shard_map/ppermute | solution.py:802
  224.3 34.1 %collective-permute-start.6 = (bf16[2,128,2816]{2,1,0:T(8,128)(2,1)}, bf16[2,128,2816]{2,1,0:T(8,128)(2,1)}, u32[]{:S(2)}, u32[]{:S(2)}) collective-permute-start(bf16[2,128,2816]{2,1,0:T(8,128)(2,1)} %collective-permute-done.1), channel_id=1, source_target_pairs={{0,2},{1,3},{2,4},{3,5},{4,6},{5,7},{6,22},{7,23},{8,10},{9,11},{1... | collective-permute-start | bytes 4325384 | tf_op jit(solution)/shard_map/ppermute | solution.py:802
  228.0 32.8 %collective-permute-start.7 = (bf16[2,128,2816]{2,1,0:T(8,128)(2,1)}, bf16[2,128,2816]{2,1,0:T(8,128)(2,1)}, u32[]{:S(2)}, u32[]{:S(2)}) collective-permute-start(bf16[2,128,2816]{2,1,0:T(8,128)(2,1)} %collective-permute-done.2), channel_id=1, source_target_pairs={{0,16},{1,17},{2,0},{3,1},{4,2},{5,3},{6,4},{7,5},{8,24},{9,25},{1... | collective-permute-start | bytes 4325384 | tf_op jit(solution)/shard_map/ppermute | solution.py:802
  269.6 114.0 %collective-permute-start.23 = (bf16[384,2048]{1,0:T(8,128)(2,1)}, bf16[384,2048]{1,0:T(8,128)(2,1)}, u32[]{:S(2)}, u32[]{:S(2)}) collective-permute-start(bf16[384,2048]{1,0:T(8,128)(2,1)} %collective-permute-done.22), channel_id=1, source_target_pairs={{0,1},{1,0},{2,3},{3,2},{4,5},{5,4},{6,7},{7,6},{8,9},{9,8},{10,11... | collective-permute-start | bytes 4718600 | tf_op jit(solution)/shard_map/ppermute | solution.py:802
  272.2 41.1 %collective-permute-start.8 = (bf16[2,128,2816]{2,1,0:T(8,128)(2,1)}, bf16[2,128,2816]{2,1,0:T(8,128)(2,1)S(1)}, u32[]{:S(2)}, u32[]{:S(2)}) collective-permute-start(bf16[2,128,2816]{2,1,0:T(8,128)(2,1)} %collective-permute-done.6), channel_id=1, source_target_pairs={{0,2},{1,3},{2,4},{3,5},{4,6},{5,7},{6,22},{7,23},{8,10},{9,11},{1... | collective-permute-start | bytes 4325384 | tf_op jit(solution)/shard_map/ppermute | solution.py:802
  273.9 39.4 %collective-permute-start.9 = (bf16[2,128,2816]{2,1,0:T(8,128)(2,1)}, bf16[2,128,2816]{2,1,0:T(8,128)(2,1)S(1)}, u32[]{:S(2)}, u32[]{:S(2)}) collective-permute-start(bf16[2,128,2816]{2,1,0:T(8,128)(2,1)} %collective-permute-done.7), channel_id=1, source_target_pairs={{0,16},{1,17},{2,0},{3,1},{4,2},{5,3},{6,4},{7,5},{8,24},{9,25},{1... | collective-permute-start | bytes 4325384 | tf_op jit(solution)/shard_map/ppermute | solution.py:802
  275.3 37.6 %collective-permute-start.14 = (bf16[384,2048]{1,0:T(8,128)(2,1)S(1)}, bf16[384,2048]{1,0:T(8,128)(2,1)S(1)}, u32[]{:S(2)}, u32[]{:S(2)}) collective-permute-start(bf16[384,2048]{1,0:T(8,128)(2,1)S(1)} %add_convert_fusion.5), channel_id=1, source_target_pairs={{0,8},{1,9},{2,10},{3,11},{4,12},{5,13},{6,14},{7,15},{8,0},{9,1},... | collective-permute-start | bytes 4718600 | tf_op jit(solution)/shard_map/ppermute | solution.py:802
  342.9 36.1 %collective-permute-start.16 = (bf16[384,2048]{1,0:T(8,128)(2,1)S(1)}, bf16[384,2048]{1,0:T(8,128)(2,1)}, u32[]{:S(2)}, u32[]{:S(2)}) collective-permute-start(bf16[384,2048]{1,0:T(8,128)(2,1)S(1)} %multiply_convert_fusion), channel_id=1, source_target_pairs={{0,8},{1,9},{2,10},{3,11},{4,12},{5,13},{6,14},{7,15},{8,0},{9,1},... | collective-permute-start | bytes 4718600 | tf_op jit(solution)/shard_map/ppermute | solution.py:802
  445.4 48.5 %collective-permute-start.30 = (bf16[384,2048]{1,0:T(8,128)(2,1)}, bf16[384,2048]{1,0:T(8,128)(2,1)}, u32[]{:S(2)}, u32[]{:S(2)}) collective-permute-start(bf16[384,2048]{1,0:T(8,128)(2,1)} %slice.430), channel_id=1, source_target_pairs={{0,1},{1,0},{2,3},{3,2},{4,5},{5,4},{6,7},{7,6},{8,9},{9,8},{10,11... | collective-permute-start | bytes 4718600 | tf_op jit(solution)/shard_map/ppermute | solution.py:802
  448.9 45.0 %collective-permute-start.27 = (bf16[384,2048]{1,0:T(8,128)(2,1)}, bf16[384,2048]{1,0:T(8,128)(2,1)}, u32[]{:S(2)}, u32[]{:S(2)}) collective-permute-start(bf16[384,2048]{1,0:T(8,128)(2,1)} %add_convert_fusion.4), channel_id=1, source_target_pairs={{0,8},{1,9},{2,10},{3,11},{4,12},{5,13},{6,14},{7,15},{8,0},{9,1},... | collective-permute-start | bytes 4718600 | tf_op jit(solution)/shard_map/ppermute | solution.py:802
  466.0 27.9 %collective-permute-start.25 = (bf16[1,128,1408]{2,1,0:T(8,128)(2,1)}, bf16[1,128,1408]{2,1,0:T(8,128)(2,1)}, u32[]{:S(2)}, u32[]{:S(2)}) collective-permute-start(bf16[1,128,1408]{2,1,0:T(8,128)(2,1)} %get-tuple-element.193), channel_id=1, source_target_pairs={{0,2},{1,3},{2,4},{3,5},{4,6},{5,7},{6,22},{7,23},{8,10},{9,11},{1... | collective-permute-start | bytes 1081352 | tf_op jit(solution)/shard_map/ppermute | solution.py:802
  467.7 26.2 %collective-permute-start.26 = (bf16[1,128,1408]{2,1,0:T(8,128)(2,1)S(1)}, bf16[1,128,1408]{2,1,0:T(8,128)(2,1)}, u32[]{:S(2)}, u32[]{:S(2)}) collective-permute-start(bf16[1,128,1408]{2,1,0:T(8,128)(2,1)S(1)} %get-tuple-element.192), channel_id=1, source_target_pairs={{0,16},{1,17},{2,0},{3,1},{4,2},{5,3},{6,4},{7,5},{8,24},{9,25},{1... | collective-permute-start | bytes 1081352 | tf_op jit(solution)/shard_map/ppermute | solution.py:802
  505.9 41.1 %collective-permute-start.36 = (bf16[384,2048]{1,0:T(8,128)(2,1)S(1)}, bf16[384,2048]{1,0:T(8,128)(2,1)S(1)}, u32[]{:S(2)}, u32[]{:S(2)}) collective-permute-start(bf16[384,2048]{1,0:T(8,128)(2,1)S(1)} %get-tuple-element.172), channel_id=1, source_target_pairs={{0,8},{1,9},{2,10},{3,11},{4,12},{5,13},{6,14},{7,15},{8,0},{9,1},... | collective-permute-start | bytes 4718600 | tf_op jit(solution)/shard_map/ppermute | solution.py:802
  512.7 34.2 %collective-permute-start.35 = (bf16[2,128,1408]{2,1,0:T(8,128)(2,1)}, bf16[2,128,1408]{2,1,0:T(8,128)(2,1)}, u32[]{:S(2)}, u32[]{:S(2)}) collective-permute-start(bf16[2,128,1408]{2,1,0:T(8,128)(2,1)} %pad_maximum_fusion.18), channel_id=1, source_target_pairs={{0,16},{1,17},{2,0},{3,1},{4,2},{5,3},{6,4},{7,5},{8,24},{9,25},{1... | collective-permute-start | bytes 2162696 | tf_op jit(solution)/shard_map/ppermute | solution.py:802
  515.4 31.6 %collective-permute-start.34 = (bf16[2,128,1408]{2,1,0:T(8,128)(2,1)S(1)}, bf16[2,128,1408]{2,1,0:T(8,128)(2,1)S(1)}, u32[]{:S(2)}, u32[]{:S(2)}) collective-permute-start(bf16[2,128,1408]{2,1,0:T(8,128)(2,1)S(1)} %pad_maximum_fusion.17), channel_id=1, source_target_pairs={{0,2},{1,3},{2,4},{3,5},{4,6},{5,7},{6,22},{7,23},{8,10},{9,11},{1... | collective-permute-start | bytes 2162696 | tf_op jit(solution)/shard_map/ppermute | solution.py:802
  531.7 42.3 %collective-permute-start.33 = (bf16[2,128,2816]{2,1,0:T(8,128)(2,1)}, bf16[2,128,2816]{2,1,0:T(8,128)(2,1)S(1)}, u32[]{:S(2)}, u32[]{:S(2)}) collective-permute-start(bf16[2,128,2816]{2,1,0:T(8,128)(2,1)} %pad_maximum_fusion.10), channel_id=1, source_target_pairs={{0,16},{1,17},{2,0},{3,1},{4,2},{5,3},{6,4},{7,5},{8,24},{9,25},{1... | collective-permute-start | bytes 4325384 | tf_op jit(solution)/shard_map/ppermute | solution.py:802
  533.4 40.6 %collective-permute-start.32 = (bf16[2,128,2816]{2,1,0:T(8,128)(2,1)}, bf16[2,128,2816]{2,1,0:T(8,128)(2,1)S(1)}, u32[]{:S(2)}, u32[]{:S(2)}) collective-permute-start(bf16[2,128,2816]{2,1,0:T(8,128)(2,1)} %pad_maximum_fusion.9), channel_id=1, source_target_pairs={{0,2},{1,3},{2,4},{3,5},{4,6},{5,7},{6,22},{7,23},{8,10},{9,11},{1... | collective-permute-start | bytes 4325384 | tf_op jit(solution)/shard_map/ppermute | solution.py:802
  598.4 50.5 %collective-permute-start.39 = (bf16[2,128,1408]{2,1,0:T(8,128)(2,1)}, bf16[2,128,1408]{2,1,0:T(8,128)(2,1)}, u32[]{:S(2)}, u32[]{:S(2)}) collective-permute-start(bf16[2,128,1408]{2,1,0:T(8,128)(2,1)} %get-tuple-element.189), channel_id=1, source_target_pairs={{0,2},{1,3},{2,4},{3,5},{4,6},{5,7},{6,22},{7,23},{8,10},{9,11},{1... | collective-permute-start | bytes 2162696 | tf_op jit(solution)/shard_map/ppermute | solution.py:802
  606.3 42.5 %collective-permute-start.40 = (bf16[2,128,1408]{2,1,0:T(8,128)(2,1)}, bf16[2,128,1408]{2,1,0:T(8,128)(2,1)}, u32[]{:S(2)}, u32[]{:S(2)}) collective-permute-start(bf16[2,128,1408]{2,1,0:T(8,128)(2,1)} %get-tuple-element.188), channel_id=1, source_target_pairs={{0,16},{1,17},{2,0},{3,1},{4,2},{5,3},{6,4},{7,5},{8,24},{9,25},{1... | collective-permute-start | bytes 2162696 | tf_op jit(solution)/shard_map/ppermute | solution.py:802
  608.1 47.1 %collective-permute-start.38 = (bf16[2,128,2816]{2,1,0:T(8,128)(2,1)}, bf16[2,128,2816]{2,1,0:T(8,128)(2,1)}, u32[]{:S(2)}, u32[]{:S(2)}) collective-permute-start(bf16[2,128,2816]{2,1,0:T(8,128)(2,1)} %fusion.39), channel_id=1, source_target_pairs={{0,16},{1,17},{2,0},{3,1},{4,2},{5,3},{6,4},{7,5},{8,24},{9,25},{1... | collective-permute-start | bytes 4325384 | tf_op jit(solution)/shard_map/ppermute | solution.py:802
  608.3 46.9 %collective-permute-start.37 = (bf16[2,128,2816]{2,1,0:T(8,128)(2,1)}, bf16[2,128,2816]{2,1,0:T(8,128)(2,1)}, u32[]{:S(2)}, u32[]{:S(2)}) collective-permute-start(bf16[2,128,2816]{2,1,0:T(8,128)(2,1)} %fusion.40), channel_id=1, source_target_pairs={{0,2},{1,3},{2,4},{3,5},{4,6},{5,7},{6,22},{7,23},{8,10},{9,11},{1... | collective-permute-start | bytes 4325384 | tf_op jit(solution)/shard_map/ppermute | solution.py:802
  612.2 34.6 %collective-permute-start.46 = (bf16[384,2048]{1,0:T(8,128)(2,1)}, bf16[384,2048]{1,0:T(8,128)(2,1)S(1)}, u32[]{:S(2)}, u32[]{:S(2)}) collective-permute-start(bf16[384,2048]{1,0:T(8,128)(2,1)} %add_convert_fusion.3), channel_id=1, source_target_pairs={{0,8},{1,9},{2,10},{3,11},{4,12},{5,13},{6,14},{7,15},{8,0},{9,1},... | collective-permute-start | bytes 4718600 | tf_op jit(solution)/shard_map/ppermute | solution.py:802
  674.9 65.6 %collective-permute-start.53 = (bf16[2,128,1408]{2,1,0:T(8,128)(2,1)}, bf16[2,128,1408]{2,1,0:T(8,128)(2,1)}, u32[]{:S(2)}, u32[]{:S(2)}) collective-permute-start(bf16[2,128,1408]{2,1,0:T(8,128)(2,1)} %get-tuple-element.186), channel_id=1, source_target_pairs={{0,2},{1,3},{2,4},{3,5},{4,6},{5,7},{6,22},{7,23},{8,10},{9,11},{1... | collective-permute-start | bytes 2162696 | tf_op jit(solution)/shard_map/ppermute | solution.py:802
  674.9 65.6 %collective-permute-start.54 = (bf16[2,128,1408]{2,1,0:T(8,128)(2,1)}, bf16[2,128,1408]{2,1,0:T(8,128)(2,1)}, u32[]{:S(2)}, u32[]{:S(2)}) collective-permute-start(bf16[2,128,1408]{2,1,0:T(8,128)(2,1)} %get-tuple-element.187), channel_id=1, source_target_pairs={{0,16},{1,17},{2,0},{3,1},{4,2},{5,3},{6,4},{7,5},{8,24},{9,25},{1... | collective-permute-start | bytes 2162696 | tf_op jit(solution)/shard_map/ppermute | solution.py:802
  678.2 35.1 %collective-permute-start.49 = (bf16[768,128]{1,0:T(8,128)(2,1)S(1)}, bf16[768,128]{1,0:T(8,128)(2,1)S(1)}, u32[]{:S(2)}, u32[]{:S(2)}) collective-permute-start(bf16[768,128]{1,0:T(8,128)(2,1)S(1)} %get-tuple-element.224), channel_id=1, source_target_pairs={{4,0},{5,1},{6,2},{7,3},{12,8},{13,9},{14,10},{15,11},{20,16},{21,... | collective-permute-start | bytes 589832 | tf_op jit(solution)/shard_map/ppermute | solution.py:802
  679.5 33.8 %collective-permute-start.50 = (bf16[768,128]{1,0:T(8,128)(2,1)S(1)}, bf16[768,128]{1,0:T(8,128)(2,1)S(1)}, u32[]{:S(2)}, u32[]{:S(2)}) collective-permute-start(bf16[768,128]{1,0:T(8,128)(2,1)S(1)} %get-tuple-element.223), channel_id=1, source_target_pairs={{6,0},{7,1},{14,8},{15,9},{22,16},{23,17},{30,24},{31,25}} | collective-permute-start | bytes 589832 | tf_op jit(solution)/shard_map/ppermute | solution.py:802
  700.0 43.1 %collective-permute-start.51 = (bf16[2,128,2816]{2,1,0:T(8,128)(2,1)}, bf16[2,128,2816]{2,1,0:T(8,128)(2,1)}, u32[]{:S(2)}, u32[]{:S(2)}) collective-permute-start(bf16[2,128,2816]{2,1,0:T(8,128)(2,1)} %get-tuple-element.176), channel_id=1, source_target_pairs={{0,2},{1,3},{2,4},{3,5},{4,6},{5,7},{6,22},{7,23},{8,10},{9,11},{1... | collective-permute-start | bytes 4325384 | tf_op jit(solution)/shard_map/ppermute | solution.py:802
  713.3 30.1 %collective-permute-start.52 = (bf16[2,128,2816]{2,1,0:T(8,128)(2,1)S(1)}, bf16[2,128,2816]{2,1,0:T(8,128)(2,1)}, u32[]{:S(2)}, u32[]{:S(2)}) collective-permute-start(bf16[2,128,2816]{2,1,0:T(8,128)(2,1)S(1)} %get-tuple-element.177), channel_id=1, source_target_pairs={{0,16},{1,17},{2,0},{3,1},{4,2},{5,3},{6,4},{7,5},{8,24},{9,25},{1... | collective-permute-start | bytes 4325384 | tf_op jit(solution)/shard_map/ppermute | solution.py:802
  713.3 127.6 %collective-permute-start.47 = (bf16[384,2048]{1,0:T(8,128)(2,1)}, bf16[384,2048]{1,0:T(8,128)(2,1)}, u32[]{:S(2)}, u32[]{:S(2)}) collective-permute-start(bf16[384,2048]{1,0:T(8,128)(2,1)} %slice.436), channel_id=1, source_target_pairs={{0,1},{1,0},{2,3},{3,2},{4,5},{5,4},{6,7},{7,6},{8,9},{9,8},{10,11... | collective-permute-start | bytes 4718600 | tf_op jit(solution)/shard_map/ppermute | solution.py:802
  (109 other events, 1912.1 us)

commit v5 on v4

--- a/solution.py
+++ b/solution.py
@@ -220,7 +220,7 @@
     specs = attention_specs(rows, heads, keys)
     wide = heads * rows
     return pl.pallas_call(
-        functools.partial(forward_kernel, rows=rows, heads=heads, pair=2),
+        functools.partial(forward_kernel, rows=rows, heads=heads, pair=4),
         grid_spec=pltpu.PrefetchScalarGridSpec(
             num_scalar_prefetch=1,
             grid=(2,),
@@ -254,7 +254,7 @@
     specs = attention_specs(rows, heads, keys)
     wide = heads * rows
     return pl.pallas_call(
-        functools.partial(backward_kernel, rows=rows, heads=heads, pair=2),
+        functools.partial(backward_kernel, rows=rows, heads=heads, pair=4),
         grid_spec=pltpu.PrefetchScalarGridSpec(
             num_scalar_prefetch=1,
             grid=(2,),
@@ -306,25 +306,27 @@
         d_gate_up[:, columns + low : columns + high] = (d_hidden * silu).astype(BF)
 
 
-def feed_forward(normed, cotangent, w_gate_up, w_down_t, half, before=()):
-    tokens, width = normed.shape
+def feed_forward(normed, cotangent, w_gate_up, w_down_t, halves, before=()):
+    tokens, width = cotangent.shape[0] // 2, cotangent.shape[1]
     columns = w_down_t.shape[1]
     tile = min(256, tokens)
-    shift = half * (tokens // tile)
-    token_spec = pl.BlockSpec((tile, width), lambda i: (i, 0))
+    shifts = [half * (tokens // tile) for half in halves]
+
+    def token_spec(shift):
+        return pl.BlockSpec((tile, width), lambda i: (i + shift, 0))
 
     def weight_spec(wide):
         return pl.BlockSpec((width, wide), lambda i: (0, 0), pipeline_mode=pl.Buffered(1))
 
     def out_spec(wide):
-        return pl.BlockSpec((tile, wide), lambda i: (i + shift, 0))
+        return pl.BlockSpec((tile, wide), lambda i: (i + shifts[2], 0))
 
     return pl.pallas_call(
         functools.partial(feed_kernel, columns=columns),
         grid=(tokens // tile,),
         in_specs=[
-            token_spec,
-            token_spec,
+            token_spec(shifts[0]),
+            token_spec(shifts[1]),
             weight_spec(2 * columns),
             weight_spec(columns),
             *[pl.BlockSpec(memory_space=pl.ANY) for _ in before],
@@ -986,7 +988,11 @@
             member.advance(times)
 
     advance(rings)
-    group_cotangent = gather_group(after(cotangent[0], group_blocks))
+    own_cotangent = after(cotangent[0], group_blocks)
+    far_cotangent = send(own_cotangent, x_perm)
+    both_cotangent = jnp.concatenate(
+        [own_cotangent, send(own_cotangent, core_perm), far_cotangent, send(far_cotangent, core_perm)]
+    )
 
     heads = HEADS // GROUP
     normed, scales, queries, keyvals, attended, lses = ([None, None] for _ in range(6))
@@ -1020,17 +1026,18 @@
     scale_mlp = lax.rsqrt(jnp.mean(middle * middle, axis=1, keepdims=True) + EPSILON)
     normed_own = (middle * scale_mlp * gain_mlp).astype(BF)
     normed_far = send(normed_own, x_perm)
-    normed_mlp = [with_core(normed_own), None]
+    normed_near = [normed_own, send(normed_own, core_perm)]
     w_gate_up = ring_gate_up.whole()
-    both = feed_forward(normed_mlp[0], group_cotangent[0], w_gate_up, w_down_t, 0)
+    normed_near, both_cotangent = stage([], (normed_near, both_cotangent))
+    both = feed_forward(
+        jnp.concatenate(normed_near), both_cotangent, w_gate_up, w_down_t, (0, 0, 0)
+    )
     normed_far, both = stage([], (normed_far, both))
-    normed_mlp[1] = with_core(normed_far)
-    both = feed_forward(normed_mlp[1], group_cotangent[1], w_gate_up, w_down_t, 1, both)
+    both_normed = jnp.concatenate([*normed_near, normed_far, send(normed_far, core_perm)])
+    both = feed_forward(both_normed, both_cotangent, w_gate_up, w_down_t, (1, 1, 1), both)
     both_hidden, both_d_gate_up = both
     hidden = [both_hidden[: 2 * rows], both_hidden[2 * rows :]]
     d_gate_up = [both_d_gate_up[: 2 * rows], both_d_gate_up[2 * rows :]]
-    both_cotangent = jnp.concatenate(group_cotangent)
-    both_normed = jnp.concatenate(normed_mlp)
     far_part = contract(d_gate_up[1], w_gate_up, 1, 1).astype(BF)
     far_sum = reduce_core(far_part).astype(BF)
     far = send(far_sum, x_perm)
@@ -1067,8 +1074,9 @@
     def keyval_home(d_keyvals):
         chunks = [d_keyvals[2 * rows * i : 2 * rows * (i + 1)] for i in range(deep)]
         total = chunks[deep - 1].astype(F32)
-        for step in range(1, deep):
-            total = total + send(chunks[deep - 1 - step], perm_of(along(-step))).astype(F32)
+        came = [send(chunks[deep - 1 - step], perm_of(along(-step))) for step in range(1, deep)]
+        for part in came:
+            total = total + part.astype(F32)
         return jnp.concatenate(swap_pair(c_at, [total[:rows], total[rows:]])).T
 
     d_near = stage([ring_gate_up], d_attended(0))

time: 854 us -> 842 us (0.986)
  other arithmetic: 106 us -> 91.5 us
    ppermute x55, waiting for transfers between devices: 139 us -> 147 us  [send(): return lax.ppermute(value, AXES, perm)]
    unnamed x188 -> x207, local copies, waits for them, and re-layouts: 13 us -> 19.1 us
  transfers between devices with their start and end apart: 55 -> 55, of which waited for: 14 -> 13; matrix products, arithmetic and copies ran while one was open for 28% -> 28% of each run, Pallas kernels for 17% -> 17%
where the time goes in v5:
time: 842 us; the launch traced here: 833 us
  Pallas kernels  294 us (35%)
  waiting for transfers between devices  147 us (17%)
  matrix products  133 us (16%)
  other arithmetic  91.5 us (11%)
  local copies, waits for them, and re-layouts  79.8 us (9%)
  starting transfers between devices  75.8 us (9%)
  between operations  11.2 us (1%)
    ppermute x55, waiting for transfers between devices, send(): return lax.ppermute(value, AXES, perm)  147 us
    dot_general x18, matrix products, contract(): lax.dot_general(left, right, (((left_dim,), (right_dim,)), ((), ())), pre...  133 us
    pallas_call x1, Pallas kernels, opening(): pl.pallas_call(functools.partial(opening_kernel, wide=wide, deep=deep, ow...  133 us
    pallas_call x1, Pallas kernels, closing(): pl.pallas_call(functools.partial(closing_kernel, wide=wide, deep=deep, ow...  77.2 us
    ppermute x55, starting transfers between devices, send(): return lax.ppermute(value, AXES, perm)  75.8 us
    pallas_call x2, Pallas kernels, feed_forward(): pl.pallas_call(functools.partial(feed_kernel, columns=columns), grid=(tok...  46.9 us
    pallas_call x2, Pallas kernels, attend_backward(): pl.pallas_call(functools.partial(backward_kernel, rows=rows, heads=heads,...  22.6 us
    convert_element_type x7, other arithmetic, add_low(): return (one.astype(F32) + other.astype(F32)).astype(BF)  19.4 us
  transfers between devices with their start and end apart: 55, of which 13 were waited for; matrix products, arithmetic and copies ran while one was open for 28% of the time, Pallas kernels for 17%

profile of v5, /device:TPU:0, one launch (start us, length us, event | category | flops | bytes accessed | tf_op | source)
XLA Modules:
  0.0 833.3 jit_solution(9916809214468742467)
XLA Ops:
  29.0 132.7 %opening.1 = (bf16[4,384,2048]{2,1,0:T(8,128)(2,1)}, bf16[2,2,4,128,1280]{4,3,2,1,0:T(8,128)(2,1)}, bf16[2,2,4,128,1408]{4,3,2,1,0:T(8,128)(2,1)}, bf16[2,2,4,128,2816]{4,3,2,1,0:T(8,128)(2,1)}) custom-call(bf16[384,2048]{1,0:T(8,128)(2,1)} %bitcast.360, bf16[4,64,1280]{2,1,0:T(8,128)(2,1)} %concatenate.122.quarters_attn, bf16[4,64,1408]{2,1,0:T(8,128)(2,1)} %bitcast.386, ...), custom_call_target="tpu_custom_call" | custom-call | tf_op jit(solution)/shard_map/opening/pallas_call | solution.py:512
  176.1 5.1 fusion.32
  213.7 7.4 collective-permute-start.13
  228.2 7.4 attend_forward.2
  235.6 23.1 %collective-permute-done.6 = bf16[2,128,2816]{2,1,0:T(8,128)(2,1)S(1)} collective-permute-done((bf16[2,128,2816]{2,1,0:T(8,128)(2,1)}, bf16[2,128,2816]{2,1,0:T(8,128)(2,1)S(1)}, u32[]{:S(2)}, u32[]{:S(2)}) %collective-permute-start.6) | collective-permute-done | bytes 1441824 | tf_op jit(solution)/shard_map/ppermute | solution.py:804
  279.8 7.4 attend_forward.3
  287.2 26.9 %collective-permute-done.14 = bf16[384,2048]{1,0:T(8,128)(2,1)S(1)} collective-permute-done((bf16[384,2048]{1,0:T(8,128)(2,1)}, bf16[384,2048]{1,0:T(8,128)(2,1)S(1)}, u32[]{:S(2)}, u32[]{:S(2)}) %collective-permute-start.14) | collective-permute-done | bytes 1572896 | tf_op jit(solution)/shard_map/ppermute | solution.py:804
  331.2 13.1 %collective-permute-done.21 = bf16[1,128,2816]{2,1,0:T(8,128)(2,1)S(1)} collective-permute-done((bf16[1,128,2816]{2,1,0:T(8,128)(2,1)S(1)}, bf16[1,128,2816]{2,1,0:T(8,128)(2,1)S(1)}, u32[]{:S(2)}, u32[]{:S(2)}) %collective-permute-start.21) | collective-permute-done | bytes 720928 | tf_op jit(solution)/shard_map/ppermute | solution.py:804
  350.0 23.7 %feed_forward.2 = (bf16[1536,1408]{1,0:T(8,128)(2,1)}, bf16[1536,2816]{1,0:T(8,128)(2,1)}) custom-call(bf16[768,2048]{1,0:T(8,128)(2,1)} %pad_maximum_fusion.2.normed, bf16[1536,2048]{1,0:T(8,128)(2,1)} %pad_maximum_fusion.cotangent, bf16[2048,2816]{1,0:T(8,128)(2,1)} %bitcast.405, bf16[2048,1408]{1,0:T(8,128)(2,1)} %bitcast.430), custom_call_target="tpu_custom_call" | custom-call | flops 13287555072 | bytes 17301504 | tf_op jit(solution)/shard_map/feed_forward/pallas_call | solution.py:324
  373.7 7.6 collective-permute-done.20
  392.1 23.3 %feed_forward.3 = (bf16[1536,1408]{1,0:T(8,128)(2,1)}, bf16[1536,2816]{1,0:T(8,128)(2,1)}) custom-call(bf16[1536,2048]{1,0:T(8,128)(2,1)} %constant_dynamic-update-slice_fusion.10.normed, bf16[1536,2048]{1,0:T(8,128)(2,1)} %pad_maximum_fusion.cotangent, bf16[2048,2816]{1,0:T(8,128)(2,1)} %bitcast.406, ...), custom_call_target="tpu_custom_call", output_to_operand_aliasing={{0}: (4, {}), {1}: (5, {})} | custom-call | flops 13287555072 | bytes 17301504 | tf_op jit(solution)/shard_map/feed_forward/pallas_call | solution.py:324
  415.3 13.4 %fusion.12 = bf16[768,2048]{1,0:T(8,128)(2,1)S(1)} fusion(bf16[2048,2816]{1,0:T(8,128)(2,1)} %bitcast.407, bf16[1536,2816]{1,0:T(8,128)(2,1)} %get-tuple-element.127), kind=kOutput, calls=%fused_computation.31 | convolution fusion | flops 8859942912 | bytes 19005440 | tf_op jit(solution)/shard_map/dot_general | solution.py:23
  433.2 12.3 %convolution_convert_fusion.8 = bf16[768,2048]{1,0:T(8,128)(2,1)S(1)} fusion(bf16[768,2816]{1,0:T(8,128)(2,1)S(1)} %slice.342, bf16[2048,2816]{1,0:T(8,128)(2,1)} %bitcast.408), kind=kOutput, calls=%fused_computation.34 | convolution fusion | flops 8859942912 | bytes 19005440 | tf_op jit(solution)/shard_map/dot_general | solution.py:23
  450.9 12.5 %convolution_convert_fusion.1 = bf16[2048,1408]{1,0:T(8,128)(2,1)S(1)} fusion(bf16[1536,2048]{1,0:T(8,128)(2,1)S(1)} %bitcast.371, bf16[1536,1408]{1,0:T(8,128)(2,1)} %get-tuple-element.126), kind=kOutput, calls=%fused_computation.1 | convolution fusion | flops 8861253632 | bytes 16384000 | tf_op jit(solution)/shard_map/dot_general | solution.py:23
  466.4 23.1 %convolution_convert_fusion = bf16[2048,2816]{1,0:T(8,128)(2,1)S(1)} fusion(bf16[1536,2048]{1,0:T(8,128)(2,1)} %constant_dynamic-update-slice_fusion.10.normed, bf16[1536,2816]{1,0:T(8,128)(2,1)} %get-tuple-element.127), kind=kOutput, calls=%fused_computation | convolution fusion | flops 17722507264 | bytes 26476544 | tf_op jit(solution)/shard_map/dot_general | solution.py:23
  508.4 9.3 %collective-permute-done.28 = bf16[1,128,2816]{2,1,0:T(8,128)(2,1)S(1)} collective-permute-done((bf16[1,128,2816]{2,1,0:T(8,128)(2,1)S(1)}, bf16[1,128,2816]{2,1,0:T(8,128)(2,1)S(1)}, u32[]{:S(2)}, u32[]{:S(2)}) %collective-permute-start.28) | collective-permute-done | bytes 720928 | tf_op jit(solution)/shard_map/ppermute | solution.py:804
  524.7 11.2 %attend_backward.2 = (bf16[8,64,768]{2,1,0:T(8,128)(2,1)S(1)}, bf16[3072,128]{1,0:T(8,128)(2,1)S(1)}) custom-call(s32[2,5]{1,0:T(2,128)S(1)} %get-tuple-element.102.meta, bf16[8,64,768]{2,1,0:T(8,128)(2,1)S(1)} %copy-done.3, bf16[3072,128]{1,0:T(8,128)(2,1)S(1)} %copy-done.5, s32[2,1,384]{2,1,0:T(1,128)S(1)} %broadcast_in_dim.67.first_ref, ...), custom_call_target="tpu_custom_call" | custom-call | flops 80000000000 | bytes 16000000 | tf_op jit(solution)/shard_map/attend_backward/pallas_call | solution.py:256
  536.0 27.6 %collective-permute-done.33 = bf16[2,128,2816]{2,1,0:T(8,128)(2,1)S(1)} collective-permute-done((bf16[2,128,2816]{2,1,0:T(8,128)(2,1)}, bf16[2,128,2816]{2,1,0:T(8,128)(2,1)S(1)}, u32[]{:S(2)}, u32[]{:S(2)}) %collective-permute-start.33) | collective-permute-done | bytes 1441824 | tf_op jit(solution)/shard_map/ppermute | solution.py:804
  564.7 7.9 convolution_convert_fusion.7
  589.2 6.5 collective-permute-done.44
  606.3 11.4 %attend_backward.3 = (bf16[8,64,768]{2,1,0:T(8,128)(2,1)S(1)}, bf16[3072,128]{1,0:T(8,128)(2,1)S(1)}) custom-call(s32[2,5]{1,0:T(2,128)S(1)} %copy-done.11, bf16[8,64,768]{2,1,0:T(8,128)(2,1)S(1)} %copy-done.1, bf16[3072,128]{1,0:T(8,128)(2,1)S(1)} %copy-done.7, s32[2,1,384]{2,1,0:T(1,128)S(1)} %copy-done.9, bf16[8,64,768]{2,1,0:T(8,128)(2,1)S(1)} %copy-done.13, ...), custom_call_target="tpu_custom_call" | custom-call | flops 80000000000 | bytes 16000000 | tf_op jit(solution)/shard_map/attend_backward/pallas_call | solution.py:256
  617.7 16.4 %collective-permute-done.46 = bf16[384,2048]{1,0:T(8,128)(2,1)S(1)} collective-permute-done((bf16[384,2048]{1,0:T(8,128)(2,1)S(1)}, bf16[384,2048]{1,0:T(8,128)(2,1)S(1)}, u32[]{:S(2)}, u32[]{:S(2)}) %collective-permute-start.46) | collective-permute-done | bytes 1572896 | tf_op jit(solution)/shard_map/ppermute | solution.py:804
  636.3 8.3 collective-permute-done.38
  647.6 7.2 fusion.53
  654.8 5.8 convolution_convert_fusion.5.near_part
  672.5 5.3 convolution_convert_fusion.6
  677.9 5.6 fusion.22
  689.3 6.4 collective-permute-start.51
  706.0 8.1 add_convert_fusion
  714.2 7.6 fusion.9
  722.2 5.2 pad_maximum_fusion.1.partial
  734.0 77.2 %closing.1 = (f32[384,2048]{1,0:T(8,128)}, bf16[4,64,1280]{2,1,0:T(8,128)(2,1)}, bf16[4,64,2816]{2,1,0:T(8,128)(2,1)}, bf16[4,64,1408]{2,1,0:T(8,128)(2,1)}) custom-call(bf16[2,2,4,128,1280]{4,3,2,1,0:T(8,128)(2,1)} %pad_maximum_fusion.1.partial, bf16[768,2048]{1,0:T(8,128)(2,1)} %convolution_convert_fusion.5.near_part, ...), custom_call_target="tpu_custom_call" | custom-call | tf_op jit(solution)/shard_map/closing/pallas_call | solution.py:713
  (494 shorter events, 256.0 us)
Async XLA Ops:
  164.3 60.1 %collective-permute-start.1 = (bf16[2,128,2816]{2,1,0:T(8,128)(2,1)}, bf16[2,128,2816]{2,1,0:T(8,128)(2,1)}, u32[]{:S(2)}, u32[]{:S(2)}) collective-permute-start(bf16[2,128,2816]{2,1,0:T(8,128)(2,1)} %dynamic-slice_bitcast_fusion), channel_id=1, source_target_pairs={{0,2},{1,3},{2,4},{3,5},{4,6},{5,7},{6,22},{7,23},{8,10},{9,11},{1... | collective-permute-start | bytes 4325384 | tf_op jit(solution)/shard_map/ppermute | solution.py:804
  165.4 59.1 %collective-permute-start.2 = (bf16[2,128,2816]{2,1,0:T(8,128)(2,1)}, bf16[2,128,2816]{2,1,0:T(8,128)(2,1)}, u32[]{:S(2)}, u32[]{:S(2)}) collective-permute-start(bf16[2,128,2816]{2,1,0:T(8,128)(2,1)} %dynamic-slice_bitcast_fusion), channel_id=1, source_target_pairs={{0,16},{1,17},{2,0},{3,1},{4,2},{5,3},{6,4},{7,5},{8,24},{9,25},{1... | collective-permute-start | bytes 4325384 | tf_op jit(solution)/shard_map/ppermute | solution.py:804
  189.4 24.2 %collective-permute-start.4 = (bf16[768,128]{1,0:T(8,128)(2,1)}, bf16[768,128]{1,0:T(8,128)(2,1)}, u32[]{:S(2)}, u32[]{:S(2)}) collective-permute-start(bf16[768,128]{1,0:T(8,128)(2,1)} %pad_maximum_fusion.21), channel_id=1, source_target_pairs={{0,4},{1,5},{2,6},{3,7},{8,12},{9,13},{10,14},{11,15},{16,20},{17,... | collective-permute-start | bytes 589832 | tf_op jit(solution)/shard_map/ppermute | solution.py:804
  222.1 47.2 %collective-permute-start.18 = (bf16[384,2048]{1,0:T(8,128)(2,1)S(1)}, bf16[384,2048]{1,0:T(8,128)(2,1)S(1)}, u32[]{:S(2)}, u32[]{:S(2)}) collective-permute-start(bf16[384,2048]{1,0:T(8,128)(2,1)S(1)} %bitcast.374), channel_id=1, source_target_pairs={{0,8},{1,9},{2,10},{3,11},{4,12},{5,13},{6,14},{7,15},{8,0},{9,1},... | collective-permute-start | bytes 4718600 | tf_op jit(solution)/shard_map/ppermute | solution.py:804
  224.3 95.2 %collective-permute-start.17 = (bf16[384,2048]{1,0:T(8,128)(2,1)S(1)}, bf16[384,2048]{1,0:T(8,128)(2,1)S(1)}, u32[]{:S(2)}, u32[]{:S(2)}) collective-permute-start(bf16[384,2048]{1,0:T(8,128)(2,1)S(1)} %bitcast.375), channel_id=1, source_target_pairs={{0,1},{1,0},{2,3},{3,2},{4,5},{5,4},{6,7},{7,6},{8,9},{9,8},{10,11... | collective-permute-start | bytes 4718600 | tf_op jit(solution)/shard_map/ppermute | solution.py:804
  224.5 34.2 %collective-permute-start.6 = (bf16[2,128,2816]{2,1,0:T(8,128)(2,1)}, bf16[2,128,2816]{2,1,0:T(8,128)(2,1)S(1)}, u32[]{:S(2)}, u32[]{:S(2)}) collective-permute-start(bf16[2,128,2816]{2,1,0:T(8,128)(2,1)} %collective-permute-done.1), channel_id=1, source_target_pairs={{0,2},{1,3},{2,4},{3,5},{4,6},{5,7},{6,22},{7,23},{8,10},{9,11},{1... | collective-permute-start | bytes 4325384 | tf_op jit(solution)/shard_map/ppermute | solution.py:804
  228.1 32.3 %collective-permute-start.7 = (bf16[2,128,2816]{2,1,0:T(8,128)(2,1)}, bf16[2,128,2816]{2,1,0:T(8,128)(2,1)S(1)}, u32[]{:S(2)}, u32[]{:S(2)}) collective-permute-start(bf16[2,128,2816]{2,1,0:T(8,128)(2,1)} %collective-permute-done.2), channel_id=1, source_target_pairs={{0,16},{1,17},{2,0},{3,1},{4,2},{5,3},{6,4},{7,5},{8,24},{9,25},{1... | collective-permute-start | bytes 4325384 | tf_op jit(solution)/shard_map/ppermute | solution.py:804
  269.3 50.2 %collective-permute-start.19 = (bf16[384,2048]{1,0:T(8,128)(2,1)S(1)}, bf16[384,2048]{1,0:T(8,128)(2,1)}, u32[]{:S(2)}, u32[]{:S(2)}) collective-permute-start(bf16[384,2048]{1,0:T(8,128)(2,1)S(1)} %collective-permute-done.18), channel_id=1, source_target_pairs={{0,1},{1,0},{2,3},{3,2},{4,5},{5,4},{6,7},{7,6},{8,9},{9,8},{10,11... | collective-permute-start | bytes 4718600 | tf_op jit(solution)/shard_map/ppermute | solution.py:804
  269.8 44.8 %collective-permute-start.8 = (bf16[2,128,2816]{2,1,0:T(8,128)(2,1)}, bf16[2,128,2816]{2,1,0:T(8,128)(2,1)S(1)}, u32[]{:S(2)}, u32[]{:S(2)}) collective-permute-start(bf16[2,128,2816]{2,1,0:T(8,128)(2,1)} %copy-done.50), channel_id=1, source_target_pairs={{0,2},{1,3},{2,4},{3,5},{4,6},{5,7},{6,22},{7,23},{8,10},{9,11},{1... | collective-permute-start | bytes 4325384 | tf_op jit(solution)/shard_map/ppermute | solution.py:804
  271.6 43.0 %collective-permute-start.9 = (bf16[2,128,2816]{2,1,0:T(8,128)(2,1)S(1)}, bf16[2,128,2816]{2,1,0:T(8,128)(2,1)S(1)}, u32[]{:S(2)}, u32[]{:S(2)}) collective-permute-start(bf16[2,128,2816]{2,1,0:T(8,128)(2,1)S(1)} %collective-permute-done.7), channel_id=1, source_target_pairs={{0,16},{1,17},{2,0},{3,1},{4,2},{5,3},{6,4},{7,5},{8,24},{9,25},{1... | collective-permute-start | bytes 4325384 | tf_op jit(solution)/shard_map/ppermute | solution.py:804
  276.3 37.8 %collective-permute-start.14 = (bf16[384,2048]{1,0:T(8,128)(2,1)}, bf16[384,2048]{1,0:T(8,128)(2,1)S(1)}, u32[]{:S(2)}, u32[]{:S(2)}) collective-permute-start(bf16[384,2048]{1,0:T(8,128)(2,1)} %add_convert_fusion.5), channel_id=1, source_target_pairs={{0,8},{1,9},{2,10},{3,11},{4,12},{5,13},{6,14},{7,15},{8,0},{9,1},... | collective-permute-start | bytes 4718600 | tf_op jit(solution)/shard_map/ppermute | solution.py:804
  345.1 36.1 %collective-permute-start.20 = (bf16[384,2048]{1,0:T(8,128)(2,1)S(1)}, bf16[384,2048]{1,0:T(8,128)(2,1)}, u32[]{:S(2)}, u32[]{:S(2)}) collective-permute-start(bf16[384,2048]{1,0:T(8,128)(2,1)S(1)} %multiply_convert_fusion), channel_id=1, source_target_pairs={{0,8},{1,9},{2,10},{3,11},{4,12},{5,13},{6,14},{7,15},{8,0},{9,1},... | collective-permute-start | bytes 4718600 | tf_op jit(solution)/shard_map/ppermute | solution.py:804
  445.7 43.8 %collective-permute-start.30 = (bf16[384,2048]{1,0:T(8,128)(2,1)S(1)}, bf16[384,2048]{1,0:T(8,128)(2,1)S(1)}, u32[]{:S(2)}, u32[]{:S(2)}) collective-permute-start(bf16[384,2048]{1,0:T(8,128)(2,1)S(1)} %slice.430), channel_id=1, source_target_pairs={{0,1},{1,0},{2,3},{3,2},{4,5},{5,4},{6,7},{7,6},{8,9},{9,8},{10,11... | collective-permute-start | bytes 4718600 | tf_op jit(solution)/shard_map/ppermute | solution.py:804
  449.2 40.3 %collective-permute-start.27 = (bf16[384,2048]{1,0:T(8,128)(2,1)}, bf16[384,2048]{1,0:T(8,128)(2,1)S(1)}, u32[]{:S(2)}, u32[]{:S(2)}) collective-permute-start(bf16[384,2048]{1,0:T(8,128)(2,1)} %add_convert_fusion.4), channel_id=1, source_target_pairs={{0,8},{1,9},{2,10},{3,11},{4,12},{5,13},{6,14},{7,15},{8,0},{9,1},... | collective-permute-start | bytes 4718600 | tf_op jit(solution)/shard_map/ppermute | solution.py:804
  463.5 26.0 %collective-permute-start.25 = (bf16[1,128,1408]{2,1,0:T(8,128)(2,1)S(1)}, bf16[1,128,1408]{2,1,0:T(8,128)(2,1)S(1)}, u32[]{:S(2)}, u32[]{:S(2)}) collective-permute-start(bf16[1,128,1408]{2,1,0:T(8,128)(2,1)S(1)} %get-tuple-element.199), channel_id=1, source_target_pairs={{0,2},{1,3},{2,4},{3,5},{4,6},{5,7},{6,22},{7,23},{8,10},{9,11},{1... | collective-permute-start | bytes 1081352 | tf_op jit(solution)/shard_map/ppermute | solution.py:804
  498.1 37.9 %collective-permute-start.36 = (bf16[384,2048]{1,0:T(8,128)(2,1)S(1)}, bf16[384,2048]{1,0:T(8,128)(2,1)S(1)}, u32[]{:S(2)}, u32[]{:S(2)}) collective-permute-start(bf16[384,2048]{1,0:T(8,128)(2,1)S(1)} %get-tuple-element.178), channel_id=1, source_target_pairs={{0,8},{1,9},{2,10},{3,11},{4,12},{5,13},{6,14},{7,15},{8,0},{9,1},... | collective-permute-start | bytes 4718600 | tf_op jit(solution)/shard_map/ppermute | solution.py:804
  502.0 33.9 %collective-permute-start.35 = (bf16[2,128,1408]{2,1,0:T(8,128)(2,1)S(1)}, bf16[2,128,1408]{2,1,0:T(8,128)(2,1)}, u32[]{:S(2)}, u32[]{:S(2)}) collective-permute-start(bf16[2,128,1408]{2,1,0:T(8,128)(2,1)S(1)} %pad_maximum_fusion.16), channel_id=1, source_target_pairs={{0,16},{1,17},{2,0},{3,1},{4,2},{5,3},{6,4},{7,5},{8,24},{9,25},{1... | collective-permute-start | bytes 2162696 | tf_op jit(solution)/shard_map/ppermute | solution.py:804
  504.4 31.6 %collective-permute-start.34 = (bf16[2,128,1408]{2,1,0:T(8,128)(2,1)S(1)}, bf16[2,128,1408]{2,1,0:T(8,128)(2,1)S(1)}, u32[]{:S(2)}, u32[]{:S(2)}) collective-permute-start(bf16[2,128,1408]{2,1,0:T(8,128)(2,1)S(1)} %pad_maximum_fusion.15), channel_id=1, source_target_pairs={{0,2},{1,3},{2,4},{3,5},{4,6},{5,7},{6,22},{7,23},{8,10},{9,11},{1... | collective-permute-start | bytes 2162696 | tf_op jit(solution)/shard_map/ppermute | solution.py:804
  521.1 42.5 %collective-permute-start.33 = (bf16[2,128,2816]{2,1,0:T(8,128)(2,1)}, bf16[2,128,2816]{2,1,0:T(8,128)(2,1)S(1)}, u32[]{:S(2)}, u32[]{:S(2)}) collective-permute-start(bf16[2,128,2816]{2,1,0:T(8,128)(2,1)} %pad_maximum_fusion.8), channel_id=1, source_target_pairs={{0,16},{1,17},{2,0},{3,1},{4,2},{5,3},{6,4},{7,5},{8,24},{9,25},{1... | collective-permute-start | bytes 4325384 | tf_op jit(solution)/shard_map/ppermute | solution.py:804
  522.6 41.0 %collective-permute-start.32 = (bf16[2,128,2816]{2,1,0:T(8,128)(2,1)}, bf16[2,128,2816]{2,1,0:T(8,128)(2,1)S(1)}, u32[]{:S(2)}, u32[]{:S(2)}) collective-permute-start(bf16[2,128,2816]{2,1,0:T(8,128)(2,1)} %pad_maximum_fusion.7), channel_id=1, source_target_pairs={{0,2},{1,3},{2,4},{3,5},{4,6},{5,7},{6,22},{7,23},{8,10},{9,11},{1... | collective-permute-start | bytes 4325384 | tf_op jit(solution)/shard_map/ppermute | solution.py:804
  587.5 48.8 %collective-permute-start.39 = (bf16[2,128,1408]{2,1,0:T(8,128)(2,1)}, bf16[2,128,1408]{2,1,0:T(8,128)(2,1)}, u32[]{:S(2)}, u32[]{:S(2)}) collective-permute-start(bf16[2,128,1408]{2,1,0:T(8,128)(2,1)} %get-tuple-element.195), channel_id=1, source_target_pairs={{0,2},{1,3},{2,4},{3,5},{4,6},{5,7},{6,22},{7,23},{8,10},{9,11},{1... | collective-permute-start | bytes 2162696 | tf_op jit(solution)/shard_map/ppermute | solution.py:804
  595.7 40.5 %collective-permute-start.40 = (bf16[2,128,1408]{2,1,0:T(8,128)(2,1)}, bf16[2,128,1408]{2,1,0:T(8,128)(2,1)}, u32[]{:S(2)}, u32[]{:S(2)}) collective-permute-start(bf16[2,128,1408]{2,1,0:T(8,128)(2,1)} %get-tuple-element.194), channel_id=1, source_target_pairs={{0,16},{1,17},{2,0},{3,1},{4,2},{5,3},{6,4},{7,5},{8,24},{9,25},{1... | collective-permute-start | bytes 2162696 | tf_op jit(solution)/shard_map/ppermute | solution.py:804
  596.7 47.8 %collective-permute-start.38 = (bf16[2,128,2816]{2,1,0:T(8,128)(2,1)}, bf16[2,128,2816]{2,1,0:T(8,128)(2,1)}, u32[]{:S(2)}, u32[]{:S(2)}) collective-permute-start(bf16[2,128,2816]{2,1,0:T(8,128)(2,1)} %fusion.25), channel_id=1, source_target_pairs={{0,16},{1,17},{2,0},{3,1},{4,2},{5,3},{6,4},{7,5},{8,24},{9,25},{1... | collective-permute-start | bytes 4325384 | tf_op jit(solution)/shard_map/ppermute | solution.py:804
  596.9 47.6 %collective-permute-start.37 = (bf16[2,128,2816]{2,1,0:T(8,128)(2,1)}, bf16[2,128,2816]{2,1,0:T(8,128)(2,1)}, u32[]{:S(2)}, u32[]{:S(2)}) collective-permute-start(bf16[2,128,2816]{2,1,0:T(8,128)(2,1)} %fusion.26), channel_id=1, source_target_pairs={{0,2},{1,3},{2,4},{3,5},{4,6},{5,7},{6,22},{7,23},{8,10},{9,11},{1... | collective-permute-start | bytes 4325384 | tf_op jit(solution)/shard_map/ppermute | solution.py:804
  599.7 34.5 %collective-permute-start.46 = (bf16[384,2048]{1,0:T(8,128)(2,1)S(1)}, bf16[384,2048]{1,0:T(8,128)(2,1)S(1)}, u32[]{:S(2)}, u32[]{:S(2)}) collective-permute-start(bf16[384,2048]{1,0:T(8,128)(2,1)S(1)} %add_convert_fusion.3), channel_id=1, source_target_pairs={{0,8},{1,9},{2,10},{3,11},{4,12},{5,13},{6,14},{7,15},{8,0},{9,1},... | collective-permute-start | bytes 4718600 | tf_op jit(solution)/shard_map/ppermute | solution.py:804
  664.2 63.3 %collective-permute-start.53 = (bf16[2,128,1408]{2,1,0:T(8,128)(2,1)}, bf16[2,128,1408]{2,1,0:T(8,128)(2,1)}, u32[]{:S(2)}, u32[]{:S(2)}) collective-permute-start(bf16[2,128,1408]{2,1,0:T(8,128)(2,1)} %get-tuple-element.192), channel_id=1, source_target_pairs={{0,2},{1,3},{2,4},{3,5},{4,6},{5,7},{6,22},{7,23},{8,10},{9,11},{1... | collective-permute-start | bytes 2162696 | tf_op jit(solution)/shard_map/ppermute | solution.py:804
  664.2 63.3 %collective-permute-start.54 = (bf16[2,128,1408]{2,1,0:T(8,128)(2,1)}, bf16[2,128,1408]{2,1,0:T(8,128)(2,1)}, u32[]{:S(2)}, u32[]{:S(2)}) collective-permute-start(bf16[2,128,1408]{2,1,0:T(8,128)(2,1)} %get-tuple-element.193), channel_id=1, source_target_pairs={{0,16},{1,17},{2,0},{3,1},{4,2},{5,3},{6,4},{7,5},{8,24},{9,25},{1... | collective-permute-start | bytes 2162696 | tf_op jit(solution)/shard_map/ppermute | solution.py:804
  667.5 31.9 %collective-permute-start.49 = (bf16[768,128]{1,0:T(8,128)(2,1)S(1)}, bf16[768,128]{1,0:T(8,128)(2,1)S(1)}, u32[]{:S(2)}, u32[]{:S(2)}) collective-permute-start(bf16[768,128]{1,0:T(8,128)(2,1)S(1)} %get-tuple-element.230), channel_id=1, source_target_pairs={{4,0},{5,1},{6,2},{7,3},{12,8},{13,9},{14,10},{15,11},{20,16},{21,... | collective-permute-start | bytes 589832 | tf_op jit(solution)/shard_map/ppermute | solution.py:804
  668.8 31.6 %collective-permute-start.50 = (bf16[768,128]{1,0:T(8,128)(2,1)S(1)}, bf16[768,128]{1,0:T(8,128)(2,1)S(1)}, u32[]{:S(2)}, u32[]{:S(2)}) collective-permute-start(bf16[768,128]{1,0:T(8,128)(2,1)S(1)} %get-tuple-element.229), channel_id=1, source_target_pairs={{6,0},{7,1},{14,8},{15,9},{22,16},{23,17},{30,24},{31,25}} | collective-permute-start | bytes 589832 | tf_op jit(solution)/shard_map/ppermute | solution.py:804
  689.3 40.8 %collective-permute-start.51 = (bf16[2,128,2816]{2,1,0:T(8,128)(2,1)}, bf16[2,128,2816]{2,1,0:T(8,128)(2,1)}, u32[]{:S(2)}, u32[]{:S(2)}) collective-permute-start(bf16[2,128,2816]{2,1,0:T(8,128)(2,1)} %get-tuple-element.182), channel_id=1, source_target_pairs={{0,2},{1,3},{2,4},{3,5},{4,6},{5,7},{6,22},{7,23},{8,10},{9,11},{1... | collective-permute-start | bytes 4325384 | tf_op jit(solution)/shard_map/ppermute | solution.py:804
  699.4 30.7 %collective-permute-start.52 = (bf16[2,128,2816]{2,1,0:T(8,128)(2,1)S(1)}, bf16[2,128,2816]{2,1,0:T(8,128)(2,1)}, u32[]{:S(2)}, u32[]{:S(2)}) collective-permute-start(bf16[2,128,2816]{2,1,0:T(8,128)(2,1)S(1)} %get-tuple-element.183), channel_id=1, source_target_pairs={{0,16},{1,17},{2,0},{3,1},{4,2},{5,3},{6,4},{7,5},{8,24},{9,25},{1... | collective-permute-start | bytes 4325384 | tf_op jit(solution)/shard_map/ppermute | solution.py:804
  700.5 127.5 %collective-permute-start.47 = (bf16[384,2048]{1,0:T(8,128)(2,1)}, bf16[384,2048]{1,0:T(8,128)(2,1)}, u32[]{:S(2)}, u32[]{:S(2)}) collective-permute-start(bf16[384,2048]{1,0:T(8,128)(2,1)} %slice.436), channel_id=1, source_target_pairs={{0,1},{1,0},{2,3},{3,2},{4,5},{5,4},{6,7},{7,6},{8,9},{9,8},{10,11... | collective-permute-start | bytes 4718600 | tf_op jit(solution)/shard_map/ppermute | solution.py:804
  (117 other events, 2513.2 us)

commit v6 on v5

--- a/solution.py
+++ b/solution.py
@@ -23,11 +23,6 @@
     return lax.dot_general(
         left, right, (((left_dim,), (right_dim,)), ((), ())), preferred_element_type=F32
     )
-
-
-def doc_first(start_row, places):
-    inside = start_row[None, :] <= places[:, None]
-    return jnp.max(jnp.where(inside, start_row[None, :], 0), axis=1)
 
 
 def rotary_tables(offsets):
@@ -944,11 +939,16 @@
     block_at = [rows * (2 * z_at + (c_at ^ dc)) for dc in range(2)]
     within = jnp.arange(rows, dtype=jnp.int32)
     base_block = 2 * (z_at - deep + 1)
+    places = jnp.concatenate([block_at[dc] + within for dc in range(2)])[None]
+    both_starts = jnp.stack(start_rows)
+    both_firsts = jnp.zeros((2, 2 * rows), jnp.int32)
+    for slot in range(both_starts.shape[1]):
+        start = both_starts[:, slot : slot + 1]
+        both_firsts = jnp.maximum(both_firsts, jnp.where(start <= places, start, 0))
     tables, first_rows, metas = [], [], []
     for dx in range(2):
-        places = [block_at[dc] + within for dc in range(2)]
-        firsts = [doc_first(start_rows[dx], places[dc]) for dc in range(2)]
-        tables.append(rotary_tables(jnp.concatenate([p - f for p, f in zip(places, firsts)])))
+        tables.append(rotary_tables((places - both_firsts)[dx]))
+        firsts = [both_firsts[dx, dc * rows : (dc + 1) * rows] for dc in range(2)]
         first_rows.append(jnp.stack(firsts)[:, None, :])
         cells = [
             [
@@ -1017,8 +1017,9 @@
     far = send(far_sum, x_perm).astype(F32)
     query_near = after(queries[0], far_sum)
     attended[0], lses[0] = attend_forward(metas[0], query_near, keyvals[0], first_rows[0])
-    attended[0], far = stage(rings, (attended[0], far))
+    attended[0] = stage(rings, attended[0])
     advance(rings, half_ring)
+    attended[0], far = stage([], (attended[0], far))
     near = reduce_core(contract(attended[0].reshape(q_cols, -1), w_out_t, 0, 1).astype(BF))
     middle = own_tokens.astype(F32) + near + far
     attended_t = [a.reshape(q_cols, -1) for a in attended]

time: 842 us -> 840 us (level)
    unnamed x207 -> x211, local copies, waits for them, and re-layouts: 19.1 us -> 19.3 us
  transfers between devices with their start and end apart: 55 -> 55, of which waited for: 13 -> 15; matrix products, arithmetic and copies ran while one was open for 28% -> 28% of each run, Pallas kernels for 17% -> 17%
where the time goes in v6:
time: 840 us; the launch traced here: 832 us
  Pallas kernels  295 us (35%)
  waiting for transfers between devices  147 us (18%)
  matrix products  133 us (16%)
  other arithmetic  91.3 us (11%)
  local copies, waits for them, and re-layouts  78.3 us (9%)
  starting transfers between devices  75.4 us (9%)
  between operations  11.2 us (1%)
    ppermute x55, waiting for transfers between devices, send(): return lax.ppermute(value, AXES, perm)  147 us
    dot_general x18, matrix products, contract(): lax.dot_general(left, right, (((left_dim,), (right_dim,)), ((), ())), pre...  133 us
    pallas_call x1, Pallas kernels, opening(): pl.pallas_call(functools.partial(opening_kernel, wide=wide, deep=deep, ow...  133 us
    pallas_call x1, Pallas kernels, closing(): pl.pallas_call(functools.partial(closing_kernel, wide=wide, deep=deep, ow...  77.9 us
    ppermute x55, starting transfers between devices, send(): return lax.ppermute(value, AXES, perm)  75.4 us
    pallas_call x2, Pallas kernels, feed_forward(): pl.pallas_call(functools.partial(feed_kernel, columns=columns), grid=(tok...  46.9 us
    pallas_call x2, Pallas kernels, attend_backward(): pl.pallas_call(functools.partial(backward_kernel, rows=rows, heads=heads,...  22.6 us
    convert_element_type x7, other arithmetic, add_low(): return (one.astype(F32) + other.astype(F32)).astype(BF)  19.4 us
  transfers between devices with their start and end apart: 55, of which 15 were waited for; matrix products, arithmetic and copies ran while one was open for 28% of the time, Pallas kernels for 17%

profile of v6, /device:TPU:0, one launch (start us, length us, event | category | flops | bytes accessed | tf_op | source)
XLA Modules:
  0.0 832.0 jit_solution(7054344522157423911)
XLA Ops:
  27.3 132.7 %opening.1 = (bf16[4,384,2048]{2,1,0:T(8,128)(2,1)}, bf16[2,2,4,128,1280]{4,3,2,1,0:T(8,128)(2,1)}, bf16[2,2,4,128,1408]{4,3,2,1,0:T(8,128)(2,1)}, bf16[2,2,4,128,2816]{4,3,2,1,0:T(8,128)(2,1)}) custom-call(bf16[384,2048]{1,0:T(8,128)(2,1)} %bitcast.364, bf16[4,64,1280]{2,1,0:T(8,128)(2,1)} %concatenate.110.quarters_attn, bf16[4,64,1408]{2,1,0:T(8,128)(2,1)} %bitcast.390, ...), custom_call_target="tpu_custom_call" | custom-call | tf_op jit(solution)/shard_map/opening/pallas_call | solution.py:507
  212.0 7.4 collective-permute-start.13
  226.5 7.5 attend_forward.2
  234.0 23.0 %collective-permute-done.6 = bf16[2,128,2816]{2,1,0:T(8,128)(2,1)S(1)} collective-permute-done((bf16[2,128,2816]{2,1,0:T(8,128)(2,1)}, bf16[2,128,2816]{2,1,0:T(8,128)(2,1)S(1)}, u32[]{:S(2)}, u32[]{:S(2)}) %collective-permute-start.6) | collective-permute-done | bytes 1441824 | tf_op jit(solution)/shard_map/ppermute | solution.py:799
  278.1 7.5 attend_forward.3
  285.6 16.2 %collective-permute-done.8 = bf16[2,128,2816]{2,1,0:T(8,128)(2,1)S(1)} collective-permute-done((bf16[2,128,2816]{2,1,0:T(8,128)(2,1)}, bf16[2,128,2816]{2,1,0:T(8,128)(2,1)S(1)}, u32[]{:S(2)}, u32[]{:S(2)}) %collective-permute-start.8) | collective-permute-done | bytes 1441824 | tf_op jit(solution)/shard_map/ppermute | solution.py:799
  303.3 9.1 %collective-permute-done.14 = bf16[384,2048]{1,0:T(8,128)(2,1)S(1)} collective-permute-done((bf16[384,2048]{1,0:T(8,128)(2,1)}, bf16[384,2048]{1,0:T(8,128)(2,1)S(1)}, u32[]{:S(2)}, u32[]{:S(2)}) %collective-permute-start.14) | collective-permute-done | bytes 1572896 | tf_op jit(solution)/shard_map/ppermute | solution.py:799
  329.3 13.1 %collective-permute-done.21 = bf16[1,128,2816]{2,1,0:T(8,128)(2,1)S(1)} collective-permute-done((bf16[1,128,2816]{2,1,0:T(8,128)(2,1)S(1)}, bf16[1,128,2816]{2,1,0:T(8,128)(2,1)S(1)}, u32[]{:S(2)}, u32[]{:S(2)}) %collective-permute-start.21) | collective-permute-done | bytes 720928 | tf_op jit(solution)/shard_map/ppermute | solution.py:799
  348.2 23.6 %feed_forward.2 = (bf16[1536,1408]{1,0:T(8,128)(2,1)}, bf16[1536,2816]{1,0:T(8,128)(2,1)}) custom-call(bf16[768,2048]{1,0:T(8,128)(2,1)} %pad_maximum_fusion.2.normed, bf16[1536,2048]{1,0:T(8,128)(2,1)} %pad_maximum_fusion.cotangent, bf16[2048,2816]{1,0:T(8,128)(2,1)} %bitcast.409, bf16[2048,1408]{1,0:T(8,128)(2,1)} %bitcast.432), custom_call_target="tpu_custom_call" | custom-call | flops 13287555072 | bytes 17301504 | tf_op jit(solution)/shard_map/feed_forward/pallas_call | solution.py:319
  371.8 7.6 collective-permute-done.20
  390.3 23.3 %feed_forward.3 = (bf16[1536,1408]{1,0:T(8,128)(2,1)}, bf16[1536,2816]{1,0:T(8,128)(2,1)}) custom-call(bf16[1536,2048]{1,0:T(8,128)(2,1)} %constant_dynamic-update-slice_fusion.10.normed, bf16[1536,2048]{1,0:T(8,128)(2,1)} %pad_maximum_fusion.cotangent, bf16[2048,2816]{1,0:T(8,128)(2,1)} %bitcast.410, ...), custom_call_target="tpu_custom_call", output_to_operand_aliasing={{0}: (4, {}), {1}: (5, {})} | custom-call | flops 13287555072 | bytes 17301504 | tf_op jit(solution)/shard_map/feed_forward/pallas_call | solution.py:319
  413.6 13.4 %fusion.12 = bf16[768,2048]{1,0:T(8,128)(2,1)S(1)} fusion(bf16[2048,2816]{1,0:T(8,128)(2,1)} %bitcast.411, bf16[1536,2816]{1,0:T(8,128)(2,1)} %get-tuple-element.129), kind=kOutput, calls=%fused_computation.31 | convolution fusion | flops 8859942912 | bytes 19005440 | tf_op jit(solution)/shard_map/dot_general | solution.py:23
  431.4 12.3 %convolution_convert_fusion.8 = bf16[768,2048]{1,0:T(8,128)(2,1)S(1)} fusion(bf16[768,2816]{1,0:T(8,128)(2,1)S(1)} %slice.406, bf16[2048,2816]{1,0:T(8,128)(2,1)} %bitcast.412), kind=kOutput, calls=%fused_computation.34 | convolution fusion | flops 8859942912 | bytes 19005440 | tf_op jit(solution)/shard_map/dot_general | solution.py:23
  449.2 12.5 %convolution_convert_fusion.1 = bf16[2048,1408]{1,0:T(8,128)(2,1)S(1)} fusion(bf16[1536,2048]{1,0:T(8,128)(2,1)S(1)} %bitcast.375, bf16[1536,1408]{1,0:T(8,128)(2,1)} %get-tuple-element.128), kind=kOutput, calls=%fused_computation.1 | convolution fusion | flops 8861253632 | bytes 16384000 | tf_op jit(solution)/shard_map/dot_general | solution.py:23
  464.6 23.0 %convolution_convert_fusion = bf16[2048,2816]{1,0:T(8,128)(2,1)S(1)} fusion(bf16[1536,2048]{1,0:T(8,128)(2,1)} %constant_dynamic-update-slice_fusion.10.normed, bf16[1536,2816]{1,0:T(8,128)(2,1)} %get-tuple-element.129), kind=kOutput, calls=%fused_computation | convolution fusion | flops 17722507264 | bytes 26476544 | tf_op jit(solution)/shard_map/dot_general | solution.py:23
  506.5 9.4 %collective-permute-done.28 = bf16[1,128,2816]{2,1,0:T(8,128)(2,1)S(1)} collective-permute-done((bf16[1,128,2816]{2,1,0:T(8,128)(2,1)S(1)}, bf16[1,128,2816]{2,1,0:T(8,128)(2,1)S(1)}, u32[]{:S(2)}, u32[]{:S(2)}) %collective-permute-start.28) | collective-permute-done | bytes 720928 | tf_op jit(solution)/shard_map/ppermute | solution.py:799
  523.0 11.2 %attend_backward.2 = (bf16[8,64,768]{2,1,0:T(8,128)(2,1)S(1)}, bf16[3072,128]{1,0:T(8,128)(2,1)S(1)}) custom-call(s32[2,5]{1,0:T(2,128)S(1)} %get-tuple-element.103.meta, bf16[8,64,768]{2,1,0:T(8,128)(2,1)S(1)} %copy-done.3, bf16[3072,128]{1,0:T(8,128)(2,1)S(1)} %copy-done.5, s32[2,1,384]{2,1,0:T(1,128)S(1)} %copy-done.11, ...), custom_call_target="tpu_custom_call" | custom-call | flops 80000000000 | bytes 16000000 | tf_op jit(solution)/shard_map/attend_backward/pallas_call | solution.py:251
  534.3 27.5 %collective-permute-done.33 = bf16[2,128,2816]{2,1,0:T(8,128)(2,1)S(1)} collective-permute-done((bf16[2,128,2816]{2,1,0:T(8,128)(2,1)}, bf16[2,128,2816]{2,1,0:T(8,128)(2,1)S(1)}, u32[]{:S(2)}, u32[]{:S(2)}) %collective-permute-start.33) | collective-permute-done | bytes 1441824 | tf_op jit(solution)/shard_map/ppermute | solution.py:799
  562.9 7.9 convolution_convert_fusion.7
  587.3 6.6 collective-permute-done.44
  604.4 11.4 %attend_backward.3 = (bf16[8,64,768]{2,1,0:T(8,128)(2,1)S(1)}, bf16[3072,128]{1,0:T(8,128)(2,1)S(1)}) custom-call(s32[2,5]{1,0:T(2,128)S(1)} %copy-done.13, bf16[8,64,768]{2,1,0:T(8,128)(2,1)S(1)} %copy-done.1, bf16[3072,128]{1,0:T(8,128)(2,1)S(1)} %copy-done.7, s32[2,1,384]{2,1,0:T(1,128)S(1)} %copy-done.9, bf16[8,64,768]{2,1,0:T(8,128)(2,1)S(1)} %copy-done.15, ...), custom_call_target="tpu_custom_call" | custom-call | flops 80000000000 | bytes 16000000 | tf_op jit(solution)/shard_map/attend_backward/pallas_call | solution.py:251
  615.8 16.5 %collective-permute-done.46 = bf16[384,2048]{1,0:T(8,128)(2,1)S(1)} collective-permute-done((bf16[384,2048]{1,0:T(8,128)(2,1)S(1)}, bf16[384,2048]{1,0:T(8,128)(2,1)S(1)}, u32[]{:S(2)}, u32[]{:S(2)}) %collective-permute-start.46) | collective-permute-done | bytes 1572896 | tf_op jit(solution)/shard_map/ppermute | solution.py:799
  634.4 8.4 %collective-permute-done.38 = bf16[2,128,2816]{2,1,0:T(8,128)(2,1)} collective-permute-done((bf16[2,128,2816]{2,1,0:T(8,128)(2,1)}, bf16[2,128,2816]{2,1,0:T(8,128)(2,1)}, u32[]{:S(2)}, u32[]{:S(2)}) %collective-permute-start.38) | collective-permute-done | bytes 1441824 | tf_op jit(solution)/shard_map/ppermute | solution.py:799
  645.8 7.2 fusion.53
  653.0 5.8 convolution_convert_fusion.5.near_part
  670.7 5.3 convolution_convert_fusion.6
  676.0 5.6 fusion.22
  687.5 6.4 collective-permute-start.51
  704.1 8.1 add_convert_fusion
  712.3 7.6 fusion.9
  720.3 5.2 pad_maximum_fusion.1.partial
  732.0 77.9 %closing.1 = (f32[384,2048]{1,0:T(8,128)}, bf16[4,64,1280]{2,1,0:T(8,128)(2,1)}, bf16[4,64,2816]{2,1,0:T(8,128)(2,1)}, bf16[4,64,1408]{2,1,0:T(8,128)(2,1)}) custom-call(bf16[2,2,4,128,1280]{4,3,2,1,0:T(8,128)(2,1)} %pad_maximum_fusion.1.partial, bf16[768,2048]{1,0:T(8,128)(2,1)} %convolution_convert_fusion.5.near_part, ...), custom_call_target="tpu_custom_call" | custom-call | tf_op jit(solution)/shard_map/closing/pallas_call | solution.py:708
  (492 shorter events, 260.6 us)
Async XLA Ops:
  162.6 60.0 %collective-permute-start.1 = (bf16[2,128,2816]{2,1,0:T(8,128)(2,1)}, bf16[2,128,2816]{2,1,0:T(8,128)(2,1)}, u32[]{:S(2)}, u32[]{:S(2)}) collective-permute-start(bf16[2,128,2816]{2,1,0:T(8,128)(2,1)} %dynamic-slice_bitcast_fusion), channel_id=1, source_target_pairs={{0,2},{1,3},{2,4},{3,5},{4,6},{5,7},{6,22},{7,23},{8,10},{9,11},{1... | collective-permute-start | bytes 4325384 | tf_op jit(solution)/shard_map/ppermute | solution.py:799
  163.7 59.0 %collective-permute-start.2 = (bf16[2,128,2816]{2,1,0:T(8,128)(2,1)}, bf16[2,128,2816]{2,1,0:T(8,128)(2,1)}, u32[]{:S(2)}, u32[]{:S(2)}) collective-permute-start(bf16[2,128,2816]{2,1,0:T(8,128)(2,1)} %dynamic-slice_bitcast_fusion), channel_id=1, source_target_pairs={{0,16},{1,17},{2,0},{3,1},{4,2},{5,3},{6,4},{7,5},{8,24},{9,25},{1... | collective-permute-start | bytes 4325384 | tf_op jit(solution)/shard_map/ppermute | solution.py:799
  187.7 24.2 %collective-permute-start.4 = (bf16[768,128]{1,0:T(8,128)(2,1)}, bf16[768,128]{1,0:T(8,128)(2,1)}, u32[]{:S(2)}, u32[]{:S(2)}) collective-permute-start(bf16[768,128]{1,0:T(8,128)(2,1)} %pad_maximum_fusion.21), channel_id=1, source_target_pairs={{0,4},{1,5},{2,6},{3,7},{8,12},{9,13},{10,14},{11,15},{16,20},{17,... | collective-permute-start | bytes 589832 | tf_op jit(solution)/shard_map/ppermute | solution.py:799
  220.4 47.2 %collective-permute-start.18 = (bf16[384,2048]{1,0:T(8,128)(2,1)S(1)}, bf16[384,2048]{1,0:T(8,128)(2,1)S(1)}, u32[]{:S(2)}, u32[]{:S(2)}) collective-permute-start(bf16[384,2048]{1,0:T(8,128)(2,1)S(1)} %bitcast.378), channel_id=1, source_target_pairs={{0,8},{1,9},{2,10},{3,11},{4,12},{5,13},{6,14},{7,15},{8,0},{9,1},... | collective-permute-start | bytes 4718600 | tf_op jit(solution)/shard_map/ppermute | solution.py:799
  222.5 95.2 %collective-permute-start.17 = (bf16[384,2048]{1,0:T(8,128)(2,1)S(1)}, bf16[384,2048]{1,0:T(8,128)(2,1)S(1)}, u32[]{:S(2)}, u32[]{:S(2)}) collective-permute-start(bf16[384,2048]{1,0:T(8,128)(2,1)S(1)} %bitcast.379), channel_id=1, source_target_pairs={{0,1},{1,0},{2,3},{3,2},{4,5},{5,4},{6,7},{7,6},{8,9},{9,8},{10,11... | collective-permute-start | bytes 4718600 | tf_op jit(solution)/shard_map/ppermute | solution.py:799
  222.7 34.2 %collective-permute-start.6 = (bf16[2,128,2816]{2,1,0:T(8,128)(2,1)}, bf16[2,128,2816]{2,1,0:T(8,128)(2,1)S(1)}, u32[]{:S(2)}, u32[]{:S(2)}) collective-permute-start(bf16[2,128,2816]{2,1,0:T(8,128)(2,1)} %collective-permute-done.1), channel_id=1, source_target_pairs={{0,2},{1,3},{2,4},{3,5},{4,6},{5,7},{6,22},{7,23},{8,10},{9,11},{1... | collective-permute-start | bytes 4325384 | tf_op jit(solution)/shard_map/ppermute | solution.py:799
  226.4 32.3 %collective-permute-start.7 = (bf16[2,128,2816]{2,1,0:T(8,128)(2,1)}, bf16[2,128,2816]{2,1,0:T(8,128)(2,1)S(1)}, u32[]{:S(2)}, u32[]{:S(2)}) collective-permute-start(bf16[2,128,2816]{2,1,0:T(8,128)(2,1)} %collective-permute-done.2), channel_id=1, source_target_pairs={{0,16},{1,17},{2,0},{3,1},{4,2},{5,3},{6,4},{7,5},{8,24},{9,25},{1... | collective-permute-start | bytes 4325384 | tf_op jit(solution)/shard_map/ppermute | solution.py:799
  267.6 50.1 %collective-permute-start.19 = (bf16[384,2048]{1,0:T(8,128)(2,1)S(1)}, bf16[384,2048]{1,0:T(8,128)(2,1)}, u32[]{:S(2)}, u32[]{:S(2)}) collective-permute-start(bf16[384,2048]{1,0:T(8,128)(2,1)S(1)} %collective-permute-done.18), channel_id=1, source_target_pairs={{0,1},{1,0},{2,3},{3,2},{4,5},{5,4},{6,7},{7,6},{8,9},{9,8},{10,11... | collective-permute-start | bytes 4718600 | tf_op jit(solution)/shard_map/ppermute | solution.py:799
  268.1 33.8 %collective-permute-start.8 = (bf16[2,128,2816]{2,1,0:T(8,128)(2,1)}, bf16[2,128,2816]{2,1,0:T(8,128)(2,1)S(1)}, u32[]{:S(2)}, u32[]{:S(2)}) collective-permute-start(bf16[2,128,2816]{2,1,0:T(8,128)(2,1)} %copy-done.52), channel_id=1, source_target_pairs={{0,2},{1,3},{2,4},{3,5},{4,6},{5,7},{6,22},{7,23},{8,10},{9,11},{1... | collective-permute-start | bytes 4325384 | tf_op jit(solution)/shard_map/ppermute | solution.py:799
  269.9 33.5 %collective-permute-start.9 = (bf16[2,128,2816]{2,1,0:T(8,128)(2,1)S(1)}, bf16[2,128,2816]{2,1,0:T(8,128)(2,1)S(1)}, u32[]{:S(2)}, u32[]{:S(2)}) collective-permute-start(bf16[2,128,2816]{2,1,0:T(8,128)(2,1)S(1)} %collective-permute-done.7), channel_id=1, source_target_pairs={{0,16},{1,17},{2,0},{3,1},{4,2},{5,3},{6,4},{7,5},{8,24},{9,25},{1... | collective-permute-start | bytes 4325384 | tf_op jit(solution)/shard_map/ppermute | solution.py:799
  274.6 37.8 %collective-permute-start.14 = (bf16[384,2048]{1,0:T(8,128)(2,1)}, bf16[384,2048]{1,0:T(8,128)(2,1)S(1)}, u32[]{:S(2)}, u32[]{:S(2)}) collective-permute-start(bf16[384,2048]{1,0:T(8,128)(2,1)} %add_convert_fusion.5), channel_id=1, source_target_pairs={{0,8},{1,9},{2,10},{3,11},{4,12},{5,13},{6,14},{7,15},{8,0},{9,1},... | collective-permute-start | bytes 4718600 | tf_op jit(solution)/shard_map/ppermute | solution.py:799
  343.3 36.1 %collective-permute-start.20 = (bf16[384,2048]{1,0:T(8,128)(2,1)S(1)}, bf16[384,2048]{1,0:T(8,128)(2,1)}, u32[]{:S(2)}, u32[]{:S(2)}) collective-permute-start(bf16[384,2048]{1,0:T(8,128)(2,1)S(1)} %multiply_convert_fusion), channel_id=1, source_target_pairs={{0,8},{1,9},{2,10},{3,11},{4,12},{5,13},{6,14},{7,15},{8,0},{9,1},... | collective-permute-start | bytes 4718600 | tf_op jit(solution)/shard_map/ppermute | solution.py:799
  444.0 43.7 %collective-permute-start.30 = (bf16[384,2048]{1,0:T(8,128)(2,1)S(1)}, bf16[384,2048]{1,0:T(8,128)(2,1)S(1)}, u32[]{:S(2)}, u32[]{:S(2)}) collective-permute-start(bf16[384,2048]{1,0:T(8,128)(2,1)S(1)} %slice.508), channel_id=1, source_target_pairs={{0,1},{1,0},{2,3},{3,2},{4,5},{5,4},{6,7},{7,6},{8,9},{9,8},{10,11... | collective-permute-start | bytes 4718600 | tf_op jit(solution)/shard_map/ppermute | solution.py:799
  447.4 40.2 %collective-permute-start.27 = (bf16[384,2048]{1,0:T(8,128)(2,1)}, bf16[384,2048]{1,0:T(8,128)(2,1)S(1)}, u32[]{:S(2)}, u32[]{:S(2)}) collective-permute-start(bf16[384,2048]{1,0:T(8,128)(2,1)} %add_convert_fusion.4), channel_id=1, source_target_pairs={{0,8},{1,9},{2,10},{3,11},{4,12},{5,13},{6,14},{7,15},{8,0},{9,1},... | collective-permute-start | bytes 4718600 | tf_op jit(solution)/shard_map/ppermute | solution.py:799
  461.8 25.8 %collective-permute-start.25 = (bf16[1,128,1408]{2,1,0:T(8,128)(2,1)S(1)}, bf16[1,128,1408]{2,1,0:T(8,128)(2,1)S(1)}, u32[]{:S(2)}, u32[]{:S(2)}) collective-permute-start(bf16[1,128,1408]{2,1,0:T(8,128)(2,1)S(1)} %get-tuple-element.200), channel_id=1, source_target_pairs={{0,2},{1,3},{2,4},{3,5},{4,6},{5,7},{6,22},{7,23},{8,10},{9,11},{1... | collective-permute-start | bytes 1081352 | tf_op jit(solution)/shard_map/ppermute | solution.py:799
  496.2 38.0 %collective-permute-start.36 = (bf16[384,2048]{1,0:T(8,128)(2,1)S(1)}, bf16[384,2048]{1,0:T(8,128)(2,1)S(1)}, u32[]{:S(2)}, u32[]{:S(2)}) collective-permute-start(bf16[384,2048]{1,0:T(8,128)(2,1)S(1)} %get-tuple-element.179), channel_id=1, source_target_pairs={{0,8},{1,9},{2,10},{3,11},{4,12},{5,13},{6,14},{7,15},{8,0},{9,1},... | collective-permute-start | bytes 4718600 | tf_op jit(solution)/shard_map/ppermute | solution.py:799
  500.2 34.0 %collective-permute-start.35 = (bf16[2,128,1408]{2,1,0:T(8,128)(2,1)S(1)}, bf16[2,128,1408]{2,1,0:T(8,128)(2,1)}, u32[]{:S(2)}, u32[]{:S(2)}) collective-permute-start(bf16[2,128,1408]{2,1,0:T(8,128)(2,1)S(1)} %pad_maximum_fusion.16), channel_id=1, source_target_pairs={{0,16},{1,17},{2,0},{3,1},{4,2},{5,3},{6,4},{7,5},{8,24},{9,25},{1... | collective-permute-start | bytes 2162696 | tf_op jit(solution)/shard_map/ppermute | solution.py:799
  502.4 31.8 %collective-permute-start.34 = (bf16[2,128,1408]{2,1,0:T(8,128)(2,1)S(1)}, bf16[2,128,1408]{2,1,0:T(8,128)(2,1)S(1)}, u32[]{:S(2)}, u32[]{:S(2)}) collective-permute-start(bf16[2,128,1408]{2,1,0:T(8,128)(2,1)S(1)} %pad_maximum_fusion.15), channel_id=1, source_target_pairs={{0,2},{1,3},{2,4},{3,5},{4,6},{5,7},{6,22},{7,23},{8,10},{9,11},{1... | collective-permute-start | bytes 2162696 | tf_op jit(solution)/shard_map/ppermute | solution.py:799
  519.3 42.5 %collective-permute-start.33 = (bf16[2,128,2816]{2,1,0:T(8,128)(2,1)}, bf16[2,128,2816]{2,1,0:T(8,128)(2,1)S(1)}, u32[]{:S(2)}, u32[]{:S(2)}) collective-permute-start(bf16[2,128,2816]{2,1,0:T(8,128)(2,1)} %pad_maximum_fusion.8), channel_id=1, source_target_pairs={{0,16},{1,17},{2,0},{3,1},{4,2},{5,3},{6,4},{7,5},{8,24},{9,25},{1... | collective-permute-start | bytes 4325384 | tf_op jit(solution)/shard_map/ppermute | solution.py:799
  520.8 41.0 %collective-permute-start.32 = (bf16[2,128,2816]{2,1,0:T(8,128)(2,1)}, bf16[2,128,2816]{2,1,0:T(8,128)(2,1)S(1)}, u32[]{:S(2)}, u32[]{:S(2)}) collective-permute-start(bf16[2,128,2816]{2,1,0:T(8,128)(2,1)} %pad_maximum_fusion.7), channel_id=1, source_target_pairs={{0,2},{1,3},{2,4},{3,5},{4,6},{5,7},{6,22},{7,23},{8,10},{9,11},{1... | collective-permute-start | bytes 4325384 | tf_op jit(solution)/shard_map/ppermute | solution.py:799
  585.6 48.7 %collective-permute-start.39 = (bf16[2,128,1408]{2,1,0:T(8,128)(2,1)}, bf16[2,128,1408]{2,1,0:T(8,128)(2,1)}, u32[]{:S(2)}, u32[]{:S(2)}) collective-permute-start(bf16[2,128,1408]{2,1,0:T(8,128)(2,1)} %get-tuple-element.196), channel_id=1, source_target_pairs={{0,2},{1,3},{2,4},{3,5},{4,6},{5,7},{6,22},{7,23},{8,10},{9,11},{1... | collective-permute-start | bytes 2162696 | tf_op jit(solution)/shard_map/ppermute | solution.py:799
  593.9 40.4 %collective-permute-start.40 = (bf16[2,128,1408]{2,1,0:T(8,128)(2,1)}, bf16[2,128,1408]{2,1,0:T(8,128)(2,1)}, u32[]{:S(2)}, u32[]{:S(2)}) collective-permute-start(bf16[2,128,1408]{2,1,0:T(8,128)(2,1)} %get-tuple-element.195), channel_id=1, source_target_pairs={{0,16},{1,17},{2,0},{3,1},{4,2},{5,3},{6,4},{7,5},{8,24},{9,25},{1... | collective-permute-start | bytes 2162696 | tf_op jit(solution)/shard_map/ppermute | solution.py:799
  594.8 47.9 %collective-permute-start.38 = (bf16[2,128,2816]{2,1,0:T(8,128)(2,1)}, bf16[2,128,2816]{2,1,0:T(8,128)(2,1)}, u32[]{:S(2)}, u32[]{:S(2)}) collective-permute-start(bf16[2,128,2816]{2,1,0:T(8,128)(2,1)} %fusion.25), channel_id=1, source_target_pairs={{0,16},{1,17},{2,0},{3,1},{4,2},{5,3},{6,4},{7,5},{8,24},{9,25},{1... | collective-permute-start | bytes 4325384 | tf_op jit(solution)/shard_map/ppermute | solution.py:799
  595.0 47.7 %collective-permute-start.37 = (bf16[2,128,2816]{2,1,0:T(8,128)(2,1)}, bf16[2,128,2816]{2,1,0:T(8,128)(2,1)}, u32[]{:S(2)}, u32[]{:S(2)}) collective-permute-start(bf16[2,128,2816]{2,1,0:T(8,128)(2,1)} %fusion.26), channel_id=1, source_target_pairs={{0,2},{1,3},{2,4},{3,5},{4,6},{5,7},{6,22},{7,23},{8,10},{9,11},{1... | collective-permute-start | bytes 4325384 | tf_op jit(solution)/shard_map/ppermute | solution.py:799
  597.7 34.5 %collective-permute-start.46 = (bf16[384,2048]{1,0:T(8,128)(2,1)S(1)}, bf16[384,2048]{1,0:T(8,128)(2,1)S(1)}, u32[]{:S(2)}, u32[]{:S(2)}) collective-permute-start(bf16[384,2048]{1,0:T(8,128)(2,1)S(1)} %add_convert_fusion.3), channel_id=1, source_target_pairs={{0,8},{1,9},{2,10},{3,11},{4,12},{5,13},{6,14},{7,15},{8,0},{9,1},... | collective-permute-start | bytes 4718600 | tf_op jit(solution)/shard_map/ppermute | solution.py:799
  662.3 63.2 %collective-permute-start.53 = (bf16[2,128,1408]{2,1,0:T(8,128)(2,1)}, bf16[2,128,1408]{2,1,0:T(8,128)(2,1)}, u32[]{:S(2)}, u32[]{:S(2)}) collective-permute-start(bf16[2,128,1408]{2,1,0:T(8,128)(2,1)} %get-tuple-element.193), channel_id=1, source_target_pairs={{0,2},{1,3},{2,4},{3,5},{4,6},{5,7},{6,22},{7,23},{8,10},{9,11},{1... | collective-permute-start | bytes 2162696 | tf_op jit(solution)/shard_map/ppermute | solution.py:799
  662.3 63.2 %collective-permute-start.54 = (bf16[2,128,1408]{2,1,0:T(8,128)(2,1)}, bf16[2,128,1408]{2,1,0:T(8,128)(2,1)}, u32[]{:S(2)}, u32[]{:S(2)}) collective-permute-start(bf16[2,128,1408]{2,1,0:T(8,128)(2,1)} %get-tuple-element.194), channel_id=1, source_target_pairs={{0,16},{1,17},{2,0},{3,1},{4,2},{5,3},{6,4},{7,5},{8,24},{9,25},{1... | collective-permute-start | bytes 2162696 | tf_op jit(solution)/shard_map/ppermute | solution.py:799
  665.7 31.9 %collective-permute-start.49 = (bf16[768,128]{1,0:T(8,128)(2,1)S(1)}, bf16[768,128]{1,0:T(8,128)(2,1)S(1)}, u32[]{:S(2)}, u32[]{:S(2)}) collective-permute-start(bf16[768,128]{1,0:T(8,128)(2,1)S(1)} %get-tuple-element.231), channel_id=1, source_target_pairs={{4,0},{5,1},{6,2},{7,3},{12,8},{13,9},{14,10},{15,11},{20,16},{21,... | collective-permute-start | bytes 589832 | tf_op jit(solution)/shard_map/ppermute | solution.py:799
  667.0 31.5 %collective-permute-start.50 = (bf16[768,128]{1,0:T(8,128)(2,1)S(1)}, bf16[768,128]{1,0:T(8,128)(2,1)S(1)}, u32[]{:S(2)}, u32[]{:S(2)}) collective-permute-start(bf16[768,128]{1,0:T(8,128)(2,1)S(1)} %get-tuple-element.230), channel_id=1, source_target_pairs={{6,0},{7,1},{14,8},{15,9},{22,16},{23,17},{30,24},{31,25}} | collective-permute-start | bytes 589832 | tf_op jit(solution)/shard_map/ppermute | solution.py:799
  687.5 40.7 %collective-permute-start.51 = (bf16[2,128,2816]{2,1,0:T(8,128)(2,1)}, bf16[2,128,2816]{2,1,0:T(8,128)(2,1)}, u32[]{:S(2)}, u32[]{:S(2)}) collective-permute-start(bf16[2,128,2816]{2,1,0:T(8,128)(2,1)} %get-tuple-element.183), channel_id=1, source_target_pairs={{0,2},{1,3},{2,4},{3,5},{4,6},{5,7},{6,22},{7,23},{8,10},{9,11},{1... | collective-permute-start | bytes 4325384 | tf_op jit(solution)/shard_map/ppermute | solution.py:799
  697.6 30.6 %collective-permute-start.52 = (bf16[2,128,2816]{2,1,0:T(8,128)(2,1)S(1)}, bf16[2,128,2816]{2,1,0:T(8,128)(2,1)}, u32[]{:S(2)}, u32[]{:S(2)}) collective-permute-start(bf16[2,128,2816]{2,1,0:T(8,128)(2,1)S(1)} %get-tuple-element.184), channel_id=1, source_target_pairs={{0,16},{1,17},{2,0},{3,1},{4,2},{5,3},{6,4},{7,5},{8,24},{9,25},{1... | collective-permute-start | bytes 4325384 | tf_op jit(solution)/shard_map/ppermute | solution.py:799
  698.6 128.2 %collective-permute-start.47 = (bf16[384,2048]{1,0:T(8,128)(2,1)}, bf16[384,2048]{1,0:T(8,128)(2,1)}, u32[]{:S(2)}, u32[]{:S(2)}) collective-permute-start(bf16[384,2048]{1,0:T(8,128)(2,1)} %slice.514), channel_id=1, source_target_pairs={{0,1},{1,0},{2,3},{3,2},{4,5},{5,4},{6,7},{7,6},{8,9},{9,8},{10,11... | collective-permute-start | bytes 4718600 | tf_op jit(solution)/shard_map/ppermute | solution.py:799
  (119 other events, 2588.9 us)
